TPU v7x, 512 devices: a whole 4x8x8 slice. The times are simulated.
512 devices in a mesh: dp: 32 (over y, x), expert: 16 (over z, core).
Axes of the slice: x: 4, y: 8, z: 8, core: 2. Of those that a mesh axis runs over, the one named last changes fastest.
Arguments:
- tokens: bfloat16 [65536, 2048], P('dp', 'expert'), may hold values from -6 to 6
- cotangent: bfloat16 [65536, 2048], P('dp', 'expert'), may hold values from -6 to 6
- down_proj: bfloat16 [2048, 512], P('expert'), may hold values from -0.125 to 0.125
- up_proj: bfloat16 [512, 2048], P(None, 'expert'), may hold values from -0.25 to 0.25
- routes: int32 [65536, 4], P(('dp', 'expert')), may hold values from 0 to 15, all different within a row; in each aligned block of 128 rows (0 to 127, 128 to 255, ...) at most 40 rows name the same one
- gate_weights: float32 [65536, 4], P(('dp', 'expert')), may hold values from 0.2 to 1
- expert_in: bfloat16 [16, 512, 2688], P('expert', 'dp'), may hold values from -0.25 to 0.25
- expert_out: bfloat16 [16, 1344, 512], P('expert', 'dp'), may hold values from -0.15625 to 0.15625
Outputs:
- mixed: bfloat16 [65536, 2048], P('dp', 'expert')
- input_grad: bfloat16 [65536, 2048], P('dp', 'expert')
- down_grad: float32 [2048, 512], P('expert')
- up_grad: float32 [512, 2048], P(None, 'expert')
Inputs may be any that keep to these rules, and one draw needn't show every extreme that they name: `routes`: the rows of one device name no expert more than 40 times, a bound that some block reaches.
All inputs are finite; a program needn't handle non-finite values.
Results may differ from a plain program's by a relative error of at most 0.034.
Values may be sent and summed in bfloat16 or wider, within the bound.
No kernel may reach another device: no remote copies, remote signals or barrier semaphores. Data moves between devices by JAX's collectives and lax.ppermute only.
A program may use at most 64 MiB of HBM per device.

v0:
```python
import math

import jax
import jax.numpy as jnp
from jax import lax
from jax.sharding import PartitionSpec as P

TOPK = 4


def swiglu_forward(pre_act, hidden):
    gate_part = pre_act[:, :hidden]
    up_part = pre_act[:, hidden:]
    return gate_part * jax.nn.sigmoid(gate_part) * up_part


def swiglu_backward(pre_act, grad_act, hidden):
    gate_part = pre_act[:, :hidden]
    up_part = pre_act[:, hidden:]
    sigmoid_gate = jax.nn.sigmoid(gate_part)
    grad_gate = grad_act * up_part * sigmoid_gate * (1.0 + gate_part * (1.0 - sigmoid_gate))
    grad_upper = grad_act * (gate_part * sigmoid_gate)
    return jnp.concatenate([grad_gate, grad_upper], axis=1)


def slot_tables(routes, gate_weights, experts, capacity):
    flat_routes = routes.reshape(-1)
    onehot = (flat_routes[:, None] == jnp.arange(experts, dtype=jnp.int32)[None, :]).astype(
        jnp.int32
    )
    before = jnp.cumsum(onehot, axis=0) - onehot
    position = jnp.sum(before * onehot, axis=1)
    slot = (flat_routes * capacity + position).reshape(routes.shape)
    slot_ids = jnp.arange(experts * capacity, dtype=jnp.int32)
    matches = slot[:, :, None] == slot_ids[None, None, :]
    spread = jnp.sum(matches.astype(jnp.float32), axis=1)
    weighted = jnp.sum(jnp.where(matches, gate_weights[:, :, None], 0.0), axis=1)
    return (spread.astype(jnp.bfloat16), weighted)


def on_device(tokens, cotangent, down_proj, up_proj, routes, gate_weights, expert_in, expert_out):
    groups = lax.axis_size("expert")
    tok_rows = routes.shape[0]
    group_rows = tokens.shape[0]
    latent_width = down_proj.shape[1]
    hidden = expert_in.shape[2] // 2
    capacity = min(tok_rows, tok_rows * TOPK * 5 // (4 * groups))
    slot_count = groups * capacity
    grad_scale = 1.0 / math.sqrt(group_rows * lax.axis_size("dp"))
    contract_rows = (((0,), (0,)), ((), ()))
    contract_cols = (((1,), (1,)), ((), ()))
    row_block = tokens
    latent = lax.psum_scatter(
        jnp.dot(row_block, down_proj, preferred_element_type=jnp.float32).astype(jnp.bfloat16),
        "expert",
        scatter_dimension=0,
        tiled=True,
    )
    spread, weighted = slot_tables(routes, gate_weights, groups, capacity)
    outgoing = lax.dot_general(
        spread, latent, contract_rows, preferred_element_type=jnp.float32
    ).astype(jnp.bfloat16)
    received = lax.all_to_all(
        outgoing.reshape(groups, capacity, latent_width),
        "expert",
        split_axis=0,
        concat_axis=0,
        tiled=True,
    )
    rows_in = received.reshape(slot_count, latent_width)
    gathered_in, gathered_out = (
        lax.all_gather(expert_in, "dp", axis=1, tiled=True),
        lax.all_gather(expert_out, "dp", axis=1, tiled=True),
    )
    weight_in = gathered_in[0]
    weight_out = gathered_out[0]
    pre_act = jnp.dot(rows_in, weight_in, preferred_element_type=jnp.float32)
    activation = swiglu_forward(pre_act, hidden).astype(jnp.bfloat16)
    rows_out = jnp.dot(activation, weight_out, preferred_element_type=jnp.float32).astype(
        jnp.bfloat16
    )
    returned = lax.all_to_all(
        rows_out.reshape(groups, capacity, latent_width),
        "expert",
        split_axis=0,
        concat_axis=0,
        tiled=True,
    )
    latent_out = jnp.dot(
        weighted,
        returned.reshape(slot_count, latent_width).astype(jnp.float32),
        precision=lax.Precision.HIGHEST,
    ).astype(jnp.bfloat16)
    portion = lax.all_gather(latent_out, "expert", axis=0, tiled=True)
    product = jnp.dot(portion, up_proj, preferred_element_type=jnp.float32)
    outputs = product
    grad_part = lax.dot_general(
        portion, cotangent, contract_rows, preferred_element_type=jnp.float32
    )
    outputs, up_grad = (outputs, grad_part)
    mixed = outputs.astype(jnp.bfloat16)
    row_block = cotangent
    latent_out_grad = lax.psum_scatter(
        lax.dot_general(
            row_block, up_proj, contract_cols, preferred_element_type=jnp.float32
        ).astype(jnp.bfloat16),
        "expert",
        scatter_dimension=0,
        tiled=True,
    )
    routed_grad = lax.dot_general(
        weighted,
        latent_out_grad.astype(jnp.float32),
        contract_rows,
        precision=lax.Precision.HIGHEST,
        preferred_element_type=jnp.float32,
    ).astype(jnp.bfloat16)
    grad_in_rows = lax.all_to_all(
        routed_grad.reshape(groups, capacity, latent_width),
        "expert",
        split_axis=0,
        concat_axis=0,
        tiled=True,
    ).reshape(slot_count, latent_width)
    grad_act = lax.dot_general(
        grad_in_rows, weight_out, contract_cols, preferred_element_type=jnp.float32
    )
    pre_grad = swiglu_backward(pre_act, grad_act, hidden).astype(jnp.bfloat16)
    rows_grad = lax.dot_general(
        pre_grad, weight_in, contract_cols, preferred_element_type=jnp.float32
    ).astype(jnp.bfloat16)
    grad_back = lax.all_to_all(
        rows_grad.reshape(groups, capacity, latent_width),
        "expert",
        split_axis=0,
        concat_axis=0,
        tiled=True,
    ).reshape(slot_count, latent_width)
    latent_grad = jnp.dot(spread, grad_back, preferred_element_type=jnp.float32).astype(
        jnp.bfloat16
    )
    portion = lax.all_gather(latent_grad, "expert", axis=0, tiled=True)
    product = lax.dot_general(portion, down_proj, contract_cols, preferred_element_type=jnp.float32)
    grad_inputs = product
    grad_part = lax.dot_general(tokens, portion, contract_rows, preferred_element_type=jnp.float32)
    grad_inputs, down_grad = (grad_inputs, grad_part)
    up_grad, down_grad = (
        lax.psum(up_grad.astype(jnp.bfloat16), "dp").astype(jnp.float32),
        lax.psum(down_grad.astype(jnp.bfloat16), "dp").astype(jnp.float32),
    )
    return (mixed, grad_inputs.astype(jnp.bfloat16), down_grad * grad_scale, up_grad * grad_scale)


def solution(mesh):
    in_specs = (
        P("dp", "expert"),
        P("dp", "expert"),
        P("expert", None),
        P(None, "expert"),
        P(("dp", "expert"), None),
        P(("dp", "expert"), None),
        P("expert", "dp", None),
        P("expert", "dp", None),
    )
    out_specs = (P("dp", "expert"), P("dp", "expert"), P("expert", None), P(None, "expert"))
    return jax.shard_map(
        on_device, mesh=mesh, in_specs=in_specs, out_specs=out_specs, check_vma=False
    )
```

profile of v0, /device:TPU:64, one launch (start us, length us, event | category | flops | bytes accessed | tf_op | source)
XLA Modules:
  0.0 480.6 jit_solution(15891864590014773237)
XLA Ops:
  8.0 0.0 copy-start
  8.0 0.0 reduce-scatter.3.cloned.1.call-start
  8.1 1.0 copy-done
  9.0 2.9 convolution_convert_fusion.1
  12.0 0.0 reduce-scatter.3.cloned.1.call-update
  12.0 0.0 copy-start.7
  12.0 0.0 copy-start.8
  12.0 0.0 copy-start.9
  12.0 0.0 reduce-scatter.5.cloned.1.call-start
  12.1 2.0 convolution_convert_fusion
  14.1 0.0 reduce-scatter.5.cloned.1.call-update
  14.1 0.0 all-gather.5.cloned.1.call-start
  14.2 0.5 all-gather.5.cloned.1.call-update
  14.7 0.0 all-gather.7.cloned.1.call-start
  14.8 0.7 copy.60
  15.5 0.0 all-gather.7.cloned.1.call-update
  15.5 0.0 copy-done.8
  15.5 0.1 copy.56
  15.6 0.1 eq.42
  15.7 0.1 eq.38
  15.9 1.2 reduce-window.6
  17.0 0.2 slice_reduce_fusion
  17.3 0.1 fusion.28
  17.4 0.1 reduce_sum.30
  17.5 0.1 copy.59
  17.6 0.3 convert_reduce_fusion
  17.9 58.2 %reduce-scatter.3.cloned.1.call-done = bf16[128,512]{1,0:T(8,128)(2,1)} async-done(((bf16[2048,512]{1,0:T(8,128)(2,1)}), bf16[128,512]{1,0:T(8,128)(2,1)}) %reduce-scatter.3.cloned.1.call-update) | async-done | bytes 131088 | tf_op jit(solution)/shard_map/reduce_scatter | solution.py:53
  76.1 2.1 convolution_convert_fusion.4
  78.2 7.5 %all-to-all-start = ((bf16[16,40,512]{2,1,0:T(8,128)(2,1)}), bf16[16,40,512]{2,1,0:T(8,128)(2,1)S(1)}, u32[]{:S(2)}, u32[]{:S(2)}) async-start(bf16[16,40,512]{2,1,0:T(8,128)(2,1)} %bitcast.1), calls=%async_computation.1 | async-start | bytes 1310720 | tf_op jit(solution)/shard_map/all_to_all | solution.py:63
  85.7 57.6 %reduce-scatter.5.cloned.1.call-done = bf16[128,512]{1,0:T(8,128)(2,1)} async-done(((bf16[2048,512]{1,0:T(8,128)(2,1)}), bf16[128,512]{1,0:T(8,128)(2,1)}) %reduce-scatter.5.cloned.1.call-update) | async-done | bytes 131088 | tf_op jit(solution)/shard_map/reduce_scatter | solution.py:103
  143.3 2.5 convolution_convert_fusion.5
  145.8 0.0 all-to-all-done
  145.8 8.8 %all-to-all-start.2 = ((bf16[16,40,512]{2,1,0:T(8,128)(2,1)}), bf16[16,40,512]{2,1,0:T(8,128)(2,1)S(1)}, u32[]{:S(2)}, u32[]{:S(2)}) async-start(bf16[16,40,512]{2,1,0:T(8,128)(2,1)} %bitcast.6), calls=%async_computation.4 | async-start | bytes 1310720 | tf_op jit(solution)/shard_map/all_to_all | solution.py:118
  154.6 0.0 all-gather.11.cloned.1.call-start
  154.7 0.0 all-gather.5.cloned.1.call-done
  154.7 6.7 %fusion.6 = f32[640,2688]{1,0:T(8,128)} fusion(bf16[640,512]{1,0:T(8,128)(2,1)S(1)} %bitcast.67, bf16[1,512,2688]{2,1,0:T(8,128)(2,1)} %all-gather.5.cloned.1.call-done), kind=kOutput, calls=%fused_computation.12 | convolution fusion | flops 1761607680 | bytes 10289152 | tf_op jit(solution)/shard_map/dot_general | solution.py:77
  161.4 30.7 %all-gather.7.cloned.1.call-done = bf16[1,1344,512]{2,0,1:T(2,128)(2,1)} async-done(((bf16[1,42,512]{2,0,1:T(2,128)(2,1)}), bf16[1,1344,512]{2,0,1:T(2,128)(2,1)}) %all-gather.7.cloned.1.call-update) | async-done | bytes 1376272 | tf_op jit(solution)/shard_map/all_gather | solution.py:73
  192.0 0.0 all-to-all-done.2
  192.1 5.6 %multiply_convert_fusion.1 = (bf16[640,1344]{1,0:T(8,128)(2,1)S(1)}, bf16[640,1344]{1,0:T(8,128)(2,1)S(1)}) fusion(f32[640,2688]{1,0:T(8,128)} %fusion.6, bf16[640,512]{1,0:T(8,128)(2,1)S(1)} %bitcast.70, bf16[1,1344,512]{2,0,1:T(2,128)(2,1)} %all-gather.7.cloned.1.call-done), kind=kOutput, calls=%fused_computation.1 | convolution fusion | flops 891985920 | bytes 12353536 | tf_op jit(solution)/shard_map/dot_general | solution.py:125
  197.6 2.1 fusion.15
  199.7 26.2 %all_to_all.20 = bf16[16,40,512]{2,1,0:T(8,128)(2,1)S(1)} all-to-all(bf16[16,40,512]{2,1,0:T(8,128)(2,1)S(1)} %bitcast.71), channel_id=1, replica_groups=mesh['dp'=32,'expert'=16] {'expert'}, dimensions={0} | all-to-all | bytes 1310720 | tf_op jit(solution)/shard_map/all_to_all | solution.py:132
  225.9 0.9 convolution_convert_fusion.8
  226.8 0.0 all-gather.11.cloned.1.call-update
  226.8 0.0 all-gather.9.cloned.1.call-start
  226.9 5.2 %fusion.12 = bf16[640,512]{1,0:T(8,128)(2,1)S(1)} fusion(f32[640,2688]{1,0:T(8,128)} %fusion.6, bf16[1,1344,512]{2,0,1:T(2,128)(2,1)} %all-gather.7.cloned.1.call-done), kind=kOutput, calls=%fused_computation.21 | convolution fusion | flops 886292480 | bytes 10616832 | tf_op jit(solution)/shard_map/dot_general | solution.py:79
  232.1 27.2 %all_to_all.21 = bf16[16,40,512]{2,1,0:T(8,128)(2,1)S(1)} all-to-all(bf16[16,40,512]{2,1,0:T(8,128)(2,1)S(1)} %bitcast.72), channel_id=1, replica_groups=mesh['dp'=32,'expert'=16] {'expert'}, dimensions={0} | all-to-all | bytes 1310720 | tf_op jit(solution)/shard_map/all_to_all | solution.py:82
  259.3 1.1 convolution_convert_fusion.9
  260.5 0.0 all-gather.9.cloned.1.call-update
  260.5 0.0 copy-start.5
  260.5 0.2 all-reduce.3.cloned.1.call-start
  260.7 7.9 %all-gather.11.cloned.1.call-done = bf16[2048,512]{1,0:T(8,128)(2,1)} async-done(((bf16[128,512]{1,0:T(8,128)(2,1)}), bf16[2048,512]{1,0:T(8,128)(2,1)}) %all-gather.11.cloned.1.call-update) | async-done | bytes 2097168 | tf_op jit(solution)/shard_map/all_gather | solution.py:142
  268.6 3.2 fusion.20
  271.8 41.0 %all-gather.9.cloned.1.call-done = bf16[2048,512]{1,0:T(8,128)(2,1)} async-done(((bf16[128,512]{1,0:T(8,128)(2,1)}), bf16[2048,512]{1,0:T(8,128)(2,1)}) %all-gather.9.cloned.1.call-update) | async-done | bytes 2097168 | tf_op jit(solution)/shard_map/all_gather | solution.py:94
  312.7 3.0 convolution_convert_fusion.6
  315.7 0.0 all-reduce.3.cloned.1.call-update
  315.8 0.0 copy-done.5
  315.8 0.0 copy-done.1
  315.8 1.5 convolution_convert_fusion.2
  317.3 0.1 copy-done.2
  317.4 1.5 convolution_convert_fusion.3
  318.9 151.0 %all-reduce.3.cloned.1.call-done = (bf16[128,512]{0,1:T(8,128)(2,1)}, bf16[512,128]{1,0:T(8,128)(2,1)}) async-done(((bf16[128,512]{0,1:T(8,128)(2,1)}, bf16[512,128]{1,0:T(8,128)(2,1)}), (bf16[128,512]{0,1:T(8,128)(2,1)}, bf16[512,128]{1,0:T(8,128)(2,1)})) %all-reduce.3.cloned.1.call-update) | async-done | bytes 262160 | tf_op jit(solution)/shard_map/psum | solution.py:149
  469.9 0.9 convert_multiply_fusion.1
  470.8 0.8 copy.63
  471.6 1.6 convert_multiply_fusion
  (14 shorter events, 0.1 us)
Async XLA Ops:
  8.0 1.0 copy-start
  8.0 4.1 copy-start.6
  8.0 4.1 copy-start.4
  8.0 68.1 %reduce-scatter.3.cloned.1.call-start = ((), (), s32[]{:S(2)}) async-start(), calls=%async_computation.6 | async-start | bytes 2228224 | tf_op jit(solution)/shard_map/reduce_scatter | solution.py:53
  12.0 2.8 copy-start.7
  12.0 3.5 copy-start.8
  12.0 5.6 %copy-start.9 = (f32[128,4]{0,1:T(4,128)S(1)}, f32[128,4]{0,1:T(4,128)}, u32[]{:S(2)}) copy-start(f32[128,4]{0,1:T(4,128)} %param.13) | copy-start | bytes 6148
  12.0 131.3 %reduce-scatter.5.cloned.1.call-start = ((), (), s32[]{:S(2)}) async-start(), calls=%async_computation.10 | async-start | bytes 2228224 | tf_op jit(solution)/shard_map/reduce_scatter | solution.py:103
  14.1 140.6 %all-gather.5.cloned.1.call-start = ((), (), s32[]{:S(2)}) async-start(), calls=%async_computation.7 | async-start | bytes 2838528 | tf_op jit(solution)/shard_map/all_gather | solution.py:72
  14.7 177.3 %all-gather.7.cloned.1.call-start = ((), (), s32[]{:S(2)}) async-start(), calls=%async_computation.8 | async-start | bytes 2838528 | tf_op jit(solution)/shard_map/all_gather | solution.py:73
  78.2 67.6 %all-to-all-start = ((bf16[16,40,512]{2,1,0:T(8,128)(2,1)}), bf16[16,40,512]{2,1,0:T(8,128)(2,1)S(1)}, u32[]{:S(2)}, u32[]{:S(2)}) async-start(bf16[16,40,512]{2,1,0:T(8,128)(2,1)} %bitcast.1), calls=%async_computation.1 | async-start | bytes 1310720 | tf_op jit(solution)/shard_map/all_to_all | solution.py:63
  145.8 46.2 %all-to-all-start.2 = ((bf16[16,40,512]{2,1,0:T(8,128)(2,1)}), bf16[16,40,512]{2,1,0:T(8,128)(2,1)S(1)}, u32[]{:S(2)}, u32[]{:S(2)}) async-start(bf16[16,40,512]{2,1,0:T(8,128)(2,1)} %bitcast.6), calls=%async_computation.4 | async-start | bytes 1310720 | tf_op jit(solution)/shard_map/all_to_all | solution.py:118
  154.6 114.0 %all-gather.11.cloned.1.call-start = ((), (), s32[]{:S(2)}) async-start(), calls=%async_computation.11 | async-start | bytes 2228224 | tf_op jit(solution)/shard_map/all_gather | solution.py:142
  192.1 5.6 %copy-start.3 = (bf16[1,512,2688]{2,1,0:T(8,128)(2,1)S(1)}, bf16[1,512,2688]{2,1,0:T(8,128)(2,1)}, u32[]{:S(2)}) copy-start(bf16[1,512,2688]{2,1,0:T(8,128)(2,1)} %all-gather.5.cloned.1.call-done) | copy-start | bytes 8257540
  226.8 85.9 %all-gather.9.cloned.1.call-start = ((), (), s32[]{:S(2)}) async-start(), calls=%async_computation.9 | async-start | bytes 2228224 | tf_op jit(solution)/shard_map/all_gather | solution.py:94
  260.5 55.3 %copy-start.5 = (bf16[128,512]{1,0:T(8,128)(2,1)S(1)}, bf16[128,512]{1,0:T(8,128)(2,1)}, u32[]{:S(2)}) copy-start(bf16[128,512]{1,0:T(8,128)(2,1)} %param.10) | copy-start | bytes 393220
  260.5 209.4 %all-reduce.3.cloned.1.call-start = ((), (), s32[]{:S(2)}) async-start(), calls=%async_computation.12 | async-start | bytes 524288 | tf_op jit(solution)/shard_map/psum | solution.py:149
  268.6 47.2 %copy-start.1 = (bf16[2048,512]{1,0:T(8,128)(2,1)S(1)}, bf16[2048,512]{1,0:T(8,128)(2,1)}, u32[]{:S(2)}) copy-start(bf16[2048,512]{1,0:T(8,128)(2,1)} %all-gather.11.cloned.1.call-done) | copy-start | bytes 6291460
  315.8 1.6 copy-start.2
Sparse Core Ops, SparseCore 0:
  12.1 63.9 reduce-scatter.2
  78.9 64.3 reduce-scatter.4
  227.0 41.5 all-gather.10
  271.2 41.5 all-gather.8
Sparse Core Ops, SparseCore 1:
  17.8 88.4 all-gather.4
  109.9 82.1 all-gather.6
  315.8 154.0 all-reduce.2
where the time goes:
time: 481 us
  waiting for transfers between devices  347 us (72%)
  blocking collectives  53.4 us (11%)
  matrix products  40.3 us (8%)
  starting transfers between devices  16.7 us (3%)
  between operations  15.7 us (3%)
    psum x1, waiting for transfers between devices, on_device(): lax.psum(down_grad.astype(jnp.bfloat16), 'dp').astype(jnp.float32)  151 us
    reduce_scatter x1, waiting for transfers between devices, on_device(): lax.psum_scatter(jnp.dot(row_block, down_proj, preferred_element_type=jnp...  58.2 us
    reduce_scatter x1, waiting for transfers between devices, on_device(): lax.psum_scatter(lax.dot_general(row_block, up_proj, contract_cols, prefe...  57.6 us
    all_gather x1, waiting for transfers between devices, on_device(): portion = lax.all_gather(latent_out, 'expert', axis=0, tiled=True)  41 us
    all_gather x1, waiting for transfers between devices, on_device(): lax.all_gather(expert_out, 'dp', axis=1, tiled=True)  30.7 us
    all_to_all x1, blocking collectives, on_device(): lax.all_to_all(rows_out.reshape(groups, capacity, latent_width), 'expert'...  27.2 us
    all_to_all x1, blocking collectives, on_device(): lax.all_to_all(rows_grad.reshape(groups, capacity, latent_width), 'expert...  26.2 us
  transfers between devices with their start and end apart: 9, of which 6 were waited for; matrix products, arithmetic and copies ran while one was open for 6% of the time, Pallas kernels for 0%

commit v1 on v0

v1 whole, which is shorter than its diff:
```python
import math

import jax
import jax.numpy as jnp
from jax import lax
from jax.sharding import Mesh
from jax.sharding import PartitionSpec as P

TOPK = 4
CORES = 2
COLS = (((1,), (1,)), ((), ()))
ROWS = (((0,), (0,)), ((), ()))


def dot(left, right, dims=(((1,), (0,)), ((), ()))):
    return lax.dot_general(left, right, dims, preferred_element_type=jnp.float32)


def slot_tables(routes, gate_weights, experts, capacity):
    flat_routes = routes.reshape(-1)
    onehot = (flat_routes[:, None] == jnp.arange(experts, dtype=jnp.int32)[None, :]).astype(
        jnp.int32
    )
    before = jnp.cumsum(onehot, axis=0) - onehot
    position = jnp.sum(before * onehot, axis=1)
    slot = (flat_routes * capacity + position).reshape(routes.shape)
    slot_ids = jnp.arange(experts * capacity, dtype=jnp.int32)
    matches = slot.T[:, None, :] == slot_ids[None, :, None]
    spread = jnp.any(matches, axis=0)
    weighted = jnp.sum(jnp.where(matches, gate_weights.T[:, None, :], 0.0), axis=0)
    return spread.astype(jnp.bfloat16), weighted


def on_device(tokens, cotangent, down_proj, up_proj, routes, gate_weights, expert_in, expert_out):
    chips = lax.axis_size("z")
    groups = chips * CORES
    dp = lax.axis_size("dp")
    core = lax.axis_index("c")
    tok_rows = routes.shape[0]
    group_rows = tokens.shape[0]
    features = tokens.shape[1]
    latent_width = down_proj.shape[1]
    hidden = expert_in.shape[2] // 2
    capacity = min(tok_rows, tok_rows * TOPK * 5 // (4 * groups))
    slot_count = groups * capacity
    grad_scale = 1.0 / math.sqrt(group_rows * dp)
    bf16 = jnp.bfloat16

    weight_in = lax.all_gather(expert_in, "dp", axis=1, tiled=True)[0]
    weight_out = lax.all_gather(expert_out, "dp", axis=1, tiled=True)[0]

    swap = [(0, 1), (1, 0)]

    def halves(array):
        blocks = array.reshape(chips, CORES, tok_rows, features)
        kept = lax.dynamic_index_in_dim(blocks, core, 1, keepdims=False)
        given = lax.dynamic_index_in_dim(blocks, 1 - core, 1, keepdims=False)
        got = lax.ppermute(given, "c", swap)
        return jnp.concatenate([kept, got], axis=2).reshape(chips * tok_rows, CORES * features)

    down_both = jnp.concatenate([down_proj, lax.ppermute(down_proj, "c", swap)], axis=0)
    up_both = jnp.concatenate([up_proj, lax.ppermute(up_proj, "c", swap)], axis=1)
    part = dot(halves(tokens), down_both).astype(bf16)
    part_grad = dot(halves(cotangent), up_both, COLS).astype(bf16)
    parts = jnp.concatenate([part, part_grad], axis=1).reshape(chips, tok_rows, 2 * latent_width)
    parts = lax.all_to_all(parts, "z", split_axis=0, concat_axis=0, tiled=True)
    latents = jnp.sum(parts.astype(jnp.float32), axis=0).astype(bf16)

    spread, weighted = slot_tables(routes, gate_weights, groups, capacity)
    slot_gate = jnp.sum(weighted, axis=1, keepdims=True)
    gate_high = weighted.astype(bf16)
    gate_low = (weighted - gate_high.astype(jnp.float32)).astype(bf16)

    outgoing = dot(spread, latents)
    outgoing = jnp.concatenate(
        [outgoing[:, :latent_width], outgoing[:, latent_width:] * slot_gate], axis=1
    ).astype(bf16)

    def exchange(rows):
        return lax.all_to_all(
            rows.reshape(groups, capacity, 2 * latent_width),
            ("z", "c"),
            split_axis=0,
            concat_axis=0,
            tiled=True,
        ).reshape(slot_count, 2 * latent_width)

    received = exchange(outgoing)
    pre_act = dot(received[:, :latent_width], weight_in)
    gate_part = pre_act[:, :hidden]
    up_part = pre_act[:, hidden:]
    sigmoid_gate = jax.nn.sigmoid(gate_part)
    silu = gate_part * sigmoid_gate
    rows_out = dot((silu * up_part).astype(bf16), weight_out).astype(bf16)
    grad_act = dot(received[:, latent_width:], weight_out, COLS)
    grad_gate = grad_act * up_part * sigmoid_gate * (1.0 + gate_part * (1.0 - sigmoid_gate))
    grad_upper = grad_act * silu
    pre_grad = jnp.concatenate([grad_gate, grad_upper], axis=1).astype(bf16)
    rows_grad = dot(pre_grad, weight_in, COLS).astype(bf16)
    returned = exchange(jnp.concatenate([rows_out, rows_grad], axis=1))
    returned_out = returned[:, :latent_width]
    latent_out = (dot(gate_high, returned_out, ROWS) + dot(gate_low, returned_out, ROWS)).astype(
        bf16
    )
    latent_grad = dot(spread, returned[:, latent_width:], ROWS).astype(bf16)

    all_out = lax.all_gather(latent_out, ("z", "c"), axis=0, tiled=True)
    all_grad = lax.all_gather(latent_grad, ("z", "c"), axis=0, tiled=True)
    mixed = dot(all_out, up_proj).astype(bf16)
    input_grad = dot(all_grad, down_proj, COLS).astype(bf16)
    up_part_grad = dot(all_out, cotangent, ROWS)
    down_part_grad = dot(all_grad, tokens, ROWS)
    grads = jnp.concatenate([up_part_grad, down_part_grad], axis=1).astype(bf16)
    grads = grads.reshape(dp, latent_width // dp, 2 * features)
    grads = lax.all_to_all(grads, "dp", split_axis=0, concat_axis=0, tiled=True)
    summed = jnp.sum(grads.astype(jnp.float32), axis=0).astype(bf16)
    summed = jnp.broadcast_to(summed[None], grads.shape)
    summed = lax.all_to_all(summed, "dp", split_axis=0, concat_axis=0, tiled=True)
    summed = summed.reshape(latent_width, 2 * features).astype(jnp.float32) * grad_scale
    return mixed, input_grad, summed[:, features:].T, summed[:, :features]


def solution(mesh):
    dp, experts = mesh.devices.shape
    fine = Mesh(mesh.devices.reshape(dp, experts // CORES, CORES), ("dp", "z", "c"))
    expert = ("z", "c")
    in_specs = (
        P("dp", expert),
        P("dp", expert),
        P(expert, None),
        P(None, expert),
        P(("dp", "z", "c"), None),
        P(("dp", "z", "c"), None),
        P(expert, "dp", None),
        P(expert, "dp", None),
    )
    out_specs = (P("dp", expert), P("dp", expert), P(expert, None), P(None, expert))
    return jax.shard_map(
        on_device, mesh=fine, in_specs=in_specs, out_specs=out_specs, check_vma=False
    )
```

time: 481 us -> 372 us (0.77)
  the two profiles are of different devices: /device:TPU:64 before, /device:TPU:8 now
where the time goes in v1:
time: 372 us; the launch traced here: 371 us
  waiting for transfers between devices  225 us (60%)
  blocking collectives  63.2 us (17%)
  matrix products  28.2 us (8%)
  starting transfers between devices  27.6 us (7%)
  between operations  14.1 us (4%)
  local copies, waits for them, and re-layouts  7.77 us (2%)
  other arithmetic  5.46 us (1%)
    all_gather x1, waiting for transfers between devices, on_device(): weight_out = lax.all_gather(expert_out, 'dp', axis=1, tiled=True)[0]  58 us
    all_to_all x1, waiting for transfers between devices, on_device(): parts = lax.all_to_all(parts, 'z', split_axis=0, concat_axis=0, tiled=True)  49.3 us
    all_gather x1, waiting for transfers between devices, on_device(): all_out = lax.all_gather(latent_out, ('z', 'c'), axis=0, tiled=True)  41.5 us
    all_to_all x1, blocking collectives, exchange(): lax.all_to_all(rows.reshape(groups, capacity, 2 * latent_width), ('z', 'c...  40.9 us
    all_gather x1, waiting for transfers between devices, on_device(): all_grad = lax.all_gather(latent_grad, ('z', 'c'), axis=0, tiled=True)  36.2 us
    dot_general x14, matrix products, dot(): lax.dot_general(left, right, dims, preferred_element_type=jnp.float32)  28.2 us
    all_to_all x1, blocking collectives, on_device(): grads = lax.all_to_all(grads, 'dp', split_axis=0, concat_axis=0, tiled=True)  22.2 us
    all_to_all x1, waiting for transfers between devices, exchange(): lax.all_to_all(rows.reshape(groups, capacity, 2 * latent_width), ('z', 'c...  20.9 us
  transfers between devices with their start and end apart: 11, of which 8 were waited for; matrix products, arithmetic and copies ran while one was open for 6% of the time, Pallas kernels for 0%

profile of v1, /device:TPU:8, one launch (start us, length us, event | category | flops | bytes accessed | tf_op | source)
XLA Modules:
  0.0 371.4 jit_solution(5906620332826413703)
XLA Ops:
  7.2 0.0 all-gather.5.cloned.1.call-start
  7.2 1.1 constant_dynamic-slice_fusion.1
  8.4 1.9 collective-permute-start
  10.3 2.4 collective-permute-start.1
  12.7 0.0 all-gather.5.cloned.1.call-update
  12.7 1.1 constant_dynamic-slice_fusion
  13.8 1.9 collective-permute-start.2
  15.7 2.4 collective-permute-start.3
  18.2 0.5 convolution_convert_fusion.3
  18.7 0.4 collective-permute-done.3
  19.1 0.5 convolution_convert_fusion.2
  19.6 1.7 copy_bitcast_fusion
  21.3 10.5 %all-to-all-start = ((bf16[8,128,1024]{1,2,0:T(8,128)(2,1)}), bf16[8,128,1024]{1,2,0:T(8,128)(2,1)S(1)}, u32[]{:S(2)}, u32[]{:S(2)}) async-start(bf16[8,128,1024]{1,2,0:T(8,128)(2,1)} %copy_bitcast_fusion), calls=%async_computation | async-start | bytes 4194304 | tf_op jit(solution)/shard_map/all_to_all | solution.py:66
  31.8 0.1 copy.64
  31.9 0.1 eq.42
  32.0 0.1 eq.38
  32.1 1.2 reduce-window.6
  33.3 0.2 slice_reduce_fusion
  33.5 0.1 fusion.48
  33.6 0.1 reduce_sum.54
  33.8 0.1 copy.67
  33.8 0.2 fusion.21
  34.0 0.2 select_reduce_fusion.1
  34.2 49.3 %all-to-all-done = bf16[8,128,1024]{1,2,0:T(8,128)(2,1)S(1)} async-done(((bf16[8,128,1024]{1,2,0:T(8,128)(2,1)}), bf16[8,128,1024]{1,2,0:T(8,128)(2,1)S(1)}, u32[]{:S(2)}, u32[]{:S(2)}) %all-to-all-start) | async-done | bytes 2097184 | tf_op jit(solution)/shard_map/all_to_all | solution.py:66
  83.5 0.4 reduce_sum.56
  83.9 0.5 fusion.55
  84.4 0.1 slice.88
  84.5 0.2 fusion.20
  84.7 1.2 pad_maximum_fusion
  85.9 3.7 all-to-all-start.1
  89.6 0.0 all-gather.7.cloned.1.call-start
  89.7 0.7 copy.70
  90.4 0.0 all-gather.11.cloned.1.call-start
  90.5 10.4 %all-gather.5.cloned.1.call-done = bf16[1,512,2688]{2,1,0:T(8,128)(2,1)} async-done(((bf16[1,16,2688]{2,1,0:T(8,128)(2,1)}), bf16[1,512,2688]{2,1,0:T(8,128)(2,1)}) %all-gather.5.cloned.1.call-update) | async-done | bytes 2752528 | tf_op jit(solution)/shard_map/all_gather | solution.py:49
  100.9 20.9 %all-to-all-done.1 = bf16[16,40,1024]{2,1,0:T(8,128)(2,1)S(1)} async-done(((bf16[16,40,1024]{2,1,0:T(8,128)(2,1)}), bf16[16,40,1024]{2,1,0:T(8,128)(2,1)S(1)}, u32[]{:S(2)}, u32[]{:S(2)}) %all-to-all-start.1) | async-done | bytes 1310752 | tf_op jit(solution)/shard_map/all_to_all | solution.py:80
  121.8 6.7 %fusion.6 = f32[640,2688]{1,0:T(8,128)} fusion(bf16[1,512,2688]{2,1,0:T(8,128)(2,1)} %all-gather.5.cloned.1.call-done, bf16[640,1024]{1,0:T(8,128)(2,1)S(1)} %bitcast.78), kind=kOutput, calls=%fused_computation.10 | convolution fusion | flops 1761607680 | bytes 10289152 | tf_op jit(solution)/shard_map/dot_general | solution.py:16
  128.4 58.0 %all-gather.7.cloned.1.call-done = bf16[1,1344,512]{2,0,1:T(2,128)(2,1)} async-done(((bf16[1,42,512]{2,0,1:T(2,128)(2,1)}), bf16[1,1344,512]{2,0,1:T(2,128)(2,1)}) %all-gather.7.cloned.1.call-update) | async-done | bytes 1376272 | tf_op jit(solution)/shard_map/all_gather | solution.py:50
  186.5 5.6 %multiply_convert_fusion.1 = (bf16[640,1344]{1,0:T(8,128)(2,1)S(1)}, bf16[640,1344]{1,0:T(8,128)(2,1)S(1)}) fusion(f32[640,2688]{1,0:T(8,128)} %fusion.6, bf16[1,1344,512]{2,0,1:T(2,128)(2,1)} %all-gather.7.cloned.1.call-done, bf16[640,1024]{1,0:T(8,128)(2,1)S(1)} %bitcast.79), kind=kOutput, calls=%fused_computation.1 | convolution fusion | flops 891985920 | bytes 12353536 | tf_op jit(solution)/shard_map/dot_general | solution.py:16
  192.1 0.2 copy-done.2
  192.3 0.8 copy-done.11
  193.1 2.1 fusion.12
  195.2 2.5 fusion.15
  197.6 0.1 pad_maximum_fusion.1
  197.8 0.7 copy.73
  198.4 40.9 %all_to_all.25 = bf16[16,40,1024]{2,1,0:T(8,128)(2,1)S(1)} all-to-all(bf16[16,40,1024]{2,1,0:T(8,128)(2,1)S(1)} %bitcast.77), channel_id=1, replica_groups=mesh['dp'=32,'z'=8,'c'=2] {'z','c'}, dimensions={0} | all-to-all | bytes 2621440 | tf_op jit(solution)/shard_map/all_to_all | solution.py:80
  239.3 1.0 convolution_convert_fusion.6
  240.3 0.0 all-gather.9.cloned.1.call-start
  240.4 0.3 fusion.27
  240.7 1.0 fusion.22
  241.7 36.2 %all-gather.11.cloned.1.call-done = bf16[2048,512]{1,0:T(8,128)(2,1)} async-done(((bf16[128,512]{1,0:T(8,128)(2,1)}), bf16[2048,512]{1,0:T(8,128)(2,1)}) %all-gather.11.cloned.1.call-update) | async-done | bytes 2097168 | tf_op jit(solution)/shard_map/all_gather | solution.py:108
  277.9 2.3 convolution_convert_fusion.4
  280.2 41.5 %all-gather.9.cloned.1.call-done = bf16[2048,512]{1,0:T(8,128)(2,1)} async-done(((bf16[128,512]{1,0:T(8,128)(2,1)}), bf16[2048,512]{1,0:T(8,128)(2,1)}) %all-gather.9.cloned.1.call-update) | async-done | bytes 2097168 | tf_op jit(solution)/shard_map/all_gather | solution.py:107
  321.7 2.3 convolution_convert_fusion.5
  324.1 22.2 %all_to_all.26 = bf16[32,16,256]{2,1,0:T(8,128)(2,1)S(1)} all-to-all(bf16[32,16,256]{2,1,0:T(8,128)(2,1)S(1)} %pad_maximum_fusion.2), channel_id=1, replica_groups=mesh['dp'=32,'z'=8,'c'=2] {'dp'}, dimensions={0} | all-to-all | bytes 524288 | tf_op jit(solution)/shard_map/all_to_all | solution.py:115
  346.4 0.1 reduce_sum.58
  346.4 0.7 broadcast_in_dim.16
  347.1 4.6 %all-to-all-start.4 = ((bf16[32,16,256]{2,1,0:T(8,128)(2,1)}), bf16[32,16,256]{2,1,0:T(8,128)(2,1)S(1)}, u32[]{:S(2)}, u32[]{:S(2)}) async-start(bf16[32,16,256]{2,1,0:T(8,128)(2,1)} %broadcast_in_dim.16), calls=%async_computation.4 | async-start | bytes 524288 | tf_op jit(solution)/shard_map/all_to_all | solution.py:118
  351.8 1.5 convolution_convert_fusion
  353.3 0.1 copy-done.1
  353.4 1.5 convolution_convert_fusion.1
  354.9 8.4 %all-to-all-done.4 = bf16[32,16,256]{2,1,0:T(8,128)(2,1)S(1)} async-done(((bf16[32,16,256]{2,1,0:T(8,128)(2,1)}), bf16[32,16,256]{2,1,0:T(8,128)(2,1)S(1)}, u32[]{:S(2)}, u32[]{:S(2)}) %all-to-all-start.4) | async-done | bytes 262176 | tf_op jit(solution)/shard_map/all_to_all | solution.py:118
  363.3 0.1 convert_multiply_fusion
  363.3 0.7 fusion.54
  364.1 0.8 copy.74
  (32 shorter events, 0.2 us)
Async XLA Ops:
  7.2 11.0 %copy-start.6 = (bf16[128,512]{1,0:T(8,128)(2,1)S(1)}, bf16[128,512]{1,0:T(8,128)(2,1)}, u32[]{:S(2)}) copy-start(bf16[128,512]{1,0:T(8,128)(2,1)} %param.10) | copy-start | bytes 393220
  7.2 8.6 %copy-start.7 = (bf16[512,128]{1,0:T(8,128)(2,1)S(1)}, bf16[512,128]{1,0:T(8,128)(2,1)}, u32[]{:S(2)}) copy-start(bf16[512,128]{1,0:T(8,128)(2,1)} %param.11) | copy-start | bytes 393220
  7.2 93.7 %all-gather.5.cloned.1.call-start = ((), (), s32[]{:S(2)}) async-start(), calls=%async_computation.5 | async-start | bytes 2838528 | tf_op jit(solution)/shard_map/all_gather | solution.py:49
  8.4 9.8 %collective-permute-start = (bf16[8,128,128]{2,1,0:T(8,128)(2,1)S(1)}, bf16[8,128,128]{2,1,0:T(8,128)(2,1)S(1)}, u32[]{:S(2)}, u32[]{:S(2)}) collective-permute-start(bf16[8,128,128]{2,1,0:T(8,128)(2,1)S(1)} %get-tuple-element.35), channel_id=1, source_target_pairs={{0,1},{1,0},{2,3},{3,2},{4,5},{5,4},{6,7},{7,6},{8,9},{9,8},{10,11... | collective-permute-start | bytes 786440 | tf_op jit(solution)/shard_map/ppermute | solution.py:58
  10.3 7.9 %collective-permute-start.1 = (bf16[128,512]{1,0:T(8,128)(2,1)}, bf16[128,512]{1,0:T(8,128)(2,1)S(1)}, u32[]{:S(2)}, u32[]{:S(2)}) collective-permute-start(bf16[128,512]{1,0:T(8,128)(2,1)} %param.10), channel_id=1, source_target_pairs={{0,1},{1,0},{2,3},{3,2},{4,5},{5,4},{6,7},{7,6},{8,9},{9,8},{10,11... | collective-permute-start | bytes 393224 | tf_op jit(solution)/shard_map/ppermute | solution.py:61
  13.8 5.3 %collective-permute-start.2 = (bf16[8,128,128]{2,1,0:T(8,128)(2,1)S(1)}, bf16[8,128,128]{2,1,0:T(8,128)(2,1)S(1)}, u32[]{:S(2)}, u32[]{:S(2)}) collective-permute-start(bf16[8,128,128]{2,1,0:T(8,128)(2,1)S(1)} %get-tuple-element.37), channel_id=1, source_target_pairs={{0,1},{1,0},{2,3},{3,2},{4,5},{5,4},{6,7},{7,6},{8,9},{9,8},{10,11... | collective-permute-start | bytes 786440 | tf_op jit(solution)/shard_map/ppermute | solution.py:58
  15.7 3.4 collective-permute-start.3
  21.3 10.5 %copy-start.9 = (s32[128,4]{0,1:T(4,128)S(1)}, s32[128,4]{0,1:T(4,128)}, u32[]{:S(2)}) copy-start(s32[128,4]{0,1:T(4,128)} %param.12) | copy-start | bytes 6148
  21.3 12.7 %copy-start.10 = (f32[128,4]{0,1:T(4,128)S(1)}, f32[128,4]{0,1:T(4,128)}, u32[]{:S(2)}) copy-start(f32[128,4]{0,1:T(4,128)} %param.13) | copy-start | bytes 6148
  21.3 62.2 %all-to-all-start = ((bf16[8,128,1024]{1,2,0:T(8,128)(2,1)}), bf16[8,128,1024]{1,2,0:T(8,128)(2,1)S(1)}, u32[]{:S(2)}, u32[]{:S(2)}) async-start(bf16[8,128,1024]{1,2,0:T(8,128)(2,1)} %copy_bitcast_fusion), calls=%async_computation | async-start | bytes 4194304 | tf_op jit(solution)/shard_map/all_to_all | solution.py:66
  84.7 5.0 %copy-start.8 = (bf16[1,42,512]{2,1,0:T(8,128)(2,1)S(1)}, bf16[1,42,512]{2,1,0:T(8,128)(2,1)}, u32[]{:S(2)}) copy-start(bf16[1,42,512]{2,1,0:T(8,128)(2,1)} %param.15) | copy-start | bytes 129028
  85.9 35.8 %all-to-all-start.1 = ((bf16[16,40,1024]{2,1,0:T(8,128)(2,1)}), bf16[16,40,1024]{2,1,0:T(8,128)(2,1)S(1)}, u32[]{:S(2)}, u32[]{:S(2)}) async-start(bf16[16,40,1024]{2,1,0:T(8,128)(2,1)} %pad_maximum_fusion), calls=%async_computation.1 | async-start | bytes 2621440 | tf_op jit(solution)/shard_map/all_to_all | solution.py:80
  89.6 96.8 %all-gather.7.cloned.1.call-start = ((), (), s32[]{:S(2)}) async-start(), calls=%async_computation.6 | async-start | bytes 2838528 | tf_op jit(solution)/shard_map/all_gather | solution.py:50
  90.4 187.4 %all-gather.11.cloned.1.call-start = ((), (), s32[]{:S(2)}) async-start(), calls=%async_computation.8 | async-start | bytes 2228224 | tf_op jit(solution)/shard_map/all_gather | solution.py:108
  186.5 5.9 %copy-start.2 = (f32[640,2688]{1,0:T(8,128)S(1)}, f32[640,2688]{1,0:T(8,128)}, u32[]{:S(2)}) copy-start(f32[640,2688]{1,0:T(8,128)} %fusion.6) | copy-start | bytes 20643844
  186.5 6.6 %copy-start.11 = (bf16[1,1344,512]{2,0,1:T(2,128)(2,1)S(1)}, bf16[1,1344,512]{2,0,1:T(2,128)(2,1)}, u32[]{:S(2)}) copy-start(bf16[1,1344,512]{2,0,1:T(2,128)(2,1)} %all-gather.7.cloned.1.call-done) | copy-start | bytes 4128772
  193.1 2.1 copy-start.3
  239.3 38.5 %copy-start.4 = (bf16[2048,128]{1,0:T(8,128)(2,1)S(1)}, bf16[2048,128]{1,0:T(8,128)(2,1)}, u32[]{:S(2)}) copy-start(bf16[2048,128]{1,0:T(8,128)(2,1)} %param.8) | copy-start | bytes 1572868
  240.3 81.4 %all-gather.9.cloned.1.call-start = ((), (), s32[]{:S(2)}) async-start(), calls=%async_computation.7 | async-start | bytes 2228224 | tf_op jit(solution)/shard_map/all_gather | solution.py:107
  240.7 81.1 %copy-start.5 = (bf16[2048,128]{1,0:T(8,128)(2,1)S(1)}, bf16[2048,128]{1,0:T(8,128)(2,1)}, u32[]{:S(2)}) copy-start(bf16[2048,128]{1,0:T(8,128)(2,1)} %param.9) | copy-start | bytes 1572868
  280.2 71.5 %copy-start = (bf16[2048,512]{1,0:T(8,128)(2,1)S(1)}, bf16[2048,512]{1,0:T(8,128)(2,1)}, u32[]{:S(2)}) copy-start(bf16[2048,512]{1,0:T(8,128)(2,1)} %all-gather.11.cloned.1.call-done) | copy-start | bytes 6291460
  347.1 16.1 %all-to-all-start.4 = ((bf16[32,16,256]{2,1,0:T(8,128)(2,1)}), bf16[32,16,256]{2,1,0:T(8,128)(2,1)S(1)}, u32[]{:S(2)}, u32[]{:S(2)}) async-start(bf16[32,16,256]{2,1,0:T(8,128)(2,1)} %broadcast_in_dim.16), calls=%async_computation.4 | async-start | bytes 524288 | tf_op jit(solution)/shard_map/all_to_all | solution.py:118
  351.8 1.6 copy-start.1
Sparse Core Ops, SparseCore 0:
  12.8 87.9 all-gather.4
  104.6 81.7 all-gather.6
  240.5 37.3 all-gather.10
  280.4 41.2 all-gather.8

commit v2 on v1

v2 whole, which is shorter than its diff:
```python
import math

import jax
import jax.numpy as jnp
from jax import lax
from jax.experimental import pallas as pl
from jax.experimental.pallas import tpu as pltpu
from jax.sharding import Mesh
from jax.sharding import PartitionSpec as P

TOPK = 4
CORES = 2
CHUNK = 256
INNER = (((1,), (0,)), ((), ()))
COLS = (((1,), (1,)), ((), ()))
ROWS = (((0,), (0,)), ((), ()))


def dot(left, right, dims=INNER):
    return lax.dot_general(left, right, dims, preferred_element_type=jnp.float32)


def slot_tables(routes, gate_weights, experts, capacity):
    flat_routes = routes.reshape(-1)
    onehot = (flat_routes[:, None] == jnp.arange(experts, dtype=jnp.int32)[None, :]).astype(
        jnp.int32
    )
    before = jnp.cumsum(onehot, axis=0) - onehot
    position = jnp.sum(before * onehot, axis=1)
    slot = (flat_routes * capacity + position).reshape(routes.shape)
    slot_ids = jnp.arange(experts * capacity, dtype=jnp.int32)
    matches = slot.T[:, None, :] == slot_ids[None, :, None]
    spread = jnp.any(matches, axis=0)
    weighted = jnp.sum(jnp.where(matches, gate_weights.T[:, None, :], 0.0), axis=0)
    return spread.astype(jnp.bfloat16), weighted


def packed_weights(expert_in, expert_out, dp):
    in_rows, width = expert_in.shape[1:]
    own, latent_width = expert_out.shape[1:]
    hidden = width // 2
    tiles = -(-own // in_rows)
    place = jnp.arange(tiles * dp * in_rows, dtype=jnp.int32)
    tile, device, row = place // (dp * in_rows), place // in_rows % dp, place % in_rows
    unit = tile * in_rows + row
    source = jnp.where(unit < own, device * own + unit, -1)
    pick = (jnp.arange(hidden, dtype=jnp.int32)[:, None] == source[None, :]).astype(jnp.bfloat16)
    both = jnp.concatenate([expert_in[0, :, :hidden], expert_in[0, :, hidden:]], axis=0)
    both = dot(both, pick).astype(jnp.bfloat16)
    rows = jnp.pad(expert_out[0], ((0, tiles * in_rows - own), (0, 0)))
    rows = [rows[t * in_rows : (t + 1) * in_rows] for t in range(tiles)]
    return jnp.concatenate([both[:in_rows], both[in_rows:], *rows], axis=1)


def expert_kernel(rows_ref, gate_ref, up_ref, out_ref, result_ref, sum_out, sum_grad):
    step = pl.program_id(0)
    latent_width = sum_out.shape[1]

    @pl.when(step == 0)
    def _():
        sum_out[...] = jnp.zeros_like(sum_out)
        sum_grad[...] = jnp.zeros_like(sum_grad)

    rows = rows_ref[:, :latent_width]
    gate_part = dot(rows, gate_ref[...])
    up_part = dot(rows, up_ref[...])
    grad_act = dot(rows_ref[:, latent_width:], out_ref[...], COLS)
    sigmoid_gate = jax.nn.sigmoid(gate_part)
    silu = gate_part * sigmoid_gate
    sum_out[...] += dot((silu * up_part).astype(jnp.bfloat16), out_ref[...])
    grad_gate = grad_act * up_part * sigmoid_gate * (1.0 + gate_part * (1.0 - sigmoid_gate))
    sum_grad[...] += dot(grad_gate.astype(jnp.bfloat16), gate_ref[...], COLS)
    sum_grad[...] += dot((grad_act * silu).astype(jnp.bfloat16), up_ref[...], COLS)

    @pl.when(step == pl.num_programs(0) - 1)
    def _():
        result_ref[:, :latent_width] = sum_out[...].astype(jnp.bfloat16)
        result_ref[:, latent_width:] = sum_grad[...].astype(jnp.bfloat16)


def run_expert(rows, weights):
    count, latent_width = rows.shape[0], rows.shape[1] // 2
    padded = weights.shape[1] // 3
    steps = padded // CHUNK
    halves = latent_width // CHUNK
    out_base = 2 * padded // latent_width
    return pl.pallas_call(
        expert_kernel,
        grid=(steps,),
        in_specs=[
            pl.BlockSpec((count, 2 * latent_width), lambda j: (0, 0)),
            pl.BlockSpec((latent_width, CHUNK), lambda j: (0, j)),
            pl.BlockSpec((latent_width, CHUNK), lambda j: (0, steps + j)),
            pl.BlockSpec((CHUNK, latent_width), lambda j: (j % halves, out_base + j // halves)),
        ],
        out_specs=pl.BlockSpec((count, 2 * latent_width), lambda j: (0, 0)),
        out_shape=jax.ShapeDtypeStruct((count, 2 * latent_width), jnp.bfloat16),
        scratch_shapes=[pltpu.VMEM((count, latent_width), jnp.float32)] * 2,
        compiler_params=pltpu.CompilerParams(vmem_limit_bytes=32 * 1024 * 1024),
        cost_estimate=pl.CostEstimate(
            flops=12 * count * latent_width * padded,
            bytes_accessed=2 * (weights.size + 2 * rows.size),
            transcendentals=count * padded,
        ),
    )(rows, weights, weights, weights)


def on_device(tokens, cotangent, down_proj, up_proj, routes, gate_weights, expert_in, expert_out):
    expert = ("z", "c")
    chips = lax.axis_size("z")
    core = lax.axis_index("c")
    groups = chips * CORES
    dp = lax.axis_size("dp")
    tok_rows = routes.shape[0]
    group_rows = tokens.shape[0]
    features = tokens.shape[1]
    latent_width = down_proj.shape[1]
    capacity = min(tok_rows, tok_rows * TOPK * 5 // (4 * groups))
    slot_count = groups * capacity
    grad_scale = 1.0 / math.sqrt(group_rows * dp)
    bf16 = jnp.bfloat16

    swap = [(0, 1), (1, 0)]

    def partial_latent(rows, weights_here, column_dims):
        blocks = rows.reshape(chips, CORES, tok_rows, features)
        kept = lax.dynamic_index_in_dim(blocks, core, 1, keepdims=False)
        given = lax.dynamic_index_in_dim(blocks, 1 - core, 1, keepdims=False)
        got = lax.ppermute(given, "c", swap)
        weights_there = lax.ppermute(weights_here, "c", swap)
        kept = kept.reshape(chips * tok_rows, features)
        got = got.reshape(chips * tok_rows, features)
        part = dot(kept, weights_here, column_dims) + dot(got, weights_there, column_dims)
        return part.astype(bf16).reshape(chips, tok_rows, latent_width)

    weights = lax.all_gather(packed_weights(expert_in, expert_out, dp), "dp", axis=0, tiled=True)

    spread, weighted = slot_tables(routes, gate_weights, groups, capacity)
    slot_gate = jnp.sum(weighted, axis=1, keepdims=True)
    gate_high = weighted.astype(bf16)
    gate_low = (weighted - gate_high.astype(jnp.float32)).astype(bf16)

    def exchange(rows):
        return lax.all_to_all(
            rows.reshape(groups, capacity, rows.shape[1]),
            expert,
            split_axis=0,
            concat_axis=0,
            tiled=True,
        ).reshape(slot_count, rows.shape[1])

    latent = partial_latent(tokens, down_proj, INNER).reshape(chips * tok_rows, latent_width)
    latent = lax.psum_scatter(latent, "z", scatter_dimension=0, tiled=True)
    parts = partial_latent(cotangent, up_proj, COLS)
    parts = lax.all_to_all(parts, "z", split_axis=0, concat_axis=0, tiled=True)
    latent_out_grad = jnp.sum(parts.astype(jnp.float32), axis=0).astype(bf16)
    outgoing = [dot(spread, latent), dot(spread, latent_out_grad) * slot_gate]
    result = run_expert(exchange(jnp.concatenate(outgoing, axis=1).astype(bf16)), weights)
    returned = exchange(result)
    returned_out = returned[:, :latent_width]
    latent_out = (dot(gate_high, returned_out, ROWS) + dot(gate_low, returned_out, ROWS)).astype(
        bf16
    )
    latent_grad = dot(spread, returned[:, latent_width:], ROWS).astype(bf16)

    latents = jnp.concatenate([latent_out, latent_grad], axis=1)
    latents = lax.all_gather(latents, expert, axis=0, tiled=True)
    all_out = latents[:, :latent_width]
    all_grad = latents[:, latent_width:]
    up_part_grad = dot(all_out, cotangent, ROWS)
    down_part_grad = dot(all_grad, tokens, ROWS)
    grads = jnp.concatenate([up_part_grad, down_part_grad], axis=1).astype(bf16)
    grads = grads.reshape(dp, latent_width // dp, 2 * features)
    grads = lax.all_to_all(grads, "dp", split_axis=0, concat_axis=0, tiled=True)
    mixed = dot(all_out, up_proj).astype(bf16)
    input_grad = dot(all_grad, down_proj, COLS).astype(bf16)
    summed = jnp.sum(grads.astype(jnp.float32), axis=0).astype(bf16)
    summed = jnp.broadcast_to(summed[None], grads.shape)
    summed = lax.all_to_all(summed, "dp", split_axis=0, concat_axis=0, tiled=True)
    summed = summed.reshape(latent_width, 2 * features).astype(jnp.float32) * grad_scale
    return mixed, input_grad, summed[:, features:].T, summed[:, :features]


def solution(mesh):
    dp, experts = mesh.devices.shape
    fine = Mesh(mesh.devices.reshape(dp, experts // CORES, CORES), ("dp", "z", "c"))
    expert = ("z", "c")
    in_specs = (
        P("dp", expert),
        P("dp", expert),
        P(expert, None),
        P(None, expert),
        P(("dp", "z", "c"), None),
        P(("dp", "z", "c"), None),
        P(expert, "dp", None),
        P(expert, "dp", None),
    )
    out_specs = (P("dp", expert), P("dp", expert), P(expert, None), P(None, expert))
    return jax.shard_map(
        on_device, mesh=fine, in_specs=in_specs, out_specs=out_specs, check_vma=False
    )
```

time: 372 us -> 261 us (0.70)
  waiting for transfers between devices: 225 us -> 81.3 us
  blocking collectives: 63.2 us -> 102 us
  matrix products: 28.2 us -> 18.2 us
  Pallas kernels: 0 us -> 8.51 us
  starting transfers between devices: 27.6 us -> 23.8 us
    all_gather x4 -> x2, waiting for transfers between devices: 146 us -> 40.7 us  [the longest x1 40.7 us: on_device(): latents = lax.all_gather(latents, expert, axis=0, tiled=True)]
    all_to_all x1 -> x2, blocking collectives: 40.9 us -> 79.7 us  [exchange(): lax.all_to_all(rows.reshape(groups, capacity, rows.shape[1]), expert, spl...]
    all_to_all x1 -> x0, waiting for transfers between devices: 20.9 us -> none  [exchange(): lax.all_to_all(rows.reshape(groups, capacity, 2 * latent_width), ('z', 'c...]
    all_to_all x1, waiting for transfers between devices: 49.3 us -> 32 us  [on_device(): parts = lax.all_to_all(parts, 'z', split_axis=0, concat_axis=0, tiled=True)]
    dot_general x14, matrix products: 28.2 us -> 18.2 us  [dot(): lax.dot_general(left, right, dims, preferred_element_type=jnp.float32)]
    pallas_call x0 -> x1, Pallas kernels: none -> 8.51 us  [run_expert(): pl.pallas_call(expert_kernel, grid=(steps,), in_specs=[pl.BlockSpec((coun...]
  transfers between devices with their start and end apart: 11 -> 9, of which waited for: 8 -> 5; matrix products, arithmetic and copies ran while one was open for 6% -> 6% of each run, Pallas kernels for 0% -> 0%
where the time goes in v2:
time: 261 us; the launch traced here: 260 us
  blocking collectives  102 us (39%)
  waiting for transfers between devices  81.3 us (31%)
  starting transfers between devices  23.8 us (9%)
  matrix products  18.2 us (7%)
  between operations  15.8 us (6%)
  Pallas kernels  8.51 us (3%)
  local copies, waits for them, and re-layouts  7.59 us (3%)
  other arithmetic  2.89 us (1%)
    all_to_all x2, blocking collectives, exchange(): lax.all_to_all(rows.reshape(groups, capacity, rows.shape[1]), expert, spl...  79.7 us
    all_gather x1, waiting for transfers between devices, on_device(): latents = lax.all_gather(latents, expert, axis=0, tiled=True)  40.7 us
    all_to_all x1, waiting for transfers between devices, on_device(): parts = lax.all_to_all(parts, 'z', split_axis=0, concat_axis=0, tiled=True)  32 us
    all_to_all x1, blocking collectives, on_device(): grads = lax.all_to_all(grads, 'dp', split_axis=0, concat_axis=0, tiled=True)  22.4 us
    dot_general x14, matrix products, dot(): lax.dot_general(left, right, dims, preferred_element_type=jnp.float32)  18.2 us
    all_to_all x1, starting transfers between devices, on_device(): parts = lax.all_to_all(parts, 'z', split_axis=0, concat_axis=0, tiled=True)  10.4 us
    pallas_call x1, Pallas kernels, run_expert(): pl.pallas_call(expert_kernel, grid=(steps,), in_specs=[pl.BlockSpec((coun...  8.51 us
    all_to_all x1, waiting for transfers between devices, on_device(): lax.all_to_all(summed, 'dp', split_axis=0, concat_axis=0, tiled=True)  5.31 us
  transfers between devices with their start and end apart: 9, of which 5 were waited for; matrix products, arithmetic and copies ran while one was open for 6% of the time, Pallas kernels for 0%

profile of v2, /device:TPU:8, one launch (start us, length us, event | category | flops | bytes accessed | tf_op | source)
XLA Modules:
  0.0 260.2 jit_solution(4410841984134919721)
XLA Ops:
  8.0 0.0 reduce-scatter.2.cloned.1.call-start
  8.0 1.1 dynamic-slice_bitcast_fusion.1
  9.1 1.9 collective-permute-start
  11.1 2.4 collective-permute-start.1
  13.5 1.3 fusion.50
  14.8 0.0 copy-start.7
  14.8 1.5 add_convert_fusion.1
  16.3 0.0 reduce-scatter.2.cloned.1.call-update
  16.3 0.0 all-gather.3.cloned.1.call-start
  16.4 0.1 slice_bitcast_fusion.2
  16.5 0.0 copy-start.6
  16.5 1.7 fusion.2
  18.2 0.0 copy-start.3
  18.2 0.7 copy-done.3
  18.9 0.0 all-gather.3.cloned.1.call-update
  19.0 2.1 collective-permute-start.2
  21.1 2.2 collective-permute-start.3
  23.3 0.4 fusion.51
  23.8 0.6 collective-permute-done.3
  24.3 0.0 collective-permute-done.2
  24.3 1.4 add_convert_fusion
  25.8 10.4 %all-to-all-start = ((bf16[8,128,512]{2,1,0:T(8,128)(2,1)}), bf16[8,128,512]{2,1,0:T(8,128)(2,1)S(1)}, u32[]{:S(2)}, u32[]{:S(2)}) async-start(bf16[8,128,512]{2,1,0:T(8,128)(2,1)} %bitcast.13), calls=%async_computation.1 | async-start | bytes 2097152 | tf_op jit(solution)/shard_map/all_to_all | solution.py:155
  36.2 0.0 all-gather.5.cloned.1.call-start
  36.3 0.1 copy.27
  36.4 0.1 eq.58
  36.5 0.1 eq.54
  36.6 1.2 reduce-window.6
  37.8 0.2 slice_reduce_fusion
  38.0 0.1 fusion.30
  38.1 0.1 reduce_sum.54
  38.2 0.1 copy.30
  38.3 0.2 fusion.10
  38.5 0.2 select_reduce_fusion.1
  38.7 32.0 %all-to-all-done = bf16[8,128,512]{2,1,0:T(8,128)(2,1)S(1)} async-done(((bf16[8,128,512]{2,1,0:T(8,128)(2,1)}), bf16[8,128,512]{2,1,0:T(8,128)(2,1)S(1)}, u32[]{:S(2)}, u32[]{:S(2)}) %all-to-all-start) | async-done | bytes 1048608 | tf_op jit(solution)/shard_map/all_to_all | solution.py:155
  70.7 0.1 reduce_sum.56
  70.9 0.3 fusion.9
  71.2 2.7 %reduce-scatter.2.cloned.1.call-done = bf16[128,512]{1,0:T(8,128)(2,1)} async-done(((bf16[1024,512]{1,0:T(8,128)(2,1)}), bf16[128,512]{1,0:T(8,128)(2,1)}) %reduce-scatter.2.cloned.1.call-update) | async-done | bytes 131088 | tf_op jit(solution)/shard_map/reduce_scatter | solution.py:153
  73.9 1.2 convolution_convert_fusion.2
  75.1 0.2 pad_maximum_fusion
  75.3 41.3 %all_to_all.25 = bf16[16,40,1024]{2,1,0:T(8,128)(2,1)S(1)} all-to-all(bf16[16,40,1024]{2,1,0:T(8,128)(2,1)S(1)} %pad_maximum_fusion), channel_id=1, replica_groups=mesh['dp'=32,'z'=8,'c'=2] {'z','c'}, dimensions={0} | all-to-all | bytes 2621440 | tf_op jit(solution)/shard_map/all_to_all | solution.py:144
  116.5 2.3 copy-done
  118.9 8.5 %shard_map.111 = bf16[640,1024]{1,0:T(8,128)(2,1)S(1)} custom-call(bf16[640,1024]{1,0:T(8,128)(2,1)S(1)} %bitcast.71, bf16[512,4608]{1,0:T(8,128)(2,1)S(1)} %copy-done, bf16[512,4608]{1,0:T(8,128)(2,1)S(1)} %copy-done, bf16[512,4608]{1,0:T(8,128)(2,1)S(1)} %copy-done), custom_call_target="tpu_custom_call" | custom-call | flops 6039797760 | bytes 7340032 | tf_op jit(solution)/shard_map/pallas_call | solution.py:87
  127.4 38.4 %all_to_all.26 = bf16[16,40,1024]{2,1,0:T(8,128)(2,1)S(1)} all-to-all(bf16[16,40,1024]{2,1,0:T(8,128)(2,1)S(1)} %bitcast.72), channel_id=1, replica_groups=mesh['dp'=32,'z'=8,'c'=2] {'z','c'}, dimensions={0} | all-to-all | bytes 2621440 | tf_op jit(solution)/shard_map/all_to_all | solution.py:144
  165.8 0.3 convolution_convert_fusion.3
  166.1 0.3 fusion.20
  166.4 0.3 fusion.11
  166.7 0.7 pad_maximum_fusion.1
  167.5 0.0 all-gather.5.cloned.1.call-update
  167.5 0.0 copy-start.2
  167.5 40.7 %all-gather.5.cloned.1.call-done = bf16[2048,1024]{1,0:T(8,128)(2,1)} async-done(((bf16[128,1024]{1,0:T(8,128)(2,1)}), bf16[2048,1024]{1,0:T(8,128)(2,1)}) %all-gather.5.cloned.1.call-update) | async-done | bytes 4194320 | tf_op jit(solution)/shard_map/all_gather | solution.py:167
  208.2 2.5 fusion.12
  210.7 0.3 copy-done.10
  211.0 0.8 fusion.15
  211.8 0.0 copy-start.5
  211.9 22.4 %all_to_all.27 = bf16[32,16,256]{2,1,0:T(8,128)(2,1)S(1)} all-to-all(bf16[32,16,256]{2,1,0:T(8,128)(2,1)S(1)} %pad_maximum_fusion.2), channel_id=1, replica_groups=mesh['dp'=32,'z'=8,'c'=2] {'dp'}, dimensions={0} | all-to-all | bytes 524288 | tf_op jit(solution)/shard_map/all_to_all | solution.py:174
  234.2 0.1 reduce_sum.58
  234.3 0.7 broadcast_in_dim.18
  235.0 4.6 %all-to-all-start.4 = ((bf16[32,16,256]{2,1,0:T(8,128)(2,1)}), bf16[32,16,256]{2,1,0:T(8,128)(2,1)S(1)}, u32[]{:S(2)}, u32[]{:S(2)}) async-start(bf16[32,16,256]{2,1,0:T(8,128)(2,1)} %broadcast_in_dim.18), calls=%async_computation.5 | async-start | bytes 524288 | tf_op jit(solution)/shard_map/all_to_all | solution.py:179
  239.6 3.1 %convolution_convert_fusion = bf16[2048,128]{1,0:T(8,128)(2,1)} fusion(bf16[128,512]{1,0:T(8,128)(2,1)S(1)} %copy-done.5, bf16[2048,1024]{1,0:T(8,128)(2,1)} %all-gather.5.cloned.1.call-done), kind=kOutput, calls=%fused_computation.3 | convolution fusion | flops 268697600 | bytes 2752512 | tf_op jit(solution)/shard_map/dot_general | solution.py:20
  242.7 3.1 %convolution_convert_fusion.1 = bf16[2048,128]{1,0:T(8,128)(2,1)} fusion(bf16[512,128]{1,0:T(8,128)(2,1)S(1)} %copy-done.6, bf16[2048,1024]{1,0:T(8,128)(2,1)} %all-gather.5.cloned.1.call-done), kind=kOutput, calls=%fused_computation.4 | convolution fusion | flops 268697600 | bytes 2752512 | tf_op jit(solution)/shard_map/dot_general | solution.py:20
  245.8 5.3 %all-to-all-done.4 = bf16[32,16,256]{2,1,0:T(8,128)(2,1)S(1)} async-done(((bf16[32,16,256]{2,1,0:T(8,128)(2,1)}), bf16[32,16,256]{2,1,0:T(8,128)(2,1)S(1)}, u32[]{:S(2)}, u32[]{:S(2)}) %all-to-all-start.4) | async-done | bytes 262176 | tf_op jit(solution)/shard_map/all_to_all | solution.py:179
  251.1 0.1 convert_multiply_fusion
  251.2 0.7 fusion.49
  251.9 0.8 copy.31
  (29 shorter events, 0.2 us)
Async XLA Ops:
  8.0 65.9 %reduce-scatter.2.cloned.1.call-start = ((), (), s32[]{:S(2)}) async-start(), calls=%async_computation.6 | async-start | bytes 1179648 | tf_op jit(solution)/shard_map/reduce_scatter | solution.py:153
  9.1 5.7 %collective-permute-start = (bf16[8,128,128]{2,1,0:T(8,128)(2,1)S(1)}, bf16[8,128,128]{2,1,0:T(8,128)(2,1)S(1)}, u32[]{:S(2)}, u32[]{:S(2)}) collective-permute-start(bf16[8,128,128]{2,1,0:T(8,128)(2,1)S(1)} %get-tuple-element.24), channel_id=1, source_target_pairs={{0,1},{1,0},{2,3},{3,2},{4,5},{5,4},{6,7},{7,6},{8,9},{9,8},{10,11... | collective-permute-start | bytes 786440 | tf_op jit(solution)/shard_map/ppermute | solution.py:129
  11.1 3.8 %collective-permute-start.1 = (bf16[128,512]{1,0:T(8,128)(2,1)}, bf16[128,512]{1,0:T(8,128)(2,1)S(1)}, u32[]{:S(2)}, u32[]{:S(2)}) collective-permute-start(bf16[128,512]{1,0:T(8,128)(2,1)} %param.10), channel_id=1, source_target_pairs={{0,1},{1,0},{2,3},{3,2},{4,5},{5,4},{6,7},{7,6},{8,9},{9,8},{10,11... | collective-permute-start | bytes 393224 | tf_op jit(solution)/shard_map/ppermute | solution.py:130
  14.8 1.5 copy-start.7
  16.3 1.9 copy-start.4
  16.3 2.6 %copy-start.1 = (bf16[2048,128]{1,0:T(8,128)(2,1)S(1)}, bf16[2048,128]{1,0:T(8,128)(2,1)}, u32[]{:S(2)}) copy-start(bf16[2048,128]{1,0:T(8,128)(2,1)} %param.9) | copy-start | bytes 1572868
  16.3 100.2 %all-gather.3.cloned.1.call-start = ((), (), s32[]{:S(2)}) async-start(), calls=%async_computation.7 | async-start | bytes 4866048 | tf_op jit(solution)/shard_map/all_gather | solution.py:136
  16.5 4.6 %copy-start.6 = (bf16[512,128]{1,0:T(8,128)(2,1)S(1)}, bf16[512,128]{1,0:T(8,128)(2,1)}, u32[]{:S(2)}) copy-start(bf16[512,128]{1,0:T(8,128)(2,1)} %param.11) | copy-start | bytes 393220
  18.2 0.7 copy-start.3
  19.0 5.3 %collective-permute-start.2 = (bf16[8,128,128]{2,1,0:T(8,128)(2,1)S(1)}, bf16[8,128,128]{2,1,0:T(8,128)(2,1)S(1)}, u32[]{:S(2)}, u32[]{:S(2)}) collective-permute-start(bf16[8,128,128]{2,1,0:T(8,128)(2,1)S(1)} %get-tuple-element.26), channel_id=1, source_target_pairs={{0,1},{1,0},{2,3},{3,2},{4,5},{5,4},{6,7},{7,6},{8,9},{9,8},{10,11... | collective-permute-start | bytes 786440 | tf_op jit(solution)/shard_map/ppermute | solution.py:129
  21.1 3.2 %collective-permute-start.3 = (bf16[512,128]{1,0:T(8,128)(2,1)S(1)}, bf16[512,128]{1,0:T(8,128)(2,1)S(1)}, u32[]{:S(2)}, u32[]{:S(2)}) collective-permute-start(bf16[512,128]{1,0:T(8,128)(2,1)S(1)} %copy-done.6), channel_id=1, source_target_pairs={{0,1},{1,0},{2,3},{3,2},{4,5},{5,4},{6,7},{7,6},{8,9},{9,8},{10,11... | collective-permute-start | bytes 393224 | tf_op jit(solution)/shard_map/ppermute | solution.py:130
  24.3 11.9 %copy-start.8 = (s32[128,4]{0,1:T(4,128)S(1)}, s32[128,4]{0,1:T(4,128)}, u32[]{:S(2)}) copy-start(s32[128,4]{0,1:T(4,128)} %param.12) | copy-start | bytes 6148
  25.8 12.7 %copy-start.9 = (f32[128,4]{0,1:T(4,128)S(1)}, f32[128,4]{0,1:T(4,128)}, u32[]{:S(2)}) copy-start(f32[128,4]{0,1:T(4,128)} %param.13) | copy-start | bytes 6148
  25.8 45.0 %all-to-all-start = ((bf16[8,128,512]{2,1,0:T(8,128)(2,1)}), bf16[8,128,512]{2,1,0:T(8,128)(2,1)S(1)}, u32[]{:S(2)}, u32[]{:S(2)}) async-start(bf16[8,128,512]{2,1,0:T(8,128)(2,1)} %bitcast.13), calls=%async_computation.1 | async-start | bytes 2097152 | tf_op jit(solution)/shard_map/all_to_all | solution.py:155
  36.2 172.0 %all-gather.5.cloned.1.call-start = ((), (), s32[]{:S(2)}) async-start(), calls=%async_computation.8 | async-start | bytes 4456448 | tf_op jit(solution)/shard_map/all_gather | solution.py:167
  116.5 2.3 copy-start
  167.5 43.2 %copy-start.2 = (bf16[2048,128]{1,0:T(8,128)(2,1)S(1)}, bf16[2048,128]{1,0:T(8,128)(2,1)}, u32[]{:S(2)}) copy-start(bf16[2048,128]{1,0:T(8,128)(2,1)} %param.8) | copy-start | bytes 1572868
  208.2 2.8 %copy-start.10 = (bf16[2048,1024]{1,0:T(8,128)(2,1)S(1)}, bf16[2048,1024]{1,0:T(8,128)(2,1)}, u32[]{:S(2)}) copy-start(bf16[2048,1024]{1,0:T(8,128)(2,1)} %all-gather.5.cloned.1.call-done) | copy-start | bytes 12582916
  211.8 27.8 %copy-start.5 = (bf16[128,512]{1,0:T(8,128)(2,1)S(1)}, bf16[128,512]{1,0:T(8,128)(2,1)}, u32[]{:S(2)}) copy-start(bf16[128,512]{1,0:T(8,128)(2,1)} %param.10) | copy-start | bytes 393220
  235.0 16.1 %all-to-all-start.4 = ((bf16[32,16,256]{2,1,0:T(8,128)(2,1)}), bf16[32,16,256]{2,1,0:T(8,128)(2,1)S(1)}, u32[]{:S(2)}, u32[]{:S(2)}) async-start(bf16[32,16,256]{2,1,0:T(8,128)(2,1)} %broadcast_in_dim.18), calls=%async_computation.5 | async-start | bytes 524288 | tf_op jit(solution)/shard_map/all_to_all | solution.py:179
Sparse Core Ops, SparseCore 0:
  16.4 57.3 reduce-scatter.1
  167.6 40.5 all-gather.4
Sparse Core Ops, SparseCore 1:
  20.5 93.4 all-gather.2

commit v3 on v2

--- a/solution.py
+++ b/solution.py
@@ -1,3 +1,4 @@
+import functools
 import math
 
 import jax
@@ -11,6 +12,8 @@
 TOPK = 4
 CORES = 2
 CHUNK = 256
+SMALL = pltpu.CompilerParams(vmem_limit_bytes=16 * 1024 * 1024)
+LARGE = pltpu.CompilerParams(vmem_limit_bytes=56 * 1024 * 1024)
 INNER = (((1,), (0,)), ((), ()))
 COLS = (((1,), (1,)), ((), ()))
 ROWS = (((0,), (0,)), ((), ()))
@@ -96,13 +99,152 @@
         out_specs=pl.BlockSpec((count, 2 * latent_width), lambda j: (0, 0)),
         out_shape=jax.ShapeDtypeStruct((count, 2 * latent_width), jnp.bfloat16),
         scratch_shapes=[pltpu.VMEM((count, latent_width), jnp.float32)] * 2,
-        compiler_params=pltpu.CompilerParams(vmem_limit_bytes=32 * 1024 * 1024),
+        compiler_params=LARGE,
         cost_estimate=pl.CostEstimate(
             flops=12 * count * latent_width * padded,
             bytes_accessed=2 * (weights.size + 2 * rows.size),
             transcendentals=count * padded,
         ),
     )(rows, weights, weights, weights)
+
+
+def swap_kernel(core_ref, tokens_ref, cotangent_ref, down_ref, up_ref, rows_ref, weights_ref, sems):
+    other = 1 - core_ref[0]
+    features = tokens_ref.shape[3]
+    latent_width = down_ref.shape[1]
+    copies = [
+        pltpu.make_async_copy(
+            tokens_ref.at[:, other], rows_ref.at[:, :, pl.ds(0, features)], sems.at[0]
+        ),
+        pltpu.make_async_copy(
+            cotangent_ref.at[:, other], rows_ref.at[:, :, pl.ds(features, features)], sems.at[1]
+        ),
+    ]
+    for copy in copies:
+        copy.start()
+    weights_ref[:, :latent_width] = down_ref[...]
+    weights_ref[:, latent_width:] = up_ref[...].T
+    for copy in copies:
+        copy.wait()
+
+
+def swap_operands(core, tokens, cotangent, down_proj, up_proj):
+    chips, _, tok_rows, features = tokens.shape
+    latent_width = down_proj.shape[1]
+    return pl.pallas_call(
+        swap_kernel,
+        in_specs=[
+            pl.BlockSpec(memory_space=pltpu.SMEM),
+            pl.BlockSpec(memory_space=pl.ANY),
+            pl.BlockSpec(memory_space=pl.ANY),
+            pl.BlockSpec(memory_space=pltpu.VMEM),
+            pl.BlockSpec(memory_space=pltpu.VMEM),
+        ],
+        out_specs=[pl.BlockSpec(memory_space=pl.ANY), pl.BlockSpec(memory_space=pltpu.VMEM)],
+        out_shape=[
+            jax.ShapeDtypeStruct((chips, tok_rows, 2 * features), jnp.bfloat16),
+            jax.ShapeDtypeStruct((features, 2 * latent_width), jnp.bfloat16),
+        ],
+        scratch_shapes=[pltpu.SemaphoreType.DMA((2,))],
+        compiler_params=LARGE,
+    )(core, tokens, cotangent, down_proj, up_proj)
+
+
+def latent_kernel(
+    core_ref, tokens_ref, cotangent_ref, rows_ref, down_ref, up_ref, weights_ref, latent_ref, grad_ref
+):
+    features = tokens_ref.shape[3]
+    latent_width = down_ref.shape[1]
+    count = latent_ref.shape[0]
+    down = jnp.concatenate([down_ref[...], weights_ref[:, :latent_width]], axis=0)
+    up = jnp.concatenate([up_ref[...].T, weights_ref[:, latent_width:]], axis=0)
+    rows = rows_ref[...].reshape(count, 2 * features)
+    kept = tokens_ref[...].reshape(count, features)
+    left = jnp.concatenate([kept, rows[:, :features]], axis=1)
+    latent_ref[...] = dot(left, down).astype(jnp.bfloat16)
+    kept = cotangent_ref[...].reshape(count, features)
+    left = jnp.concatenate([kept, rows[:, features:]], axis=1)
+    grad_ref[...] = dot(left, up).astype(jnp.bfloat16)
+
+
+def chip_latents(core, tokens, cotangent, rows, down_proj, up_proj, weights):
+    chips, _, tok_rows, features = tokens.shape
+    latent_width = down_proj.shape[1]
+    count = chips * tok_rows
+    mine = pl.BlockSpec((chips, 1, tok_rows, features), lambda i, core: (0, core[0], 0, 0))
+    whole = lambda array: pl.BlockSpec(array.shape, lambda i, core: (0,) * array.ndim)
+    out = jax.ShapeDtypeStruct((count, latent_width), jnp.bfloat16)
+    return pl.pallas_call(
+        latent_kernel,
+        grid_spec=pltpu.PrefetchScalarGridSpec(
+            num_scalar_prefetch=1,
+            grid=(1,),
+            in_specs=[mine, mine, whole(rows), whole(down_proj), whole(up_proj), whole(weights)],
+            out_specs=[whole(out)] * 2,
+        ),
+        out_shape=[out] * 2,
+        compiler_params=SMALL,
+    )(core, tokens, cotangent, rows, down_proj, up_proj, weights)
+
+
+def grads_kernel(latents_ref, cotangent_ref, tokens_ref, result_ref, sum_up, sum_down):
+    step = pl.program_id(0)
+    features = tokens_ref.shape[1]
+    latent_width = sum_up.shape[1]
+
+    @pl.when(step == 0)
+    def _():
+        sum_up[...] = jnp.zeros_like(sum_up)
+        sum_down[...] = jnp.zeros_like(sum_down)
+
+    sum_up[...] += dot(cotangent_ref[...], latents_ref[:, :latent_width], ROWS)
+    sum_down[...] += dot(tokens_ref[...], latents_ref[:, latent_width:], ROWS)
+
+    @pl.when(step == pl.num_programs(0) - 1)
+    def _():
+        result_ref[:, :features] = sum_up[...].T.astype(jnp.bfloat16)
+        for block in range(latent_width // features):
+            here = slice(block * features, (block + 1) * features)
+            result_ref[here, features:] = sum_down[:, here].astype(jnp.bfloat16)
+
+
+def projection_grads(latents, cotangent, tokens):
+    count, features = tokens.shape
+    latent_width = latents.shape[1] // 2
+    rows = count // 4
+    return pl.pallas_call(
+        grads_kernel,
+        grid=(4,),
+        in_specs=[
+            pl.BlockSpec((rows, 2 * latent_width), lambda i: (i, 0)),
+            pl.BlockSpec((rows, features), lambda i: (i, 0)),
+            pl.BlockSpec((rows, features), lambda i: (i, 0)),
+        ],
+        out_specs=pl.BlockSpec((latent_width, 2 * features), lambda i: (0, 0)),
+        out_shape=jax.ShapeDtypeStruct((latent_width, 2 * features), jnp.bfloat16),
+        scratch_shapes=[pltpu.VMEM((features, latent_width), jnp.float32)] * 2,
+        compiler_params=LARGE,
+    )(latents, cotangent, tokens)
+
+
+def unpack_kernel(scale, packed_ref, down_ref, up_ref):
+    latent_width, features = up_ref.shape
+    up_ref[...] = packed_ref[:, :features].astype(jnp.float32) * scale
+    for block in range(latent_width // features):
+        here = slice(block * features, (block + 1) * features)
+        down_ref[:, here] = packed_ref[here, features:].astype(jnp.float32) * scale
+
+
+def unpack_grads(packed, scale):
+    latent_width, features = packed.shape[0], packed.shape[1] // 2
+    return pl.pallas_call(
+        functools.partial(unpack_kernel, scale),
+        out_shape=[
+            jax.ShapeDtypeStruct((features, latent_width), jnp.float32),
+            jax.ShapeDtypeStruct((latent_width, features), jnp.float32),
+        ],
+        compiler_params=SMALL,
+    )(packed)
 
 
 def on_device(tokens, cotangent, down_proj, up_proj, routes, gate_weights, expert_in, expert_out):
@@ -122,17 +264,15 @@
 
     swap = [(0, 1), (1, 0)]
 
-    def partial_latent(rows, weights_here, column_dims):
-        blocks = rows.reshape(chips, CORES, tok_rows, features)
-        kept = lax.dynamic_index_in_dim(blocks, core, 1, keepdims=False)
-        given = lax.dynamic_index_in_dim(blocks, 1 - core, 1, keepdims=False)
-        got = lax.ppermute(given, "c", swap)
-        weights_there = lax.ppermute(weights_here, "c", swap)
-        kept = kept.reshape(chips * tok_rows, features)
-        got = got.reshape(chips * tok_rows, features)
-        part = dot(kept, weights_here, column_dims) + dot(got, weights_there, column_dims)
-        return part.astype(bf16).reshape(chips, tok_rows, latent_width)
-
+    blocked = (chips, CORES, tok_rows, features)
+    token_blocks = tokens.reshape(blocked)
+    cotangent_blocks = cotangent.reshape(blocked)
+    place = core.reshape(1).astype(jnp.int32)
+    given = swap_operands(place, token_blocks, cotangent_blocks, down_proj, up_proj)
+    got_rows, got_weights = (lax.ppermute(array, "c", swap) for array in given)
+    latent, parts = chip_latents(
+        place, token_blocks, cotangent_blocks, got_rows, down_proj, up_proj, got_weights
+    )
     weights = lax.all_gather(packed_weights(expert_in, expert_out, dp), "dp", axis=0, tiled=True)
 
     spread, weighted = slot_tables(routes, gate_weights, groups, capacity)
@@ -149,9 +289,8 @@
             tiled=True,
         ).reshape(slot_count, rows.shape[1])
 
-    latent = partial_latent(tokens, down_proj, INNER).reshape(chips * tok_rows, latent_width)
     latent = lax.psum_scatter(latent, "z", scatter_dimension=0, tiled=True)
-    parts = partial_latent(cotangent, up_proj, COLS)
+    parts = parts.reshape(chips, tok_rows, latent_width)
     parts = lax.all_to_all(parts, "z", split_axis=0, concat_axis=0, tiled=True)
     latent_out_grad = jnp.sum(parts.astype(jnp.float32), axis=0).astype(bf16)
     outgoing = [dot(spread, latent), dot(spread, latent_out_grad) * slot_gate]
@@ -167,9 +306,7 @@
     latents = lax.all_gather(latents, expert, axis=0, tiled=True)
     all_out = latents[:, :latent_width]
     all_grad = latents[:, latent_width:]
-    up_part_grad = dot(all_out, cotangent, ROWS)
-    down_part_grad = dot(all_grad, tokens, ROWS)
-    grads = jnp.concatenate([up_part_grad, down_part_grad], axis=1).astype(bf16)
+    grads = projection_grads(latents, cotangent, tokens)
     grads = grads.reshape(dp, latent_width // dp, 2 * features)
     grads = lax.all_to_all(grads, "dp", split_axis=0, concat_axis=0, tiled=True)
     mixed = dot(all_out, up_proj).astype(bf16)
@@ -177,8 +314,8 @@
     summed = jnp.sum(grads.astype(jnp.float32), axis=0).astype(bf16)
     summed = jnp.broadcast_to(summed[None], grads.shape)
     summed = lax.all_to_all(summed, "dp", split_axis=0, concat_axis=0, tiled=True)
-    summed = summed.reshape(latent_width, 2 * features).astype(jnp.float32) * grad_scale
-    return mixed, input_grad, summed[:, features:].T, summed[:, :features]
+    down_grad, up_grad = unpack_grads(summed.reshape(latent_width, 2 * features), grad_scale)
+    return mixed, input_grad, down_grad, up_grad
 
 
 def solution(mesh):

time: 261 us -> 278 us (1.065)
  Pallas kernels: 8.51 us -> 37.1 us
  matrix products: 18.2 us -> 10.3 us
  waiting for transfers between devices: 81.3 us -> 86.9 us
  local copies, waits for them, and re-layouts: 7.59 us -> 2.25 us
  starting transfers between devices: 23.8 us -> 19.4 us
    pallas_call x0 -> x4, Pallas kernels: none -> 26.1 us  [the longest x1 18.8 us: swap_operands(): pl.pallas_call(swap_kernel, in_specs=[pl.BlockSpec(memory_space=pltpu.SME...]
    dot_general x14 -> x8, matrix products: 18.2 us -> 10.3 us  [dot(): lax.dot_general(left, right, dims, preferred_element_type=jnp.float32)]
    ppermute x4 -> x2, starting transfers between devices: 8.66 us -> 4.33 us  [on_device(): got_rows, got_weights = (lax.ppermute(array, 'c', swap) for array in given)]
    reduce_scatter x1, waiting for transfers between devices: 2.68 us -> 6.33 us  [on_device(): latent = lax.psum_scatter(latent, 'z', scatter_dimension=0, tiled=True)]
    unnamed x28 -> x23, local copies, waits for them, and re-layouts: 4.31 us -> 0.83 us
  transfers between devices with their start and end apart: 9 -> 7, of which waited for: 5 -> 6; matrix products, arithmetic and copies ran while one was open for 6% -> 4% of each run, Pallas kernels for 0% -> 0%
where the time goes in v3:
time: 278 us; the launch traced here: 277 us
  blocking collectives  103 us (37%)
  waiting for transfers between devices  86.9 us (31%)
  Pallas kernels  37.1 us (13%)
  starting transfers between devices  19.4 us (7%)
  between operations  15.8 us (6%)
  matrix products  10.3 us (4%)
  other arithmetic  2.8 us (1%)
    all_to_all x2, blocking collectives, exchange(): lax.all_to_all(rows.reshape(groups, capacity, rows.shape[1]), expert, spl...  80.5 us
    all_gather x1, waiting for transfers between devices, on_device(): latents = lax.all_gather(latents, expert, axis=0, tiled=True)  39.2 us
    all_to_all x1, waiting for transfers between devices, on_device(): parts = lax.all_to_all(parts, 'z', split_axis=0, concat_axis=0, tiled=True)  33.1 us
    all_to_all x1, blocking collectives, on_device(): grads = lax.all_to_all(grads, 'dp', split_axis=0, concat_axis=0, tiled=True)  22.4 us
    pallas_call x1, Pallas kernels, swap_operands(): pl.pallas_call(swap_kernel, in_specs=[pl.BlockSpec(memory_space=pltpu.SME...  18.8 us
    pallas_call x1, Pallas kernels, run_expert(): pl.pallas_call(expert_kernel, grid=(steps,), in_specs=[pl.BlockSpec((coun...  11 us
    all_to_all x1, starting transfers between devices, on_device(): parts = lax.all_to_all(parts, 'z', split_axis=0, concat_axis=0, tiled=True)  10.4 us
    dot_general x8, matrix products, dot(): lax.dot_general(left, right, dims, preferred_element_type=jnp.float32)  10.3 us
  transfers between devices with their start and end apart: 7, of which 6 were waited for; matrix products, arithmetic and copies ran while one was open for 4% of the time, Pallas kernels for 0%

profile of v3, /device:TPU:8, one launch (start us, length us, event | category | flops | bytes accessed | tf_op | source)
XLA Modules:
  0.0 277.4 jit_solution(18169159976327488951)
XLA Ops:
  8.0 0.0 copy-start
  8.0 0.0 copy-start.1
  8.0 0.0 copy-start.2
  8.0 0.0 copy-start.3
  8.0 0.0 reduce-scatter.2.cloned.1.call-start
  8.1 18.8 %shard_map.111 = (bf16[8,128,256]{2,1,0:T(8,128)(2,1)}, bf16[128,1024]{1,0:T(8,128)(2,1)}) custom-call(s32[1]{0:T(128)} %bitcast.4.core_ref, bf16[8,2,128,128]{3,2,1,0:T(8,128)(2,1)} %bitcast.51, bf16[8,2,128,128]{3,2,1,0:T(8,128)(2,1)} %bitcast.53, bf16[128,512]{1,0:T(8,128)(2,1)} %down_ref.3, bf16[512,128]{1,0:T(8,128)(2,1)} %up_ref.3), custom_call_target="tpu_custom_call" | custom-call | tf_op jit(solution)/shard_map/pallas_call | solution.py:134
  26.9 1.9 collective-permute-start
  28.8 2.4 collective-permute-start.1
  31.2 0.0 copy-start.6
  31.2 1.3 collective-permute-done.1.weights_ref
  32.5 0.0 collective-permute-done.rows_ref
  32.6 0.0 copy-done
  32.6 0.0 copy-done.1
  32.6 0.0 copy-done.3
  32.6 2.0 shard_map.112
  34.5 0.0 reduce-scatter.2.cloned.1.call-update
  34.6 0.0 all-gather.3.cloned.1.call-start
  34.6 0.1 slice_bitcast_fusion.1
  34.7 0.0 copy-start.5
  34.7 1.7 fusion.2
  36.4 0.0 copy-start.7
  36.5 0.0 copy-start.4
  36.5 0.7 copy-done.4
  37.1 0.0 all-gather.3.cloned.1.call-update
  37.2 0.0 copy-start.8
  37.2 10.4 %all-to-all-start = ((bf16[8,128,512]{2,1,0:T(8,128)(2,1)}), bf16[8,128,512]{2,1,0:T(8,128)(2,1)S(1)}, u32[]{:S(2)}, u32[]{:S(2)}) async-start(bf16[8,128,512]{2,1,0:T(8,128)(2,1)} %bitcast.8), calls=%async_computation.1 | async-start | bytes 2097152 | tf_op jit(solution)/shard_map/all_to_all | solution.py:294
  47.5 0.0 all-gather.5.cloned.1.call-start
  47.6 0.0 copy-done.7
  47.6 0.1 copy.24
  47.7 0.1 eq.58
  47.8 0.1 eq.54
  47.9 1.2 reduce-window.6
  49.1 0.2 slice_reduce_fusion
  49.3 0.1 fusion.20
  49.4 0.1 reduce_sum.54
  49.6 0.1 copy.27
  49.6 0.2 fusion.6
  49.8 0.0 copy-done.8
  49.8 0.2 select_reduce_fusion.1
  50.0 33.1 %all-to-all-done = bf16[8,128,512]{2,1,0:T(8,128)(2,1)S(1)} async-done(((bf16[8,128,512]{2,1,0:T(8,128)(2,1)}), bf16[8,128,512]{2,1,0:T(8,128)(2,1)S(1)}, u32[]{:S(2)}, u32[]{:S(2)}) %all-to-all-start) | async-done | bytes 1048608 | tf_op jit(solution)/shard_map/all_to_all | solution.py:294
  83.1 0.1 reduce_sum.56
  83.3 0.3 fusion.5
  83.6 6.3 %reduce-scatter.2.cloned.1.call-done = bf16[128,512]{1,0:T(8,128)(2,1)} async-done(((bf16[1024,512]{1,0:T(8,128)(2,1)}), bf16[128,512]{1,0:T(8,128)(2,1)}) %reduce-scatter.2.cloned.1.call-update) | async-done | bytes 131088 | tf_op jit(solution)/shard_map/reduce_scatter | solution.py:292
  89.9 1.2 convolution_convert_fusion.2
  91.2 0.2 pad_maximum_fusion
  91.3 39.3 %all_to_all.25 = bf16[16,40,1024]{2,1,0:T(8,128)(2,1)} all-to-all(bf16[16,40,1024]{2,1,0:T(8,128)(2,1)S(1)} %pad_maximum_fusion), channel_id=1, replica_groups=mesh['dp'=32,'z'=8,'c'=2] {'z','c'}, dimensions={0} | all-to-all | bytes 2621440 | tf_op jit(solution)/shard_map/all_to_all | solution.py:284
  130.7 1.5 all-gather.3.cloned.1.call-done.gate_ref.up_ref.out_ref
  132.2 11.0 %shard_map.113 = bf16[640,1024]{1,0:T(8,128)(2,1)} custom-call(bf16[640,1024]{1,0:T(8,128)(2,1)} %bitcast.60, bf16[512,4608]{1,0:T(8,128)(2,1)} %all-gather.3.cloned.1.call-done.gate_ref.up_ref.out_ref, bf16[512,4608]{1,0:T(8,128)(2,1)} %all-gather.3.cloned.1.call-done.gate_ref.up_ref.out_ref, ...), custom_call_target="tpu_custom_call" | custom-call | flops 6039797760 | bytes 7340032 | tf_op jit(solution)/shard_map/pallas_call | solution.py:90
  143.2 41.1 %all_to_all.26 = bf16[16,40,1024]{2,1,0:T(8,128)(2,1)S(1)} all-to-all(bf16[16,40,1024]{2,1,0:T(8,128)(2,1)} %bitcast.61), channel_id=1, replica_groups=mesh['dp'=32,'z'=8,'c'=2] {'z','c'}, dimensions={0} | all-to-all | bytes 2621440 | tf_op jit(solution)/shard_map/all_to_all | solution.py:284
  184.3 0.3 convolution_convert_fusion.3
  184.6 0.3 fusion.10
  184.9 0.3 fusion.7
  185.2 0.7 pad_maximum_fusion.1
  186.0 0.0 all-gather.5.cloned.1.call-update
  186.0 39.2 %all-gather.5.cloned.1.call-done.latents_ref = bf16[2048,1024]{1,0:T(8,128)(2,1)} async-done(((bf16[128,1024]{1,0:T(8,128)(2,1)}), bf16[2048,1024]{1,0:T(8,128)(2,1)}) %all-gather.5.cloned.1.call-update) | async-done | bytes 4194320 | tf_op jit(solution)/shard_map/all_gather | solution.py:306
  225.2 4.6 %shard_map.114 = bf16[512,256]{1,0:T(8,128)(2,1)} custom-call(bf16[2048,1024]{1,0:T(8,128)(2,1)} %all-gather.5.cloned.1.call-done.latents_ref, bf16[2048,128]{1,0:T(8,128)(2,1)} %cotangent_ref.1, bf16[2048,128]{1,0:T(8,128)(2,1)} %tokens_ref.1), custom_call_target="tpu_custom_call" | custom-call | tf_op jit(solution)/shard_map/pallas_call | solution.py:215
  229.8 22.4 %all_to_all.27 = bf16[32,16,256]{2,1,0:T(8,128)(2,1)S(1)} all-to-all(bf16[32,16,256]{2,1,0:T(8,128)(2,1)} %bitcast.62), channel_id=1, replica_groups=mesh['dp'=32,'z'=8,'c'=2] {'dp'}, dimensions={0} | all-to-all | bytes 524288 | tf_op jit(solution)/shard_map/all_to_all | solution.py:311
  252.2 0.1 reduce_sum.58
  252.3 0.7 broadcast_in_dim.18
  253.0 4.6 %all-to-all-start.4 = ((bf16[32,16,256]{2,1,0:T(8,128)(2,1)}), bf16[32,16,256]{2,1,0:T(8,128)(2,1)S(1)}, u32[]{:S(2)}, u32[]{:S(2)}) async-start(bf16[32,16,256]{2,1,0:T(8,128)(2,1)} %broadcast_in_dim.18), calls=%async_computation.5 | async-start | bytes 524288 | tf_op jit(solution)/shard_map/all_to_all | solution.py:316
  257.6 3.1 %convolution_convert_fusion = bf16[2048,128]{1,0:T(8,128)(2,1)} fusion(bf16[128,512]{1,0:T(8,128)(2,1)S(1)} %copy-done.2, bf16[2048,1024]{1,0:T(8,128)(2,1)} %all-gather.5.cloned.1.call-done.latents_ref), kind=kOutput, calls=%fused_computation.3 | convolution fusion | flops 268697600 | bytes 2752512 | tf_op jit(solution)/shard_map/dot_general | solution.py:23
  260.7 3.1 %convolution_convert_fusion.1 = bf16[2048,128]{1,0:T(8,128)(2,1)} fusion(bf16[512,128]{1,0:T(8,128)(2,1)S(1)} %copy-done.3, bf16[2048,1024]{1,0:T(8,128)(2,1)} %all-gather.5.cloned.1.call-done.latents_ref), kind=kOutput, calls=%fused_computation.4 | convolution fusion | flops 268697600 | bytes 2752512 | tf_op jit(solution)/shard_map/dot_general | solution.py:23
  263.8 5.3 %all-to-all-done.4 = bf16[32,16,256]{2,1,0:T(8,128)(2,1)S(1)} async-done(((bf16[32,16,256]{2,1,0:T(8,128)(2,1)}), bf16[32,16,256]{2,1,0:T(8,128)(2,1)S(1)}, u32[]{:S(2)}, u32[]{:S(2)}) %all-to-all-start.4) | async-done | bytes 262176 | tf_op jit(solution)/shard_map/all_to_all | solution.py:316
  269.1 0.8 shard_map.115
  (13 shorter events, 0.1 us)
Async XLA Ops:
  8.0 24.6 %copy-start = (bf16[2048,128]{1,0:T(8,128)(2,1)S(1)}, bf16[2048,128]{1,0:T(8,128)(2,1)}, u32[]{:S(2)}) copy-start(bf16[2048,128]{1,0:T(8,128)(2,1)} %tokens_ref.1) | copy-start | bytes 1572868
  8.0 24.5 %copy-start.1 = (bf16[2048,128]{1,0:T(8,128)(2,1)S(1)}, bf16[2048,128]{1,0:T(8,128)(2,1)}, u32[]{:S(2)}) copy-start(bf16[2048,128]{1,0:T(8,128)(2,1)} %cotangent_ref.1) | copy-start | bytes 1572868
  8.0 24.5 %copy-start.2 = (bf16[128,512]{1,0:T(8,128)(2,1)S(1)}, bf16[128,512]{1,0:T(8,128)(2,1)}, u32[]{:S(2)}) copy-start(bf16[128,512]{1,0:T(8,128)(2,1)} %down_ref.3) | copy-start | bytes 393220
  8.0 24.5 %copy-start.3 = (bf16[512,128]{1,0:T(8,128)(2,1)S(1)}, bf16[512,128]{1,0:T(8,128)(2,1)}, u32[]{:S(2)}) copy-start(bf16[512,128]{1,0:T(8,128)(2,1)} %up_ref.3) | copy-start | bytes 393220
  8.0 81.9 %reduce-scatter.2.cloned.1.call-start = ((), (), s32[]{:S(2)}) async-start(), calls=%async_computation.6 | async-start | bytes 1179648 | tf_op jit(solution)/shard_map/reduce_scatter | solution.py:292
  26.9 5.7 %collective-permute-start = (bf16[8,128,256]{2,1,0:T(8,128)(2,1)}, bf16[8,128,256]{2,1,0:T(8,128)(2,1)S(1)}, u32[]{:S(2)}, u32[]{:S(2)}) collective-permute-start(bf16[8,128,256]{2,1,0:T(8,128)(2,1)} %get-tuple-element.10), channel_id=1, source_target_pairs={{0,1},{1,0},{2,3},{3,2},{4,5},{5,4},{6,7},{7,6},{8,9},{9,8},{10,11... | collective-permute-start | bytes 1572872 | tf_op jit(solution)/shard_map/ppermute | solution.py:272
  28.8 3.8 %collective-permute-start.1 = (bf16[128,1024]{1,0:T(8,128)(2,1)}, bf16[128,1024]{1,0:T(8,128)(2,1)S(1)}, u32[]{:S(2)}, u32[]{:S(2)}) collective-permute-start(bf16[128,1024]{1,0:T(8,128)(2,1)} %get-tuple-element.11), channel_id=1, source_target_pairs={{0,1},{1,0},{2,3},{3,2},{4,5},{5,4},{6,7},{7,6},{8,9},{9,8},{10,11... | collective-permute-start | bytes 786440 | tf_op jit(solution)/shard_map/ppermute | solution.py:272
  31.2 3.4 %copy-start.6 = (bf16[1,16,2688]{2,1,0:T(8,128)(2,1)S(1)}, bf16[1,16,2688]{2,1,0:T(8,128)(2,1)}, u32[]{:S(2)}) copy-start(bf16[1,16,2688]{2,1,0:T(8,128)(2,1)} %param.14) | copy-start | bytes 258052
  34.6 97.6 %all-gather.3.cloned.1.call-start = ((), (), s32[]{:S(2)}) async-start(), calls=%async_computation.7 | async-start | bytes 4866048 | tf_op jit(solution)/shard_map/all_gather | solution.py:276
  34.7 1.7 copy-start.5
  36.4 11.2 %copy-start.7 = (s32[128,4]{0,1:T(4,128)S(1)}, s32[128,4]{0,1:T(4,128)}, u32[]{:S(2)}) copy-start(s32[128,4]{0,1:T(4,128)} %param.12) | copy-start | bytes 6148
  36.5 0.7 copy-start.4
  37.2 12.7 %copy-start.8 = (f32[128,4]{0,1:T(4,128)S(1)}, f32[128,4]{0,1:T(4,128)}, u32[]{:S(2)}) copy-start(f32[128,4]{0,1:T(4,128)} %param.13) | copy-start | bytes 6148
  37.2 46.0 %all-to-all-start = ((bf16[8,128,512]{2,1,0:T(8,128)(2,1)}), bf16[8,128,512]{2,1,0:T(8,128)(2,1)S(1)}, u32[]{:S(2)}, u32[]{:S(2)}) async-start(bf16[8,128,512]{2,1,0:T(8,128)(2,1)} %bitcast.8), calls=%async_computation.1 | async-start | bytes 2097152 | tf_op jit(solution)/shard_map/all_to_all | solution.py:294
  47.5 177.7 %all-gather.5.cloned.1.call-start = ((), (), s32[]{:S(2)}) async-start(), calls=%async_computation.8 | async-start | bytes 4456448 | tf_op jit(solution)/shard_map/all_gather | solution.py:306
  253.0 16.1 %all-to-all-start.4 = ((bf16[32,16,256]{2,1,0:T(8,128)(2,1)}), bf16[32,16,256]{2,1,0:T(8,128)(2,1)S(1)}, u32[]{:S(2)}, u32[]{:S(2)}) async-start(bf16[32,16,256]{2,1,0:T(8,128)(2,1)} %broadcast_in_dim.18), calls=%async_computation.5 | async-start | bytes 524288 | tf_op jit(solution)/shard_map/all_to_all | solution.py:316
Sparse Core Ops, SparseCore 0:
  34.7 55.2 reduce-scatter.1
  186.1 39.0 all-gather.4
Sparse Core Ops, SparseCore 1:
  38.8 93.4 all-gather.2

commit v4 on v3

--- a/solution.py
+++ b/solution.py
@@ -12,6 +12,7 @@
 TOPK = 4
 CORES = 2
 CHUNK = 256
+FIRST = 256
 SMALL = pltpu.CompilerParams(vmem_limit_bytes=16 * 1024 * 1024)
 LARGE = pltpu.CompilerParams(vmem_limit_bytes=56 * 1024 * 1024)
 INNER = (((1,), (0,)), ((), ()))
@@ -99,7 +100,7 @@
         out_specs=pl.BlockSpec((count, 2 * latent_width), lambda j: (0, 0)),
         out_shape=jax.ShapeDtypeStruct((count, 2 * latent_width), jnp.bfloat16),
         scratch_shapes=[pltpu.VMEM((count, latent_width), jnp.float32)] * 2,
-        compiler_params=LARGE,
+        compiler_params=pltpu.CompilerParams(vmem_limit_bytes=32 * 1024 * 1024),
         cost_estimate=pl.CostEstimate(
             flops=12 * count * latent_width * padded,
             bytes_accessed=2 * (weights.size + 2 * rows.size),
@@ -140,7 +141,7 @@
             pl.BlockSpec(memory_space=pltpu.VMEM),
             pl.BlockSpec(memory_space=pltpu.VMEM),
         ],
-        out_specs=[pl.BlockSpec(memory_space=pl.ANY), pl.BlockSpec(memory_space=pltpu.VMEM)],
+        out_specs=[pl.BlockSpec(memory_space=pltpu.VMEM)] * 2,
         out_shape=[
             jax.ShapeDtypeStruct((chips, tok_rows, 2 * features), jnp.bfloat16),
             jax.ShapeDtypeStruct((features, 2 * latent_width), jnp.bfloat16),
@@ -151,20 +152,24 @@
 
 
 def latent_kernel(
-    core_ref, tokens_ref, cotangent_ref, rows_ref, down_ref, up_ref, weights_ref, latent_ref, grad_ref
+    core_ref, tokens_ref, cotangent_ref, rows_ref, down_ref, up_ref, weights_ref, first_ref, rest_ref
 ):
     features = tokens_ref.shape[3]
     latent_width = down_ref.shape[1]
-    count = latent_ref.shape[0]
+    count, width = first_ref.shape
+    blocks = rest_ref.shape[:2]
     down = jnp.concatenate([down_ref[...], weights_ref[:, :latent_width]], axis=0)
     up = jnp.concatenate([up_ref[...].T, weights_ref[:, latent_width:]], axis=0)
     rows = rows_ref[...].reshape(count, 2 * features)
     kept = tokens_ref[...].reshape(count, features)
     left = jnp.concatenate([kept, rows[:, :features]], axis=1)
-    latent_ref[...] = dot(left, down).astype(jnp.bfloat16)
+    first_ref[...] = dot(left, down[:, :width]).astype(jnp.bfloat16)
+    part = dot(left, down[:, width:]).astype(jnp.bfloat16)
+    rest_ref[:, :, : latent_width - width] = part.reshape(*blocks, latent_width - width)
     kept = cotangent_ref[...].reshape(count, features)
     left = jnp.concatenate([kept, rows[:, features:]], axis=1)
-    grad_ref[...] = dot(left, up).astype(jnp.bfloat16)
+    part = dot(left, up).astype(jnp.bfloat16)
+    rest_ref[:, :, latent_width - width :] = part.reshape(*blocks, latent_width)
 
 
 def chip_latents(core, tokens, cotangent, rows, down_proj, up_proj, weights):
@@ -173,66 +178,51 @@
     count = chips * tok_rows
     mine = pl.BlockSpec((chips, 1, tok_rows, features), lambda i, core: (0, core[0], 0, 0))
     whole = lambda array: pl.BlockSpec(array.shape, lambda i, core: (0,) * array.ndim)
-    out = jax.ShapeDtypeStruct((count, latent_width), jnp.bfloat16)
+    out = [
+        jax.ShapeDtypeStruct((count, FIRST), jnp.bfloat16),
+        jax.ShapeDtypeStruct((chips, tok_rows, 2 * latent_width - FIRST), jnp.bfloat16),
+    ]
     return pl.pallas_call(
         latent_kernel,
         grid_spec=pltpu.PrefetchScalarGridSpec(
             num_scalar_prefetch=1,
             grid=(1,),
             in_specs=[mine, mine, whole(rows), whole(down_proj), whole(up_proj), whole(weights)],
-            out_specs=[whole(out)] * 2,
+            out_specs=[whole(array) for array in out],
         ),
-        out_shape=[out] * 2,
+        out_shape=out,
         compiler_params=SMALL,
     )(core, tokens, cotangent, rows, down_proj, up_proj, weights)
 
 
-def grads_kernel(latents_ref, cotangent_ref, tokens_ref, result_ref, sum_up, sum_down):
-    step = pl.program_id(0)
-    features = tokens_ref.shape[1]
-    latent_width = sum_up.shape[1]
-
-    @pl.when(step == 0)
-    def _():
-        sum_up[...] = jnp.zeros_like(sum_up)
-        sum_down[...] = jnp.zeros_like(sum_down)
-
-    sum_up[...] += dot(cotangent_ref[...], latents_ref[:, :latent_width], ROWS)
-    sum_down[...] += dot(tokens_ref[...], latents_ref[:, latent_width:], ROWS)
-
-    @pl.when(step == pl.num_programs(0) - 1)
-    def _():
-        result_ref[:, :features] = sum_up[...].T.astype(jnp.bfloat16)
-        for block in range(latent_width // features):
-            here = slice(block * features, (block + 1) * features)
-            result_ref[here, features:] = sum_down[:, here].astype(jnp.bfloat16)
-
-
-def projection_grads(latents, cotangent, tokens):
-    count, features = tokens.shape
-    latent_width = latents.shape[1] // 2
-    rows = count // 4
-    return pl.pallas_call(
-        grads_kernel,
-        grid=(4,),
-        in_specs=[
-            pl.BlockSpec((rows, 2 * latent_width), lambda i: (i, 0)),
-            pl.BlockSpec((rows, features), lambda i: (i, 0)),
-            pl.BlockSpec((rows, features), lambda i: (i, 0)),
-        ],
-        out_specs=pl.BlockSpec((latent_width, 2 * features), lambda i: (0, 0)),
-        out_shape=jax.ShapeDtypeStruct((latent_width, 2 * features), jnp.bfloat16),
-        scratch_shapes=[pltpu.VMEM((features, latent_width), jnp.float32)] * 2,
-        compiler_params=LARGE,
-    )(latents, cotangent, tokens)
+def dispatch_kernel(first_ref, parts_ref, spread_ref, gate_ref, result_ref):
+    width = first_ref.shape[1]
+    latent_width = result_ref.shape[1] // 2
+    rest = parts_ref[0].astype(jnp.float32)
+    for chip in range(1, parts_ref.shape[0]):
+        rest += parts_ref[chip].astype(jnp.float32)
+    rest = rest.astype(jnp.bfloat16)
+    spread = spread_ref[...]
+    result_ref[:, :width] = dot(spread, first_ref[...]).astype(jnp.bfloat16)
+    placed = dot(spread, rest[:, : latent_width - width])
+    result_ref[:, width:latent_width] = placed.astype(jnp.bfloat16)
+    placed = dot(spread, rest[:, latent_width - width :]) * gate_ref[...]
+    result_ref[:, latent_width:] = placed.astype(jnp.bfloat16)
+
+
+def dispatched_rows(first, parts, spread, slot_gate):
+    columns = first.shape[1] + parts.shape[2]
+    return pl.pallas_call(
+        dispatch_kernel,
+        out_shape=jax.ShapeDtypeStruct((spread.shape[0], columns), jnp.bfloat16),
+        compiler_params=SMALL,
+    )(first, parts, spread, slot_gate)
 
 
 def unpack_kernel(scale, packed_ref, down_ref, up_ref):
-    latent_width, features = up_ref.shape
+    features = up_ref.shape[1]
     up_ref[...] = packed_ref[:, :features].astype(jnp.float32) * scale
-    for block in range(latent_width // features):
-        here = slice(block * features, (block + 1) * features)
-        down_ref[:, here] = packed_ref[here, features:].astype(jnp.float32) * scale
+    down_ref[...] = packed_ref[:, features:].astype(jnp.float32).T * scale
 
 
 def unpack_grads(packed, scale):
@@ -270,10 +260,15 @@
     place = core.reshape(1).astype(jnp.int32)
     given = swap_operands(place, token_blocks, cotangent_blocks, down_proj, up_proj)
     got_rows, got_weights = (lax.ppermute(array, "c", swap) for array in given)
-    latent, parts = chip_latents(
+    packed, got_rows = lax.optimization_barrier(
+        (packed_weights(expert_in, expert_out, dp), got_rows)
+    )
+    weights = lax.all_gather(packed, "dp", axis=0, tiled=True)
+    first, parts = chip_latents(
         place, token_blocks, cotangent_blocks, got_rows, down_proj, up_proj, got_weights
     )
-    weights = lax.all_gather(packed_weights(expert_in, expert_out, dp), "dp", axis=0, tiled=True)
+    first = lax.psum_scatter(first, "z", scatter_dimension=0, tiled=True)
+    parts = lax.all_to_all(parts, "z", split_axis=0, concat_axis=0, tiled=True)
 
     spread, weighted = slot_tables(routes, gate_weights, groups, capacity)
     slot_gate = jnp.sum(weighted, axis=1, keepdims=True)
@@ -289,12 +284,8 @@
             tiled=True,
         ).reshape(slot_count, rows.shape[1])
 
-    latent = lax.psum_scatter(latent, "z", scatter_dimension=0, tiled=True)
-    parts = parts.reshape(chips, tok_rows, latent_width)
-    parts = lax.all_to_all(parts, "z", split_axis=0, concat_axis=0, tiled=True)
-    latent_out_grad = jnp.sum(parts.astype(jnp.float32), axis=0).astype(bf16)
-    outgoing = [dot(spread, latent), dot(spread, latent_out_grad) * slot_gate]
-    result = run_expert(exchange(jnp.concatenate(outgoing, axis=1).astype(bf16)), weights)
+    outgoing = dispatched_rows(first, parts, spread, slot_gate)
+    result = run_expert(exchange(outgoing), weights)
     returned = exchange(result)
     returned_out = returned[:, :latent_width]
     latent_out = (dot(gate_high, returned_out, ROWS) + dot(gate_low, returned_out, ROWS)).astype(
@@ -306,7 +297,9 @@
     latents = lax.all_gather(latents, expert, axis=0, tiled=True)
     all_out = latents[:, :latent_width]
     all_grad = latents[:, latent_width:]
-    grads = projection_grads(latents, cotangent, tokens)
+    up_part_grad = dot(all_out, cotangent, ROWS)
+    down_part_grad = dot(all_grad, tokens, ROWS)
+    grads = jnp.concatenate([up_part_grad, down_part_grad], axis=1).astype(bf16)
     grads = grads.reshape(dp, latent_width // dp, 2 * features)
     grads = lax.all_to_all(grads, "dp", split_axis=0, concat_axis=0, tiled=True)
     mixed = dot(all_out, up_proj).astype(bf16)

time: 278 us -> 263 us (0.946)
  Pallas kernels: 37.1 us -> 14.2 us
  local copies, waits for them, and re-layouts: 2.25 us -> 7.25 us
    reduce_scatter x1, waiting for transfers between devices: 6.33 us -> 40.7 us  [on_device(): first = lax.psum_scatter(first, 'z', scatter_dimension=0, tiled=True)]
    all_to_all x1, waiting for transfers between devices: 33.1 us -> 0.89 us  [on_device(): parts = lax.all_to_all(parts, 'z', split_axis=0, concat_axis=0, tiled=True)]
    pallas_call x1, Pallas kernels: 18.8 us -> 2.99 us  [swap_operands(): pl.pallas_call(swap_kernel, in_specs=[pl.BlockSpec(memory_space=pltpu.SME...]
    pallas_call x1, Pallas kernels: 4.57 us -> 0.54 us  [dispatched_rows(): pl.pallas_call(dispatch_kernel, out_shape=jax.ShapeDtypeStruct((spread.sh...]
    unnamed x23 -> x31, local copies, waits for them, and re-layouts: 0.83 us -> 4.83 us
  transfers between devices with their start and end apart: 7 -> 7, of which waited for: 6 -> 5; matrix products, arithmetic and copies ran while one was open for 4% -> 5% of each run, Pallas kernels for 0% -> 0%
where the time goes in v4:
time: 263 us
  blocking collectives  102 us (39%)
  waiting for transfers between devices  89.3 us (34%)
  starting transfers between devices  19.4 us (7%)
  between operations  15.8 us (6%)
  Pallas kernels  14.2 us (5%)
  matrix products  12 us (5%)
  local copies, waits for them, and re-layouts  7.25 us (3%)
  other arithmetic  3.2 us (1%)
    all_to_all x2, blocking collectives, exchange(): lax.all_to_all(rows.reshape(groups, capacity, rows.shape[1]), expert, spl...  79.4 us
    reduce_scatter x1, waiting for transfers between devices, on_device(): first = lax.psum_scatter(first, 'z', scatter_dimension=0, tiled=True)  40.7 us
    all_gather x1, waiting for transfers between devices, on_device(): latents = lax.all_gather(latents, expert, axis=0, tiled=True)  39.2 us
    all_to_all x1, blocking collectives, on_device(): grads = lax.all_to_all(grads, 'dp', split_axis=0, concat_axis=0, tiled=True)  22.2 us
    dot_general x8, matrix products, dot(): lax.dot_general(left, right, dims, preferred_element_type=jnp.float32)  12 us
    all_to_all x1, starting transfers between devices, on_device(): parts = lax.all_to_all(parts, 'z', split_axis=0, concat_axis=0, tiled=True)  10.3 us
    pallas_call x1, Pallas kernels, run_expert(): pl.pallas_call(expert_kernel, grid=(steps,), in_specs=[pl.BlockSpec((coun...  8.51 us
    all_to_all x1, waiting for transfers between devices, on_device(): lax.all_to_all(summed, 'dp', split_axis=0, concat_axis=0, tiled=True)  5.32 us
  transfers between devices with their start and end apart: 7, of which 5 were waited for; matrix products, arithmetic and copies ran while one was open for 5% of the time, Pallas kernels for 0%

profile of v4, /device:TPU:8, one launch (start us, length us, event | category | flops | bytes accessed | tf_op | source)
XLA Modules:
  0.0 262.7 jit_solution(15206870909570659271)
XLA Ops:
  8.0 0.0 reduce-scatter.2.cloned.1.call-start
  8.0 0.0 copy-start.9
  8.1 0.0 copy-start
  8.1 0.0 copy-start.1
  8.1 0.0 copy-start.3
  8.1 0.0 copy-start.4
  8.1 3.0 %shard_map.111 = (bf16[8,128,256]{2,1,0:T(8,128)(2,1)}, bf16[128,1024]{1,0:T(8,128)(2,1)}) custom-call(s32[1]{0:T(128)} %bitcast.3.core_ref, bf16[8,2,128,128]{3,2,1,0:T(8,128)(2,1)} %bitcast.49, bf16[8,2,128,128]{3,2,1,0:T(8,128)(2,1)} %bitcast.47, bf16[128,512]{1,0:T(8,128)(2,1)} %down_ref.3, bf16[512,128]{1,0:T(8,128)(2,1)} %up_ref.3), custom_call_target="tpu_custom_call" | custom-call | tf_op jit(solution)/shard_map/pallas_call | solution.py:135
  11.1 1.9 collective-permute-start
  13.0 2.4 collective-permute-start.1
  15.5 0.9 slice_bitcast_fusion.1
  16.4 1.7 fusion.2
  18.1 0.0 copy-done.9
  18.1 0.0 copy-start.8
  18.2 0.0 collective-permute-done.rows_ref
  18.2 0.0 collective-permute-done.1.weights_ref
  18.2 0.0 copy-done
  18.2 0.0 copy-done.1
  18.2 0.0 copy-done.3
  18.2 0.0 copy-done.4
  18.2 1.3 shard_map.112
  19.6 1.2 copy-done.2
  20.7 0.0 reduce-scatter.2.cloned.1.call-update
  20.7 0.0 all-gather.3.cloned.1.call-start
  20.8 0.5 all-gather.3.cloned.1.call-update
  21.3 10.3 %all-to-all-start = ((bf16[8,128,768]{2,1,0:T(8,128)(2,1)}), bf16[8,128,768]{2,1,0:T(8,128)(2,1)S(1)}, u32[]{:S(2)}, u32[]{:S(2)}) async-start(bf16[8,128,768]{2,1,0:T(8,128)(2,1)} %copy-done.2), calls=%async_computation.1 | async-start | bytes 3145728 | tf_op jit(solution)/shard_map/all_to_all | solution.py:271
  31.7 0.0 all-gather.5.cloned.1.call-start
  31.7 0.1 copy.26
  31.8 0.1 eq.58
  31.9 0.1 eq.54
  32.1 1.2 reduce-window.6
  33.2 0.2 slice_reduce_fusion
  33.5 0.1 fusion.28
  33.6 0.1 reduce_sum.42
  33.7 0.1 copy.29
  33.8 0.9 select_reduce_fusion.1
  34.6 0.1 broadcast_in_dim.33.gate_ref
  34.8 0.2 fusion.9
  35.0 40.7 %reduce-scatter.2.cloned.1.call-done.first_ref = bf16[128,256]{1,0:T(8,128)(2,1)} async-done(((bf16[1024,256]{1,0:T(8,128)(2,1)}), bf16[128,256]{1,0:T(8,128)(2,1)}) %reduce-scatter.2.cloned.1.call-update) | async-done | bytes 65552 | tf_op jit(solution)/shard_map/reduce_scatter | solution.py:270
  75.7 0.9 all-to-all-done.parts_ref
  76.6 0.8 copy-done.5
  77.4 0.5 shard_map.113
  78.0 38.3 %all_to_all.25 = bf16[16,40,1024]{2,1,0:T(8,128)(2,1)S(1)} all-to-all(bf16[16,40,1024]{2,1,0:T(8,128)(2,1)S(1)} %bitcast.46), channel_id=1, replica_groups=mesh['dp'=32,'z'=8,'c'=2] {'z','c'}, dimensions={0} | all-to-all | bytes 2621440 | tf_op jit(solution)/shard_map/all_to_all | solution.py:279
  116.3 2.6 all-gather.3.cloned.1.call-done.gate_ref.up_ref.out_ref
  118.9 2.3 copy-done.6
  121.2 8.5 %shard_map.114 = bf16[640,1024]{1,0:T(8,128)(2,1)S(1)} custom-call(bf16[640,1024]{1,0:T(8,128)(2,1)S(1)} %bitcast.51, bf16[512,4608]{1,0:T(8,128)(2,1)S(1)} %copy-done.6, bf16[512,4608]{1,0:T(8,128)(2,1)S(1)} %copy-done.6, bf16[512,4608]{1,0:T(8,128)(2,1)S(1)} %copy-done.6), custom_call_target="tpu_custom_call" | custom-call | flops 6039797760 | bytes 7340032 | tf_op jit(solution)/shard_map/pallas_call | solution.py:91
  129.7 0.0 copy-start.7
  129.7 41.1 %all_to_all.26 = bf16[16,40,1024]{2,1,0:T(8,128)(2,1)S(1)} all-to-all(bf16[16,40,1024]{2,1,0:T(8,128)(2,1)S(1)} %bitcast.52), channel_id=1, replica_groups=mesh['dp'=32,'z'=8,'c'=2] {'z','c'}, dimensions={0} | all-to-all | bytes 2621440 | tf_op jit(solution)/shard_map/all_to_all | solution.py:279
  170.8 0.3 convolution_convert_fusion.2
  171.1 0.3 fusion.19
  171.4 0.3 fusion.10
  171.7 0.7 pad_maximum_fusion
  172.5 0.0 all-gather.5.cloned.1.call-update
  172.5 39.2 %all-gather.5.cloned.1.call-done = bf16[2048,1024]{1,0:T(8,128)(2,1)} async-done(((bf16[128,1024]{1,0:T(8,128)(2,1)}), bf16[2048,1024]{1,0:T(8,128)(2,1)}) %all-gather.5.cloned.1.call-update) | async-done | bytes 4194320 | tf_op jit(solution)/shard_map/all_gather | solution.py:297
  211.7 2.5 fusion.11
  214.2 0.3 copy-done.12
  214.5 0.8 fusion.14
  215.3 22.2 %all_to_all.27 = bf16[32,16,256]{2,1,0:T(8,128)(2,1)S(1)} all-to-all(bf16[32,16,256]{2,1,0:T(8,128)(2,1)S(1)} %pad_maximum_fusion.1), channel_id=1, replica_groups=mesh['dp'=32,'z'=8,'c'=2] {'dp'}, dimensions={0} | all-to-all | bytes 524288 | tf_op jit(solution)/shard_map/all_to_all | solution.py:304
  237.6 0.1 reduce_sum.45
  237.6 0.7 broadcast_in_dim.32
  238.3 4.6 %all-to-all-start.4 = ((bf16[32,16,256]{2,1,0:T(8,128)(2,1)}), bf16[32,16,256]{2,1,0:T(8,128)(2,1)S(1)}, u32[]{:S(2)}, u32[]{:S(2)}) async-start(bf16[32,16,256]{2,1,0:T(8,128)(2,1)} %broadcast_in_dim.32), calls=%async_computation.5 | async-start | bytes 524288 | tf_op jit(solution)/shard_map/all_to_all | solution.py:309
  243.0 3.1 %convolution_convert_fusion = bf16[2048,128]{1,0:T(8,128)(2,1)} fusion(bf16[128,512]{1,0:T(8,128)(2,1)S(1)} %copy-done.3, bf16[2048,1024]{1,0:T(8,128)(2,1)} %all-gather.5.cloned.1.call-done), kind=kOutput, calls=%fused_computation.3 | convolution fusion | flops 268697600 | bytes 2752512 | tf_op jit(solution)/shard_map/dot_general | solution.py:24
  246.1 3.1 %convolution_convert_fusion.1 = bf16[2048,128]{1,0:T(8,128)(2,1)} fusion(bf16[512,128]{1,0:T(8,128)(2,1)S(1)} %copy-done.4, bf16[2048,1024]{1,0:T(8,128)(2,1)} %all-gather.5.cloned.1.call-done), kind=kOutput, calls=%fused_computation.4 | convolution fusion | flops 268697600 | bytes 2752512 | tf_op jit(solution)/shard_map/dot_general | solution.py:24
  249.2 5.3 %all-to-all-done.4 = bf16[32,16,256]{2,1,0:T(8,128)(2,1)S(1)} async-done(((bf16[32,16,256]{2,1,0:T(8,128)(2,1)}), bf16[32,16,256]{2,1,0:T(8,128)(2,1)S(1)}, u32[]{:S(2)}, u32[]{:S(2)}) %all-to-all-start.4) | async-done | bytes 262176 | tf_op jit(solution)/shard_map/all_to_all | solution.py:309
  254.5 0.8 shard_map.115
  (22 shorter events, 0.2 us)
Async XLA Ops:
  8.0 67.7 %reduce-scatter.2.cloned.1.call-start = ((), (), s32[]{:S(2)}) async-start(), calls=%async_computation.6 | async-start | bytes 589824 | tf_op jit(solution)/shard_map/reduce_scatter | solution.py:270
  8.0 10.1 %copy-start.9 = (bf16[1,42,512]{2,1,0:T(8,128)(2,1)S(1)}, bf16[1,42,512]{2,1,0:T(8,128)(2,1)}, u32[]{:S(2)}) copy-start(bf16[1,42,512]{2,1,0:T(8,128)(2,1)} %param.15) | copy-start | bytes 129028
  8.1 10.1 %copy-start = (bf16[2048,128]{1,0:T(8,128)(2,1)S(1)}, bf16[2048,128]{1,0:T(8,128)(2,1)}, u32[]{:S(2)}) copy-start(bf16[2048,128]{1,0:T(8,128)(2,1)} %param.9) | copy-start | bytes 1572868
  8.1 10.1 %copy-start.1 = (bf16[2048,128]{1,0:T(8,128)(2,1)S(1)}, bf16[2048,128]{1,0:T(8,128)(2,1)}, u32[]{:S(2)}) copy-start(bf16[2048,128]{1,0:T(8,128)(2,1)} %param.8) | copy-start | bytes 1572868
  8.1 10.1 %copy-start.3 = (bf16[128,512]{1,0:T(8,128)(2,1)S(1)}, bf16[128,512]{1,0:T(8,128)(2,1)}, u32[]{:S(2)}) copy-start(bf16[128,512]{1,0:T(8,128)(2,1)} %down_ref.3) | copy-start | bytes 393220
  8.1 10.1 %copy-start.4 = (bf16[512,128]{1,0:T(8,128)(2,1)S(1)}, bf16[512,128]{1,0:T(8,128)(2,1)}, u32[]{:S(2)}) copy-start(bf16[512,128]{1,0:T(8,128)(2,1)} %up_ref.3) | copy-start | bytes 393220
  11.1 7.1 %collective-permute-start = (bf16[8,128,256]{2,1,0:T(8,128)(2,1)}, bf16[8,128,256]{2,1,0:T(8,128)(2,1)S(1)}, u32[]{:S(2)}, u32[]{:S(2)}) collective-permute-start(bf16[8,128,256]{2,1,0:T(8,128)(2,1)} %get-tuple-element.12), channel_id=1, source_target_pairs={{0,1},{1,0},{2,3},{3,2},{4,5},{5,4},{6,7},{7,6},{8,9},{9,8},{10,11... | collective-permute-start | bytes 1572872 | tf_op jit(solution)/shard_map/ppermute | solution.py:262
  13.0 5.1 %collective-permute-start.1 = (bf16[128,1024]{1,0:T(8,128)(2,1)}, bf16[128,1024]{1,0:T(8,128)(2,1)S(1)}, u32[]{:S(2)}, u32[]{:S(2)}) collective-permute-start(bf16[128,1024]{1,0:T(8,128)(2,1)} %get-tuple-element.14), channel_id=1, source_target_pairs={{0,1},{1,0},{2,3},{3,2},{4,5},{5,4},{6,7},{7,6},{8,9},{9,8},{10,11... | collective-permute-start | bytes 786440 | tf_op jit(solution)/shard_map/ppermute | solution.py:262
  18.1 2.7 %copy-start.8 = (bf16[16,4608]{1,0:T(8,128)(2,1)}, bf16[16,4608]{1,0:T(8,128)(2,1)S(1)}, u32[]{:S(2)}) copy-start(bf16[16,4608]{1,0:T(8,128)(2,1)S(1)} %fusion.34) | copy-start | bytes 442372
  19.6 1.2 copy-start.2
  20.7 11.0 %copy-start.10 = (s32[128,4]{0,1:T(4,128)S(1)}, s32[128,4]{0,1:T(4,128)}, u32[]{:S(2)}) copy-start(s32[128,4]{0,1:T(4,128)} %param.12) | copy-start | bytes 6148
  20.7 13.0 %copy-start.11 = (f32[128,4]{0,1:T(4,128)S(1)}, f32[128,4]{0,1:T(4,128)}, u32[]{:S(2)}) copy-start(f32[128,4]{0,1:T(4,128)} %param.13) | copy-start | bytes 6148
  20.7 98.1 %all-gather.3.cloned.1.call-start = ((), (), s32[]{:S(2)}) async-start(), calls=%async_computation.7 | async-start | bytes 4866048 | tf_op jit(solution)/shard_map/all_gather | solution.py:266
  21.3 55.3 %all-to-all-start = ((bf16[8,128,768]{2,1,0:T(8,128)(2,1)}), bf16[8,128,768]{2,1,0:T(8,128)(2,1)S(1)}, u32[]{:S(2)}, u32[]{:S(2)}) async-start(bf16[8,128,768]{2,1,0:T(8,128)(2,1)} %copy-done.2), calls=%async_computation.1 | async-start | bytes 3145728 | tf_op jit(solution)/shard_map/all_to_all | solution.py:271
  31.7 180.1 %all-gather.5.cloned.1.call-start = ((), (), s32[]{:S(2)}) async-start(), calls=%async_computation.8 | async-start | bytes 4456448 | tf_op jit(solution)/shard_map/all_gather | solution.py:297
  76.6 0.8 copy-start.5
  118.9 2.3 copy-start.6
  129.7 41.4 %copy-start.7 = (f32[640,128]{1,0:T(8,128)S(1)}, f32[640,128]{1,0:T(8,128)}, u32[]{:S(2)}) copy-start(f32[640,128]{1,0:T(8,128)} %get-tuple-element.20) | copy-start | bytes 983044
  211.7 2.8 %copy-start.12 = (bf16[2048,1024]{1,0:T(8,128)(2,1)S(1)}, bf16[2048,1024]{1,0:T(8,128)(2,1)}, u32[]{:S(2)}) copy-start(bf16[2048,1024]{1,0:T(8,128)(2,1)} %all-gather.5.cloned.1.call-done) | copy-start | bytes 12582916
  238.3 16.1 %all-to-all-start.4 = ((bf16[32,16,256]{2,1,0:T(8,128)(2,1)}), bf16[32,16,256]{2,1,0:T(8,128)(2,1)S(1)}, u32[]{:S(2)}, u32[]{:S(2)}) async-start(bf16[32,16,256]{2,1,0:T(8,128)(2,1)} %broadcast_in_dim.32), calls=%async_computation.5 | async-start | bytes 524288 | tf_op jit(solution)/shard_map/all_to_all | solution.py:309
Sparse Core Ops, SparseCore 0:
  20.9 54.8 reduce-scatter.1
  172.6 39.0 all-gather.4
Sparse Core Ops, SparseCore 1:
  25.4 93.4 all-gather.2

commit v5 on v4

--- a/solution.py
+++ b/solution.py
@@ -12,7 +12,7 @@
 TOPK = 4
 CORES = 2
 CHUNK = 256
-FIRST = 256
+ACROSS = 4
 SMALL = pltpu.CompilerParams(vmem_limit_bytes=16 * 1024 * 1024)
 LARGE = pltpu.CompilerParams(vmem_limit_bytes=56 * 1024 * 1024)
 INNER = (((1,), (0,)), ((), ()))
@@ -100,7 +100,7 @@
         out_specs=pl.BlockSpec((count, 2 * latent_width), lambda j: (0, 0)),
         out_shape=jax.ShapeDtypeStruct((count, 2 * latent_width), jnp.bfloat16),
         scratch_shapes=[pltpu.VMEM((count, latent_width), jnp.float32)] * 2,
-        compiler_params=pltpu.CompilerParams(vmem_limit_bytes=32 * 1024 * 1024),
+        compiler_params=pltpu.CompilerParams(vmem_limit_bytes=50 * 1024 * 1024),
         cost_estimate=pl.CostEstimate(
             flops=12 * count * latent_width * padded,
             bytes_accessed=2 * (weights.size + 2 * rows.size),
@@ -152,24 +152,20 @@
 
 
 def latent_kernel(
-    core_ref, tokens_ref, cotangent_ref, rows_ref, down_ref, up_ref, weights_ref, first_ref, rest_ref
+    core_ref, tokens_ref, cotangent_ref, rows_ref, down_ref, up_ref, weights_ref, result_ref
 ):
     features = tokens_ref.shape[3]
     latent_width = down_ref.shape[1]
-    count, width = first_ref.shape
-    blocks = rest_ref.shape[:2]
+    count = result_ref.shape[0]
     down = jnp.concatenate([down_ref[...], weights_ref[:, :latent_width]], axis=0)
     up = jnp.concatenate([up_ref[...].T, weights_ref[:, latent_width:]], axis=0)
     rows = rows_ref[...].reshape(count, 2 * features)
     kept = tokens_ref[...].reshape(count, features)
     left = jnp.concatenate([kept, rows[:, :features]], axis=1)
-    first_ref[...] = dot(left, down[:, :width]).astype(jnp.bfloat16)
-    part = dot(left, down[:, width:]).astype(jnp.bfloat16)
-    rest_ref[:, :, : latent_width - width] = part.reshape(*blocks, latent_width - width)
+    result_ref[:, :latent_width] = dot(left, down).astype(jnp.bfloat16)
     kept = cotangent_ref[...].reshape(count, features)
     left = jnp.concatenate([kept, rows[:, features:]], axis=1)
-    part = dot(left, up).astype(jnp.bfloat16)
-    rest_ref[:, :, latent_width - width :] = part.reshape(*blocks, latent_width)
+    result_ref[:, latent_width:] = dot(left, up).astype(jnp.bfloat16)
 
 
 def chip_latents(core, tokens, cotangent, rows, down_proj, up_proj, weights):
@@ -178,45 +174,50 @@
     count = chips * tok_rows
     mine = pl.BlockSpec((chips, 1, tok_rows, features), lambda i, core: (0, core[0], 0, 0))
     whole = lambda array: pl.BlockSpec(array.shape, lambda i, core: (0,) * array.ndim)
-    out = [
-        jax.ShapeDtypeStruct((count, FIRST), jnp.bfloat16),
-        jax.ShapeDtypeStruct((chips, tok_rows, 2 * latent_width - FIRST), jnp.bfloat16),
-    ]
+    out = jax.ShapeDtypeStruct((count, 2 * latent_width), jnp.bfloat16)
     return pl.pallas_call(
         latent_kernel,
         grid_spec=pltpu.PrefetchScalarGridSpec(
             num_scalar_prefetch=1,
             grid=(1,),
             in_specs=[mine, mine, whole(rows), whole(down_proj), whole(up_proj), whole(weights)],
-            out_specs=[whole(array) for array in out],
+            out_specs=whole(out),
         ),
         out_shape=out,
         compiler_params=SMALL,
     )(core, tokens, cotangent, rows, down_proj, up_proj, weights)
 
 
-def dispatch_kernel(first_ref, parts_ref, spread_ref, gate_ref, result_ref):
-    width = first_ref.shape[1]
-    latent_width = result_ref.shape[1] // 2
-    rest = parts_ref[0].astype(jnp.float32)
-    for chip in range(1, parts_ref.shape[0]):
-        rest += parts_ref[chip].astype(jnp.float32)
-    rest = rest.astype(jnp.bfloat16)
-    spread = spread_ref[...]
-    result_ref[:, :width] = dot(spread, first_ref[...]).astype(jnp.bfloat16)
-    placed = dot(spread, rest[:, : latent_width - width])
-    result_ref[:, width:latent_width] = placed.astype(jnp.bfloat16)
-    placed = dot(spread, rest[:, latent_width - width :]) * gate_ref[...]
-    result_ref[:, latent_width:] = placed.astype(jnp.bfloat16)
-
-
-def dispatched_rows(first, parts, spread, slot_gate):
-    columns = first.shape[1] + parts.shape[2]
+def dispatch_kernel(latents_ref, spread_ref, gate_ref, result_ref):
+    latent_width = latents_ref.shape[1] // 2
+    placed = dot(spread_ref[...], latents_ref[...])
+    result_ref[:, :latent_width] = placed[:, :latent_width].astype(jnp.bfloat16)
+    result_ref[:, latent_width:] = (placed[:, latent_width:] * gate_ref[...]).astype(jnp.bfloat16)
+
+
+def dispatched_rows(latents, spread, slot_gate):
     return pl.pallas_call(
         dispatch_kernel,
-        out_shape=jax.ShapeDtypeStruct((spread.shape[0], columns), jnp.bfloat16),
+        out_shape=jax.ShapeDtypeStruct((spread.shape[0], latents.shape[1]), jnp.bfloat16),
         compiler_params=SMALL,
-    )(first, parts, spread, slot_gate)
+    )(latents, spread, slot_gate)
+
+
+def arrange_kernel(place_ref, *refs):
+    *parts, result_ref = refs
+    for step, part in enumerate(parts):
+        result_ref[lax.rem(place_ref[0] + step, len(parts))] = part[...]
+
+
+def arranged(place, parts):
+    out = jax.ShapeDtypeStruct((len(parts), *parts[0].shape), parts[0].dtype)
+    return pl.pallas_call(
+        arrange_kernel,
+        in_specs=[pl.BlockSpec(memory_space=pltpu.SMEM)]
+        + [pl.BlockSpec(memory_space=pltpu.VMEM)] * len(parts),
+        out_shape=out,
+        compiler_params=SMALL,
+    )(place, *parts).reshape(-1, parts[0].shape[1])
 
 
 def unpack_kernel(scale, packed_ref, down_ref, up_ref):
@@ -242,7 +243,8 @@
     chips = lax.axis_size("z")
     core = lax.axis_index("c")
     groups = chips * CORES
-    dp = lax.axis_size("dp")
+    dp_axes = ("y", "x")
+    dp = lax.axis_size(dp_axes)
     tok_rows = routes.shape[0]
     group_rows = tokens.shape[0]
     features = tokens.shape[1]
@@ -260,15 +262,19 @@
     place = core.reshape(1).astype(jnp.int32)
     given = swap_operands(place, token_blocks, cotangent_blocks, down_proj, up_proj)
     got_rows, got_weights = (lax.ppermute(array, "c", swap) for array in given)
-    packed, got_rows = lax.optimization_barrier(
-        (packed_weights(expert_in, expert_out, dp), got_rows)
-    )
-    weights = lax.all_gather(packed, "dp", axis=0, tiled=True)
-    first, parts = chip_latents(
+    parts = chip_latents(
         place, token_blocks, cotangent_blocks, got_rows, down_proj, up_proj, got_weights
     )
-    first = lax.psum_scatter(first, "z", scatter_dimension=0, tiled=True)
-    parts = lax.all_to_all(parts, "z", split_axis=0, concat_axis=0, tiled=True)
+    latents = lax.psum_scatter(parts, "z", scatter_dimension=0, tiled=True)
+
+    packed = packed_weights(expert_in, expert_out, dp)
+    across = lax.axis_size("x")
+    neighbours = [packed]
+    for step in range(1, across):
+        backward = [(i, (i - step) % across) for i in range(across)]
+        neighbours.append(lax.ppermute(packed, "x", backward))
+    column = lax.axis_index("x").reshape(1).astype(jnp.int32)
+    weights = lax.all_gather(arranged(column, neighbours), "y", axis=0, tiled=True)
 
     spread, weighted = slot_tables(routes, gate_weights, groups, capacity)
     slot_gate = jnp.sum(weighted, axis=1, keepdims=True)
@@ -284,7 +290,7 @@
             tiled=True,
         ).reshape(slot_count, rows.shape[1])
 
-    outgoing = dispatched_rows(first, parts, spread, slot_gate)
+    outgoing = dispatched_rows(latents, spread, slot_gate)
     result = run_expert(exchange(outgoing), weights)
     returned = exchange(result)
     returned_out = returned[:, :latent_width]
@@ -301,31 +307,34 @@
     down_part_grad = dot(all_grad, tokens, ROWS)
     grads = jnp.concatenate([up_part_grad, down_part_grad], axis=1).astype(bf16)
     grads = grads.reshape(dp, latent_width // dp, 2 * features)
-    grads = lax.all_to_all(grads, "dp", split_axis=0, concat_axis=0, tiled=True)
+    grads = lax.all_to_all(grads, dp_axes, split_axis=0, concat_axis=0, tiled=True)
     mixed = dot(all_out, up_proj).astype(bf16)
     input_grad = dot(all_grad, down_proj, COLS).astype(bf16)
     summed = jnp.sum(grads.astype(jnp.float32), axis=0).astype(bf16)
     summed = jnp.broadcast_to(summed[None], grads.shape)
-    summed = lax.all_to_all(summed, "dp", split_axis=0, concat_axis=0, tiled=True)
+    summed = lax.all_to_all(summed, dp_axes, split_axis=0, concat_axis=0, tiled=True)
     down_grad, up_grad = unpack_grads(summed.reshape(latent_width, 2 * features), grad_scale)
     return mixed, input_grad, down_grad, up_grad
 
 
 def solution(mesh):
     dp, experts = mesh.devices.shape
-    fine = Mesh(mesh.devices.reshape(dp, experts // CORES, CORES), ("dp", "z", "c"))
+    across = math.gcd(dp, ACROSS)
+    shape = (dp // across, across, experts // CORES, CORES)
+    fine = Mesh(mesh.devices.reshape(shape), ("y", "x", "z", "c"))
+    group = ("y", "x")
     expert = ("z", "c")
     in_specs = (
-        P("dp", expert),
-        P("dp", expert),
+        P(group, expert),
+        P(group, expert),
         P(expert, None),
         P(None, expert),
-        P(("dp", "z", "c"), None),
-        P(("dp", "z", "c"), None),
-        P(expert, "dp", None),
-        P(expert, "dp", None),
-    )
-    out_specs = (P("dp", expert), P("dp", expert), P(expert, None), P(None, expert))
+        P(("y", "x", "z", "c"), None),
+        P(("y", "x", "z", "c"), None),
+        P(expert, group, None),
+        P(expert, group, None),
+    )
+    out_specs = (P(group, expert), P(group, expert), P(expert, None), P(None, expert))
     return jax.shard_map(
         on_device, mesh=fine, in_specs=in_specs, out_specs=out_specs, check_vma=False
     )

time: 263 us -> 255 us (0.970)
  waiting for transfers between devices: 89.3 us -> 83.7 us
  blocking collectives: 102 us -> 97 us
    reduce_scatter x1, waiting for transfers between devices: 40.7 us -> 27 us  [on_device(): latents = lax.psum_scatter(parts, 'z', scatter_dimension=0, tiled=True)]
    all_to_all x2 -> x1, starting transfers between devices: 14.9 us -> 4.61 us  [on_device(): lax.all_to_all(summed, dp_axes, split_axis=0, concat_axis=0, tiled=True)]
    ppermute x0 -> x3, starting transfers between devices: none -> 10.2 us  [on_device(): neighbours.append(lax.ppermute(packed, 'x', backward))]
    ppermute x0 -> x3, waiting for transfers between devices: none -> 6.87 us  [on_device(): neighbours.append(lax.ppermute(packed, 'x', backward))]
    all_to_all x2, blocking collectives: 79.4 us -> 74.6 us  [exchange(): lax.all_to_all(rows.reshape(groups, capacity, rows.shape[1]), expert, spl...]
    all_gather x1, waiting for transfers between devices: 39.2 us -> 43.1 us  [on_device(): latents = lax.all_gather(latents, expert, axis=0, tiled=True)]
    unnamed x31 -> x33, local copies, waits for them, and re-layouts: 4.83 us -> 6.11 us
    all_to_all x2 -> x1, waiting for transfers between devices: 6.21 us -> 5.32 us  [on_device(): lax.all_to_all(summed, dp_axes, split_axis=0, concat_axis=0, tiled=True)]
  transfers between devices with their start and end apart: 7 -> 9, of which waited for: 5 -> 7; matrix products, arithmetic and copies ran while one was open for 5% -> 4% of each run, Pallas kernels for 0% -> 1%
where the time goes in v5:
time: 255 us
  blocking collectives  97 us (38%)
  waiting for transfers between devices  83.7 us (33%)
  starting transfers between devices  19.2 us (8%)
  Pallas kernels  16.7 us (7%)
  between operations  15.8 us (6%)
  matrix products  12 us (5%)
  local copies, waits for them, and re-layouts  7.66 us (3%)
    all_to_all x2, blocking collectives, exchange(): lax.all_to_all(rows.reshape(groups, capacity, rows.shape[1]), expert, spl...  74.6 us
    all_gather x1, waiting for transfers between devices, on_device(): latents = lax.all_gather(latents, expert, axis=0, tiled=True)  43.1 us
    reduce_scatter x1, waiting for transfers between devices, on_device(): latents = lax.psum_scatter(parts, 'z', scatter_dimension=0, tiled=True)  27 us
    all_to_all x1, blocking collectives, on_device(): lax.all_to_all(grads, dp_axes, split_axis=0, concat_axis=0, tiled=True)  22.4 us
    dot_general x8, matrix products, dot(): lax.dot_general(left, right, dims, preferred_element_type=jnp.float32)  12 us
    ppermute x3, starting transfers between devices, on_device(): neighbours.append(lax.ppermute(packed, 'x', backward))  10.2 us
    pallas_call x1, Pallas kernels, run_expert(): pl.pallas_call(expert_kernel, grid=(steps,), in_specs=[pl.BlockSpec((coun...  9.49 us
    ppermute x3, waiting for transfers between devices, on_device(): neighbours.append(lax.ppermute(packed, 'x', backward))  6.87 us
  transfers between devices with their start and end apart: 9, of which 7 were waited for; matrix products, arithmetic and copies ran while one was open for 4% of the time, Pallas kernels for 1%

profile of v5, /device:TPU:8, one launch (start us, length us, event | category | flops | bytes accessed | tf_op | source)
XLA Modules:
  0.0 254.6 jit_solution(6104151551578200221)
XLA Ops:
  8.0 0.0 reduce-scatter.2.cloned.1.call-start
  8.0 2.9 %shard_map.111 = (bf16[8,128,256]{2,1,0:T(8,128)(2,1)}, bf16[128,1024]{1,0:T(8,128)(2,1)}) custom-call(s32[1]{0:T(128)} %bitcast.3.core_ref, bf16[8,2,128,128]{3,2,1,0:T(8,128)(2,1)} %bitcast.49, bf16[8,2,128,128]{3,2,1,0:T(8,128)(2,1)} %bitcast.51, bf16[128,512]{1,0:T(8,128)(2,1)} %down_ref.3, bf16[512,128]{1,0:T(8,128)(2,1)} %up_ref.3), custom_call_target="tpu_custom_call" | custom-call | tf_op jit(solution)/shard_map/pallas_call | solution.py:135
  10.9 1.9 collective-permute-start
  12.9 2.4 collective-permute-start.1
  15.3 1.4 collective-permute-done.1.weights_ref
  16.6 0.0 collective-permute-done.rows_ref
  16.6 1.0 copy-done
  17.7 1.0 copy-done.2
  18.7 0.9 copy-done.4
  19.6 0.9 copy-done.6
  20.5 2.1 shard_map.112
  22.7 0.0 reduce-scatter.2.cloned.1.call-update
  22.7 0.0 all-gather.3.cloned.1.call-start
  22.7 0.8 copy-done.10
  23.5 0.1 slice_bitcast_fusion.1
  23.6 0.0 copy-start.11
  23.6 1.7 fusion.2
  25.3 0.0 copy-start.12
  25.4 4.7 %collective-permute-start.2 = (bf16[16,4608]{1,0:T(8,128)(2,1)S(1)}, bf16[16,4608]{1,0:T(8,128)(2,1)S(1)}, u32[]{:S(2)}, u32[]{:S(2)}) collective-permute-start(bf16[16,4608]{1,0:T(8,128)(2,1)S(1)} %fusion.34.refs_0_), channel_id=1, source_target_pairs={{0,48},{16,0},{32,16},{48,32},{1,49},{17,1},{33,17},{49,33},{2,50}... | collective-permute-start | bytes 442376 | tf_op jit(solution)/shard_map/ppermute | solution.py:275
  30.1 2.7 %collective-permute-start.3 = (bf16[16,4608]{1,0:T(8,128)(2,1)S(1)}, bf16[16,4608]{1,0:T(8,128)(2,1)S(1)}, u32[]{:S(2)}, u32[]{:S(2)}) collective-permute-start(bf16[16,4608]{1,0:T(8,128)(2,1)S(1)} %fusion.34.refs_0_), channel_id=1, source_target_pairs={{0,32},{16,48},{32,0},{48,16},{1,33},{17,49},{33,1},{49,17},{2,34}... | collective-permute-start | bytes 442376 | tf_op jit(solution)/shard_map/ppermute | solution.py:275
  32.8 2.8 %collective-permute-start.4 = (bf16[16,4608]{1,0:T(8,128)(2,1)S(1)}, bf16[16,4608]{1,0:T(8,128)(2,1)S(1)}, u32[]{:S(2)}, u32[]{:S(2)}) collective-permute-start(bf16[16,4608]{1,0:T(8,128)(2,1)S(1)} %fusion.34.refs_0_), channel_id=1, source_target_pairs={{0,16},{16,32},{32,48},{48,0},{1,17},{17,33},{33,49},{49,1},{2,18}... | collective-permute-start | bytes 442376 | tf_op jit(solution)/shard_map/ppermute | solution.py:275
  35.6 1.3 collective-permute-done.2.refs_1_
  36.9 3.3 %collective-permute-done.3.refs_2_ = bf16[16,4608]{1,0:T(8,128)(2,1)S(1)} collective-permute-done((bf16[16,4608]{1,0:T(8,128)(2,1)S(1)}, bf16[16,4608]{1,0:T(8,128)(2,1)S(1)}, u32[]{:S(2)}, u32[]{:S(2)}) %collective-permute-start.3) | collective-permute-done | bytes 147488 | tf_op jit(solution)/shard_map/ppermute | solution.py:275
  40.2 2.3 collective-permute-done.4.refs_3_
  42.5 0.9 shard_map.114
  43.3 0.0 all-gather.3.cloned.1.call-update
  43.4 0.0 all-gather.5.cloned.1.call-start
  43.4 0.1 copy.26
  43.5 0.1 eq.54
  43.6 0.1 eq.58
  43.8 1.2 reduce-window.6
  44.9 0.2 slice_reduce_fusion
  45.2 0.1 fusion.28
  45.3 0.1 reduce_sum.42
  45.4 0.1 copy.29
  45.5 0.2 fusion.9
  45.7 0.2 select_reduce_fusion.1
  45.9 0.1 broadcast_in_dim.33.gate_ref
  46.1 27.0 %reduce-scatter.2.cloned.1.call-done.latents_ref = bf16[128,1024]{1,0:T(8,128)(2,1)} async-done(((bf16[1024,1024]{1,0:T(8,128)(2,1)}), bf16[128,1024]{1,0:T(8,128)(2,1)}) %reduce-scatter.2.cloned.1.call-update) | async-done | bytes 262160 | tf_op jit(solution)/shard_map/reduce_scatter | solution.py:268
  73.0 1.0 copy-done.8
  74.0 0.5 shard_map.113
  74.5 37.7 %all_to_all.20 = bf16[16,40,1024]{2,1,0:T(8,128)(2,1)S(1)} all-to-all(bf16[16,40,1024]{2,1,0:T(8,128)(2,1)S(1)} %bitcast.48), channel_id=1, replica_groups=mesh['y'=8,'x'=4,'z'=8,'c'=2] {'z','c'}, dimensions={0} | all-to-all | bytes 2621440 | tf_op jit(solution)/shard_map/all_to_all | solution.py:285
  112.2 9.5 %shard_map.115 = bf16[640,1024]{1,0:T(8,128)(2,1)S(1)} custom-call(bf16[640,1024]{1,0:T(8,128)(2,1)S(1)} %bitcast.53, bf16[512,4608]{1,0:T(8,128)(2,1)} %all-gather.3.cloned.1.call-done.gate_ref.up_ref.out_ref, bf16[512,4608]{1,0:T(8,128)(2,1)} %all-gather.3.cloned.1.call-done.gate_ref.up_ref.out_ref, ...), custom_call_target="tpu_custom_call" | custom-call | flops 6039797760 | bytes 7340032 | tf_op jit(solution)/shard_map/pallas_call | solution.py:91
  121.7 36.9 %all_to_all.21 = bf16[16,40,1024]{2,1,0:T(8,128)(2,1)S(1)} all-to-all(bf16[16,40,1024]{2,1,0:T(8,128)(2,1)S(1)} %bitcast.54), channel_id=1, replica_groups=mesh['y'=8,'x'=4,'z'=8,'c'=2] {'z','c'}, dimensions={0} | all-to-all | bytes 2621440 | tf_op jit(solution)/shard_map/all_to_all | solution.py:285
  158.6 0.3 convolution_convert_fusion.2
  158.9 0.3 fusion.19
  159.2 0.3 fusion.10
  159.5 0.7 pad_maximum_fusion
  160.2 0.0 all-gather.5.cloned.1.call-update
  160.2 0.0 copy-start.3
  160.2 43.1 %all-gather.5.cloned.1.call-done = bf16[2048,1024]{1,0:T(8,128)(2,1)} async-done(((bf16[128,1024]{1,0:T(8,128)(2,1)}), bf16[2048,1024]{1,0:T(8,128)(2,1)}) %all-gather.5.cloned.1.call-update) | async-done | bytes 4194320 | tf_op jit(solution)/shard_map/all_gather | solution.py:303
  203.4 0.0 copy-done.1
  203.4 2.5 fusion.14
  205.9 0.3 copy-done.13
  206.2 0.8 fusion.11
  207.0 0.0 copy-start.5
  207.0 22.4 %all_to_all.22 = bf16[32,16,256]{2,1,0:T(8,128)(2,1)S(1)} all-to-all(bf16[32,16,256]{2,1,0:T(8,128)(2,1)S(1)} %pad_maximum_fusion.1), channel_id=1, replica_groups=mesh['y'=8,'x'=4,'z'=8,'c'=2] {'y','x'}, dimensions={0} | all-to-all | bytes 524288 | tf_op jit(solution)/shard_map/all_to_all | solution.py:310
  229.4 0.1 reduce_sum.45
  229.4 0.7 broadcast_in_dim.32
  230.2 4.6 %all-to-all-start.3 = ((bf16[32,16,256]{2,1,0:T(8,128)(2,1)}), bf16[32,16,256]{2,1,0:T(8,128)(2,1)S(1)}, u32[]{:S(2)}, u32[]{:S(2)}) async-start(bf16[32,16,256]{2,1,0:T(8,128)(2,1)} %broadcast_in_dim.32), calls=%async_computation.4 | async-start | bytes 524288 | tf_op jit(solution)/shard_map/all_to_all | solution.py:315
  234.8 3.1 %convolution_convert_fusion.1 = bf16[2048,128]{1,0:T(8,128)(2,1)} fusion(bf16[512,128]{1,0:T(8,128)(2,1)S(1)} %copy-done.5, bf16[2048,1024]{1,0:T(8,128)(2,1)} %all-gather.5.cloned.1.call-done), kind=kOutput, calls=%fused_computation.4 | convolution fusion | flops 268697600 | bytes 2752512 | tf_op jit(solution)/shard_map/dot_general | solution.py:24
  237.9 3.1 %convolution_convert_fusion = bf16[2048,128]{1,0:T(8,128)(2,1)} fusion(bf16[128,512]{1,0:T(8,128)(2,1)S(1)} %copy-done.7, bf16[2048,1024]{1,0:T(8,128)(2,1)} %all-gather.5.cloned.1.call-done), kind=kOutput, calls=%fused_computation.3 | convolution fusion | flops 268697600 | bytes 2752512 | tf_op jit(solution)/shard_map/dot_general | solution.py:24
  241.0 5.3 %all-to-all-done.3 = bf16[32,16,256]{2,1,0:T(8,128)(2,1)S(1)} async-done(((bf16[32,16,256]{2,1,0:T(8,128)(2,1)}), bf16[32,16,256]{2,1,0:T(8,128)(2,1)S(1)}, u32[]{:S(2)}, u32[]{:S(2)}) %all-to-all-start.3) | async-done | bytes 262176 | tf_op jit(solution)/shard_map/all_to_all | solution.py:315
  246.3 0.8 shard_map.116
  (29 shorter events, 0.2 us)
Async XLA Ops:
  8.0 65.0 %reduce-scatter.2.cloned.1.call-start = ((), (), s32[]{:S(2)}) async-start(), calls=%async_computation.5 | async-start | bytes 2359296 | tf_op jit(solution)/shard_map/reduce_scatter | solution.py:268
  10.9 5.7 %collective-permute-start = (bf16[8,128,256]{2,1,0:T(8,128)(2,1)}, bf16[8,128,256]{2,1,0:T(8,128)(2,1)S(1)}, u32[]{:S(2)}, u32[]{:S(2)}) collective-permute-start(bf16[8,128,256]{2,1,0:T(8,128)(2,1)} %get-tuple-element.8), channel_id=1, source_target_pairs={{0,1},{1,0},{2,3},{3,2},{4,5},{5,4},{6,7},{7,6},{8,9},{9,8},{10,11... | collective-permute-start | bytes 1572872 | tf_op jit(solution)/shard_map/ppermute | solution.py:264
  12.9 3.8 %collective-permute-start.1 = (bf16[128,1024]{1,0:T(8,128)(2,1)}, bf16[128,1024]{1,0:T(8,128)(2,1)S(1)}, u32[]{:S(2)}, u32[]{:S(2)}) collective-permute-start(bf16[128,1024]{1,0:T(8,128)(2,1)} %get-tuple-element.9), channel_id=1, source_target_pairs={{0,1},{1,0},{2,3},{3,2},{4,5},{5,4},{6,7},{7,6},{8,9},{9,8},{10,11... | collective-permute-start | bytes 786440 | tf_op jit(solution)/shard_map/ppermute | solution.py:264
  16.6 1.0 copy-start
  17.7 1.0 copy-start.2
  18.7 0.9 copy-start.4
  19.6 0.9 copy-start.6
  22.7 0.9 copy-start.10
  22.7 2.7 %copy-start.9 = (bf16[1,42,512]{2,1,0:T(8,128)(2,1)S(1)}, bf16[1,42,512]{2,1,0:T(8,128)(2,1)}, u32[]{:S(2)}) copy-start(bf16[1,42,512]{2,1,0:T(8,128)(2,1)} %param.15) | copy-start | bytes 129028
  22.7 89.5 %all-gather.3.cloned.1.call-start = ((), (), s32[]{:S(2)}) async-start(), calls=%async_computation.6 | async-start | bytes 5308416 | tf_op jit(solution)/shard_map/all_gather | solution.py:277
  23.6 19.8 %copy-start.11 = (s32[128,4]{0,1:T(4,128)S(1)}, s32[128,4]{0,1:T(4,128)}, u32[]{:S(2)}) copy-start(s32[128,4]{0,1:T(4,128)} %param.12) | copy-start | bytes 6148
  25.3 20.4 %copy-start.12 = (f32[128,4]{0,1:T(4,128)S(1)}, f32[128,4]{0,1:T(4,128)}, u32[]{:S(2)}) copy-start(f32[128,4]{0,1:T(4,128)} %param.13) | copy-start | bytes 6148
  25.4 11.5 %collective-permute-start.2 = (bf16[16,4608]{1,0:T(8,128)(2,1)S(1)}, bf16[16,4608]{1,0:T(8,128)(2,1)S(1)}, u32[]{:S(2)}, u32[]{:S(2)}) collective-permute-start(bf16[16,4608]{1,0:T(8,128)(2,1)S(1)} %fusion.34.refs_0_), channel_id=1, source_target_pairs={{0,48},{16,0},{32,16},{48,32},{1,49},{17,1},{33,17},{49,33},{2,50}... | collective-permute-start | bytes 442376 | tf_op jit(solution)/shard_map/ppermute | solution.py:275
  30.1 10.1 %collective-permute-start.3 = (bf16[16,4608]{1,0:T(8,128)(2,1)S(1)}, bf16[16,4608]{1,0:T(8,128)(2,1)S(1)}, u32[]{:S(2)}, u32[]{:S(2)}) collective-permute-start(bf16[16,4608]{1,0:T(8,128)(2,1)S(1)} %fusion.34.refs_0_), channel_id=1, source_target_pairs={{0,32},{16,48},{32,0},{48,16},{1,33},{17,49},{33,1},{49,17},{2,34}... | collective-permute-start | bytes 442376 | tf_op jit(solution)/shard_map/ppermute | solution.py:275
  32.8 9.7 %collective-permute-start.4 = (bf16[16,4608]{1,0:T(8,128)(2,1)S(1)}, bf16[16,4608]{1,0:T(8,128)(2,1)S(1)}, u32[]{:S(2)}, u32[]{:S(2)}) collective-permute-start(bf16[16,4608]{1,0:T(8,128)(2,1)S(1)} %fusion.34.refs_0_), channel_id=1, source_target_pairs={{0,16},{16,32},{32,48},{48,0},{1,17},{17,33},{33,49},{49,1},{2,18}... | collective-permute-start | bytes 442376 | tf_op jit(solution)/shard_map/ppermute | solution.py:275
  43.4 160.0 %all-gather.5.cloned.1.call-start = ((), (), s32[]{:S(2)}) async-start(), calls=%async_computation.7 | async-start | bytes 4456448 | tf_op jit(solution)/shard_map/all_gather | solution.py:303
  73.0 1.0 copy-start.8
  158.6 44.8 %copy-start.1 = (bf16[2048,128]{1,0:T(8,128)(2,1)S(1)}, bf16[2048,128]{1,0:T(8,128)(2,1)}, u32[]{:S(2)}) copy-start(bf16[2048,128]{1,0:T(8,128)(2,1)} %param.8) | copy-start | bytes 1572868
  160.2 45.6 %copy-start.3 = (bf16[2048,128]{1,0:T(8,128)(2,1)S(1)}, bf16[2048,128]{1,0:T(8,128)(2,1)}, u32[]{:S(2)}) copy-start(bf16[2048,128]{1,0:T(8,128)(2,1)} %param.9) | copy-start | bytes 1572868
  203.4 2.8 %copy-start.13 = (bf16[2048,1024]{1,0:T(8,128)(2,1)S(1)}, bf16[2048,1024]{1,0:T(8,128)(2,1)}, u32[]{:S(2)}) copy-start(bf16[2048,1024]{1,0:T(8,128)(2,1)} %all-gather.5.cloned.1.call-done) | copy-start | bytes 12582916
  207.0 27.8 %copy-start.5 = (bf16[512,128]{1,0:T(8,128)(2,1)S(1)}, bf16[512,128]{1,0:T(8,128)(2,1)}, u32[]{:S(2)}) copy-start(bf16[512,128]{1,0:T(8,128)(2,1)} %up_ref.3) | copy-start | bytes 393220
  229.4 8.4 %copy-start.7 = (bf16[128,512]{1,0:T(8,128)(2,1)S(1)}, bf16[128,512]{1,0:T(8,128)(2,1)}, u32[]{:S(2)}) copy-start(bf16[128,512]{1,0:T(8,128)(2,1)} %down_ref.3) | copy-start | bytes 393220
  230.2 16.1 %all-to-all-start.3 = ((bf16[32,16,256]{2,1,0:T(8,128)(2,1)}), bf16[32,16,256]{2,1,0:T(8,128)(2,1)S(1)}, u32[]{:S(2)}, u32[]{:S(2)}) async-start(bf16[32,16,256]{2,1,0:T(8,128)(2,1)} %broadcast_in_dim.32), calls=%async_computation.4 | async-start | bytes 524288 | tf_op jit(solution)/shard_map/all_to_all | solution.py:315
Sparse Core Ops, SparseCore 0:
  22.8 50.1 reduce-scatter.1
  160.4 42.9 all-gather.4
Sparse Core Ops, SparseCore 1:
  43.4 63.1 all-gather.2

commit v6 on v5

--- a/solution.py
+++ b/solution.py
@@ -14,7 +14,6 @@
 CHUNK = 256
 ACROSS = 4
 SMALL = pltpu.CompilerParams(vmem_limit_bytes=16 * 1024 * 1024)
-LARGE = pltpu.CompilerParams(vmem_limit_bytes=56 * 1024 * 1024)
 INNER = (((1,), (0,)), ((), ()))
 COLS = (((1,), (1,)), ((), ()))
 ROWS = (((0,), (0,)), ((), ()))
@@ -34,9 +33,15 @@
     slot = (flat_routes * capacity + position).reshape(routes.shape)
     slot_ids = jnp.arange(experts * capacity, dtype=jnp.int32)
     matches = slot.T[:, None, :] == slot_ids[None, :, None]
-    spread = jnp.any(matches, axis=0)
+    to_slot = jnp.any(matches, axis=0).astype(jnp.bfloat16)
     weighted = jnp.sum(jnp.where(matches, gate_weights.T[:, None, :], 0.0), axis=0)
-    return spread.astype(jnp.bfloat16), weighted
+    slot_gate = jnp.sum(weighted, axis=1, keepdims=True)
+    matches = slot[:, :, None] == slot_ids[None, None, :]
+    to_token = jnp.any(matches, axis=1).astype(jnp.bfloat16)
+    weighted = jnp.sum(jnp.where(matches, gate_weights[:, :, None], 0.0), axis=1)
+    gate_high = weighted.astype(jnp.bfloat16)
+    gate_low = (weighted - gate_high.astype(jnp.float32)).astype(jnp.bfloat16)
+    return to_slot, slot_gate, to_token, jnp.concatenate([gate_high, gate_low], axis=0)
 
 
 def packed_weights(expert_in, expert_out, dp):
@@ -109,83 +114,100 @@
     )(rows, weights, weights, weights)
 
 
-def swap_kernel(core_ref, tokens_ref, cotangent_ref, down_ref, up_ref, rows_ref, weights_ref, sems):
-    other = 1 - core_ref[0]
+def swap_kernel(
+    core_ref, tokens_ref, cotangent_ref, down_ref, up_ref, rows_ref, kept_ref, weights_ref, up_here, sems
+):
+    mine = core_ref[0]
     features = tokens_ref.shape[3]
     latent_width = down_ref.shape[1]
-    copies = [
-        pltpu.make_async_copy(
-            tokens_ref.at[:, other], rows_ref.at[:, :, pl.ds(0, features)], sems.at[0]
-        ),
-        pltpu.make_async_copy(
-            cotangent_ref.at[:, other], rows_ref.at[:, :, pl.ds(features, features)], sems.at[1]
-        ),
+    first, second = pl.ds(0, features), pl.ds(features, features)
+    moves = [
+        (up_ref, up_here),
+        (tokens_ref.at[:, 1 - mine], rows_ref.at[:, :, first]),
+        (cotangent_ref.at[:, 1 - mine], rows_ref.at[:, :, second]),
+        (down_ref, weights_ref.at[:, pl.ds(0, latent_width)]),
+        (tokens_ref.at[:, mine], kept_ref.at[:, :, first]),
+        (cotangent_ref.at[:, mine], kept_ref.at[:, :, second]),
     ]
+    copies = [pltpu.make_async_copy(*move, sems.at[i]) for i, move in enumerate(moves)]
     for copy in copies:
         copy.start()
-    weights_ref[:, :latent_width] = down_ref[...]
-    weights_ref[:, latent_width:] = up_ref[...].T
-    for copy in copies:
+    copies[0].wait()
+    weights_ref[:, latent_width:] = up_here[...].T
+    for copy in copies[1:]:
         copy.wait()
 
 
 def swap_operands(core, tokens, cotangent, down_proj, up_proj):
     chips, _, tok_rows, features = tokens.shape
     latent_width = down_proj.shape[1]
+    rows = jax.ShapeDtypeStruct((chips, tok_rows, 2 * features), jnp.bfloat16)
     return pl.pallas_call(
         swap_kernel,
-        in_specs=[
-            pl.BlockSpec(memory_space=pltpu.SMEM),
-            pl.BlockSpec(memory_space=pl.ANY),
-            pl.BlockSpec(memory_space=pl.ANY),
-            pl.BlockSpec(memory_space=pltpu.VMEM),
-            pl.BlockSpec(memory_space=pltpu.VMEM),
+        in_specs=[pl.BlockSpec(memory_space=pltpu.SMEM)]
+        + [pl.BlockSpec(memory_space=pltpu.HBM)] * 4,
+        out_specs=[pl.BlockSpec(memory_space=pltpu.VMEM)] * 3,
+        out_shape=[rows, rows, jax.ShapeDtypeStruct((features, 2 * latent_width), jnp.bfloat16)],
+        scratch_shapes=[
+            pltpu.VMEM((latent_width, features), jnp.bfloat16),
+            pltpu.SemaphoreType.DMA((6,)),
         ],
-        out_specs=[pl.BlockSpec(memory_space=pltpu.VMEM)] * 2,
-        out_shape=[
-            jax.ShapeDtypeStruct((chips, tok_rows, 2 * features), jnp.bfloat16),
-            jax.ShapeDtypeStruct((features, 2 * latent_width), jnp.bfloat16),
-        ],
-        scratch_shapes=[pltpu.SemaphoreType.DMA((2,))],
-        compiler_params=LARGE,
+        compiler_params=SMALL,
     )(core, tokens, cotangent, down_proj, up_proj)
 
 
-def latent_kernel(
-    core_ref, tokens_ref, cotangent_ref, rows_ref, down_ref, up_ref, weights_ref, result_ref
-):
-    features = tokens_ref.shape[3]
-    latent_width = down_ref.shape[1]
+def latent_kernel(kept_ref, got_ref, here_ref, there_ref, result_ref):
     count = result_ref.shape[0]
-    down = jnp.concatenate([down_ref[...], weights_ref[:, :latent_width]], axis=0)
-    up = jnp.concatenate([up_ref[...].T, weights_ref[:, latent_width:]], axis=0)
-    rows = rows_ref[...].reshape(count, 2 * features)
-    kept = tokens_ref[...].reshape(count, features)
-    left = jnp.concatenate([kept, rows[:, :features]], axis=1)
-    result_ref[:, :latent_width] = dot(left, down).astype(jnp.bfloat16)
-    kept = cotangent_ref[...].reshape(count, features)
-    left = jnp.concatenate([kept, rows[:, features:]], axis=1)
-    result_ref[:, latent_width:] = dot(left, up).astype(jnp.bfloat16)
-
-
-def chip_latents(core, tokens, cotangent, rows, down_proj, up_proj, weights):
-    chips, _, tok_rows, features = tokens.shape
-    latent_width = down_proj.shape[1]
-    count = chips * tok_rows
-    mine = pl.BlockSpec((chips, 1, tok_rows, features), lambda i, core: (0, core[0], 0, 0))
-    whole = lambda array: pl.BlockSpec(array.shape, lambda i, core: (0,) * array.ndim)
-    out = jax.ShapeDtypeStruct((count, 2 * latent_width), jnp.bfloat16)
+    latent_width = here_ref.shape[1] // 2
+    features = kept_ref.shape[2] // 2
+    kept = kept_ref[...].reshape(count, 2 * features)
+    got = got_ref[...].reshape(count, 2 * features)
+    for half in range(2):
+        rows = slice(half * features, (half + 1) * features)
+        here = slice(half * latent_width, (half + 1) * latent_width)
+        left = jnp.concatenate([kept[:, rows], got[:, rows]], axis=1)
+        right = jnp.concatenate([here_ref[:, here], there_ref[:, here]], axis=0)
+        result_ref[:, here] = dot(left, right).astype(jnp.bfloat16)
+
+
+def chip_latents(kept, got, here, there):
+    count = kept.shape[0] * kept.shape[1]
     return pl.pallas_call(
         latent_kernel,
-        grid_spec=pltpu.PrefetchScalarGridSpec(
-            num_scalar_prefetch=1,
-            grid=(1,),
-            in_specs=[mine, mine, whole(rows), whole(down_proj), whole(up_proj), whole(weights)],
-            out_specs=whole(out),
-        ),
-        out_shape=out,
-        compiler_params=SMALL,
-    )(core, tokens, cotangent, rows, down_proj, up_proj, weights)
+        out_shape=jax.ShapeDtypeStruct((count, here.shape[1]), jnp.bfloat16),
+        compiler_params=SMALL,
+    )(kept, got, here, there)
+
+
+def combine_kernel(returned_ref, gates_ref, spread_ref, result_ref):
+    latent_width = returned_ref.shape[1] // 2
+    count = spread_ref.shape[0]
+    gated = dot(gates_ref[...], returned_ref[:, :latent_width])
+    result_ref[:, :latent_width] = (gated[:count] + gated[count:]).astype(jnp.bfloat16)
+    result_ref[:, latent_width:] = dot(spread_ref[...], returned_ref[:, latent_width:]).astype(
+        jnp.bfloat16
+    )
+
+
+def combined_latents(returned, gates, spread):
+    return pl.pallas_call(
+        combine_kernel,
+        out_shape=jax.ShapeDtypeStruct((spread.shape[0], returned.shape[1]), jnp.bfloat16),
+        compiler_params=SMALL,
+    )(returned, gates, spread)
+
+
+def share_kernel(pieces_ref, result_ref):
+    summed = jnp.sum(pieces_ref[...].astype(jnp.float32), axis=0).astype(jnp.bfloat16)
+    result_ref[...] = jnp.broadcast_to(summed[None], result_ref.shape)
+
+
+def shared_sums(pieces):
+    return pl.pallas_call(
+        share_kernel,
+        out_shape=jax.ShapeDtypeStruct(pieces.shape, jnp.bfloat16),
+        compiler_params=SMALL,
+    )(pieces)
 
 
 def dispatch_kernel(latents_ref, spread_ref, gate_ref, result_ref):
@@ -260,11 +282,11 @@
     token_blocks = tokens.reshape(blocked)
     cotangent_blocks = cotangent.reshape(blocked)
     place = core.reshape(1).astype(jnp.int32)
-    given = swap_operands(place, token_blocks, cotangent_blocks, down_proj, up_proj)
-    got_rows, got_weights = (lax.ppermute(array, "c", swap) for array in given)
-    parts = chip_latents(
-        place, token_blocks, cotangent_blocks, got_rows, down_proj, up_proj, got_weights
-    )
+    given, kept, here = swap_operands(
+        place, token_blocks, cotangent_blocks, down_proj, up_proj
+    )
+    got, there = (lax.ppermute(array, "c", swap) for array in (given, here))
+    parts = chip_latents(kept, got, here, there)
     latents = lax.psum_scatter(parts, "z", scatter_dimension=0, tiled=True)
 
     packed = packed_weights(expert_in, expert_out, dp)
@@ -276,10 +298,7 @@
     column = lax.axis_index("x").reshape(1).astype(jnp.int32)
     weights = lax.all_gather(arranged(column, neighbours), "y", axis=0, tiled=True)
 
-    spread, weighted = slot_tables(routes, gate_weights, groups, capacity)
-    slot_gate = jnp.sum(weighted, axis=1, keepdims=True)
-    gate_high = weighted.astype(bf16)
-    gate_low = (weighted - gate_high.astype(jnp.float32)).astype(bf16)
+    to_slot, slot_gate, to_token, gates = slot_tables(routes, gate_weights, groups, capacity)
 
     def exchange(rows):
         return lax.all_to_all(
@@ -290,16 +309,10 @@
             tiled=True,
         ).reshape(slot_count, rows.shape[1])
 
-    outgoing = dispatched_rows(latents, spread, slot_gate)
+    outgoing = dispatched_rows(latents, to_slot, slot_gate)
     result = run_expert(exchange(outgoing), weights)
     returned = exchange(result)
-    returned_out = returned[:, :latent_width]
-    latent_out = (dot(gate_high, returned_out, ROWS) + dot(gate_low, returned_out, ROWS)).astype(
-        bf16
-    )
-    latent_grad = dot(spread, returned[:, latent_width:], ROWS).astype(bf16)
-
-    latents = jnp.concatenate([latent_out, latent_grad], axis=1)
+    latents = combined_latents(returned, gates, to_token)
     latents = lax.all_gather(latents, expert, axis=0, tiled=True)
     all_out = latents[:, :latent_width]
     all_grad = latents[:, latent_width:]
@@ -310,8 +323,7 @@
     grads = lax.all_to_all(grads, dp_axes, split_axis=0, concat_axis=0, tiled=True)
     mixed = dot(all_out, up_proj).astype(bf16)
     input_grad = dot(all_grad, down_proj, COLS).astype(bf16)
-    summed = jnp.sum(grads.astype(jnp.float32), axis=0).astype(bf16)
-    summed = jnp.broadcast_to(summed[None], grads.shape)
+    summed = shared_sums(grads)
     summed = lax.all_to_all(summed, dp_axes, split_axis=0, concat_axis=0, tiled=True)
     down_grad, up_grad = unpack_grads(summed.reshape(latent_width, 2 * features), grad_scale)
     return mixed, input_grad, down_grad, up_grad

time: 255 us -> 254 us (level)
  blocking collectives: 97 us -> 60.2 us
  waiting for transfers between devices: 83.7 us -> 117 us
  starting transfers between devices: 19.2 us -> 23.1 us
    all_to_all x2 -> x1, blocking collectives: 74.6 us -> 37.8 us  [exchange(): lax.all_to_all(rows.reshape(groups, capacity, rows.shape[1]), expert, spl...]
    all_to_all x0 -> x1, waiting for transfers between devices: none -> 31.7 us  [exchange(): lax.all_to_all(rows.reshape(groups, capacity, rows.shape[1]), expert, spl...]
    all_to_all x0 -> x1, starting transfers between devices: none -> 3.7 us  [exchange(): lax.all_to_all(rows.reshape(groups, capacity, rows.shape[1]), expert, spl...]
    dot_general x8 -> x5, matrix products: 12 us -> 11.1 us  [dot(): lax.dot_general(left, right, dims, preferred_element_type=jnp.float32)]
  transfers between devices with their start and end apart: 9 -> 10, of which waited for: 7 -> 8; matrix products, arithmetic and copies ran while one was open for 4% -> 4% of each run, Pallas kernels for 1% -> 1%
where the time goes in v6:
time: 254 us; the launch traced here: 253 us
  waiting for transfers between devices  117 us (46%)
  blocking collectives  60.2 us (24%)
  starting transfers between devices  23.1 us (9%)
  Pallas kernels  17.2 us (7%)
  between operations  15.8 us (6%)
  matrix products  11.1 us (4%)
  local copies, waits for them, and re-layouts  6.15 us (2%)
    all_gather x1, waiting for transfers between devices, on_device(): latents = lax.all_gather(latents, expert, axis=0, tiled=True)  44.3 us
    all_to_all x1, blocking collectives, exchange(): lax.all_to_all(rows.reshape(groups, capacity, rows.shape[1]), expert, spl...  37.8 us
    all_to_all x1, waiting for transfers between devices, exchange(): lax.all_to_all(rows.reshape(groups, capacity, rows.shape[1]), expert, spl...  31.7 us
    reduce_scatter x1, waiting for transfers between devices, on_device(): latents = lax.psum_scatter(parts, 'z', scatter_dimension=0, tiled=True)  27.8 us
    all_to_all x1, blocking collectives, on_device(): lax.all_to_all(grads, dp_axes, split_axis=0, concat_axis=0, tiled=True)  22.4 us
    dot_general x5, matrix products, dot(): lax.dot_general(left, right, dims, preferred_element_type=jnp.float32)  11.1 us
    pallas_call x1, Pallas kernels, run_expert(): pl.pallas_call(expert_kernel, grid=(steps,), in_specs=[pl.BlockSpec((coun...  10.5 us
    ppermute x3, starting transfers between devices, on_device(): neighbours.append(lax.ppermute(packed, 'x', backward))  10.2 us
  transfers between devices with their start and end apart: 10, of which 8 were waited for; matrix products, arithmetic and copies ran while one was open for 4% of the time, Pallas kernels for 1%

profile of v6, /device:TPU:8, one launch (start us, length us, event | category | flops | bytes accessed | tf_op | source)
XLA Modules:
  0.0 253.0 jit_solution(12035036425999478331)
XLA Ops:
  8.0 0.0 reduce-scatter.2.cloned.1.call-start
  8.0 0.0 copy-start
  8.1 1.0 copy-done
  9.1 1.0 copy-done.2
  10.1 0.9 copy-done.5
  11.0 0.9 copy-done.7
  11.9 0.5 shard_map.111
  12.4 1.9 collective-permute-start
  14.4 2.4 collective-permute-start.1
  16.8 1.1 collective-permute-done.1.there_ref
  17.9 0.0 collective-permute-done.got_ref
  17.9 2.1 shard_map.112
  20.0 0.0 reduce-scatter.2.cloned.1.call-update
  20.0 0.0 all-gather.3.cloned.1.call-start
  20.1 0.1 slice_bitcast_fusion.1
  20.2 0.0 copy-start.11
  20.2 1.7 fusion.2
  21.9 0.0 copy-start.12
  22.0 4.7 %collective-permute-start.2 = (bf16[16,4608]{1,0:T(8,128)(2,1)S(1)}, bf16[16,4608]{1,0:T(8,128)(2,1)S(1)}, u32[]{:S(2)}, u32[]{:S(2)}) collective-permute-start(bf16[16,4608]{1,0:T(8,128)(2,1)S(1)} %fusion.28.refs_0_), channel_id=1, source_target_pairs={{0,48},{16,0},{32,16},{48,32},{1,49},{17,1},{33,17},{49,33},{2,50}... | collective-permute-start | bytes 442376 | tf_op jit(solution)/shard_map/ppermute | solution.py:297
  26.6 2.7 %collective-permute-start.3 = (bf16[16,4608]{1,0:T(8,128)(2,1)S(1)}, bf16[16,4608]{1,0:T(8,128)(2,1)S(1)}, u32[]{:S(2)}, u32[]{:S(2)}) collective-permute-start(bf16[16,4608]{1,0:T(8,128)(2,1)S(1)} %fusion.28.refs_0_), channel_id=1, source_target_pairs={{0,32},{16,48},{32,0},{48,16},{1,33},{17,49},{33,1},{49,17},{2,34}... | collective-permute-start | bytes 442376 | tf_op jit(solution)/shard_map/ppermute | solution.py:297
  29.4 2.8 %collective-permute-start.4 = (bf16[16,4608]{1,0:T(8,128)(2,1)S(1)}, bf16[16,4608]{1,0:T(8,128)(2,1)S(1)}, u32[]{:S(2)}, u32[]{:S(2)}) collective-permute-start(bf16[16,4608]{1,0:T(8,128)(2,1)S(1)} %fusion.28.refs_0_), channel_id=1, source_target_pairs={{0,16},{16,32},{32,48},{48,0},{1,17},{17,33},{33,49},{49,1},{2,18}... | collective-permute-start | bytes 442376 | tf_op jit(solution)/shard_map/ppermute | solution.py:297
  32.2 1.3 collective-permute-done.2.refs_1_
  33.5 3.3 %collective-permute-done.3.refs_2_ = bf16[16,4608]{1,0:T(8,128)(2,1)S(1)} collective-permute-done((bf16[16,4608]{1,0:T(8,128)(2,1)S(1)}, bf16[16,4608]{1,0:T(8,128)(2,1)S(1)}, u32[]{:S(2)}, u32[]{:S(2)}) %collective-permute-start.3) | collective-permute-done | bytes 147488 | tf_op jit(solution)/shard_map/ppermute | solution.py:297
  36.8 2.3 collective-permute-done.4.refs_3_
  39.0 0.9 shard_map.114
  39.9 0.0 all-gather.3.cloned.1.call-update
  39.9 0.1 copy.30
  40.0 0.1 eq.67
  40.2 0.1 eq.71
  40.3 1.2 reduce-window.6
  41.4 0.2 slice_reduce_fusion
  41.7 0.1 fusion.22
  41.8 0.1 reduce_sum.34
  41.9 0.1 copy.33
  42.0 0.2 fusion.10
  42.2 0.2 select_reduce_fusion.1
  42.4 0.1 broadcast_in_dim.42.gate_ref
  42.6 27.8 %reduce-scatter.2.cloned.1.call-done.latents_ref = bf16[128,1024]{1,0:T(8,128)(2,1)} async-done(((bf16[1024,1024]{1,0:T(8,128)(2,1)}), bf16[128,1024]{1,0:T(8,128)(2,1)}) %reduce-scatter.2.cloned.1.call-update) | async-done | bytes 262160 | tf_op jit(solution)/shard_map/reduce_scatter | solution.py:290
  70.4 0.9 copy-done.4
  71.4 0.5 shard_map.113
  71.9 37.8 %all_to_all.20 = bf16[16,40,1024]{2,1,0:T(8,128)(2,1)S(1)} all-to-all(bf16[16,40,1024]{2,1,0:T(8,128)(2,1)S(1)} %bitcast.47), channel_id=1, replica_groups=mesh['y'=8,'x'=4,'z'=8,'c'=2] {'z','c'}, dimensions={0} | all-to-all | bytes 2621440 | tf_op jit(solution)/shard_map/all_to_all | solution.py:304
  109.7 10.5 %shard_map.115 = bf16[640,1024]{1,0:T(8,128)(2,1)} custom-call(bf16[640,1024]{1,0:T(8,128)(2,1)S(1)} %bitcast.48, bf16[512,4608]{1,0:T(8,128)(2,1)} %all-gather.3.cloned.1.call-done.gate_ref.up_ref.out_ref, bf16[512,4608]{1,0:T(8,128)(2,1)} %all-gather.3.cloned.1.call-done.gate_ref.up_ref.out_ref, ...), custom_call_target="tpu_custom_call" | custom-call | flops 6039797760 | bytes 7340032 | tf_op jit(solution)/shard_map/pallas_call | solution.py:96
  120.2 3.7 %all-to-all-start.1 = ((bf16[16,40,1024]{2,1,0:T(8,128)(2,1)}), bf16[16,40,1024]{2,1,0:T(8,128)(2,1)S(1)}, u32[]{:S(2)}, u32[]{:S(2)}) async-start(bf16[16,40,1024]{2,1,0:T(8,128)(2,1)} %bitcast.15), calls=%async_computation.2 | async-start | bytes 2621440 | tf_op jit(solution)/shard_map/all_to_all | solution.py:304
  123.9 0.0 all-gather.5.cloned.1.call-start
  124.0 0.2 fusion.9
  124.2 0.0 copy-start.1
  124.2 0.2 select_reduce_fusion
  124.5 31.7 %all-to-all-done.1 = bf16[16,40,1024]{2,1,0:T(8,128)(2,1)S(1)} async-done(((bf16[16,40,1024]{2,1,0:T(8,128)(2,1)}), bf16[16,40,1024]{2,1,0:T(8,128)(2,1)S(1)}, u32[]{:S(2)}, u32[]{:S(2)}) %all-to-all-start.1) | async-done | bytes 1310752 | tf_op jit(solution)/shard_map/all_to_all | solution.py:304
  156.2 1.2 shard_map.116
  157.4 0.0 all-gather.5.cloned.1.call-update
  157.4 0.0 copy-start.3
  157.4 44.3 %all-gather.5.cloned.1.call-done = bf16[2048,1024]{1,0:T(8,128)(2,1)} async-done(((bf16[128,1024]{1,0:T(8,128)(2,1)}), bf16[2048,1024]{1,0:T(8,128)(2,1)}) %all-gather.5.cloned.1.call-update) | async-done | bytes 4194320 | tf_op jit(solution)/shard_map/all_gather | solution.py:316
  201.7 0.0 copy-done.1
  201.8 2.5 fusion.14
  204.3 0.3 copy-done.13
  204.6 0.8 fusion.11
  205.3 0.0 copy-start.6
  205.4 22.4 %all_to_all.21.pieces_ref = bf16[32,16,256]{2,1,0:T(8,128)(2,1)S(1)} all-to-all(bf16[32,16,256]{2,1,0:T(8,128)(2,1)S(1)} %pad_maximum_fusion.1), channel_id=1, replica_groups=mesh['y'=8,'x'=4,'z'=8,'c'=2] {'y','x'}, dimensions={0} | all-to-all | bytes 524288 | tf_op jit(solution)/shard_map/all_to_all | solution.py:323
  227.8 0.8 shard_map.117
  228.5 4.7 %all-to-all-start.3 = ((bf16[32,16,256]{2,1,0:T(8,128)(2,1)}), bf16[32,16,256]{2,1,0:T(8,128)(2,1)S(1)}, u32[]{:S(2)}, u32[]{:S(2)}) async-start(bf16[32,16,256]{2,1,0:T(8,128)(2,1)} %shard_map.117), calls=%async_computation.4 | async-start | bytes 524288 | tf_op jit(solution)/shard_map/all_to_all | solution.py:327
  233.3 3.1 %convolution_convert_fusion.1 = bf16[2048,128]{1,0:T(8,128)(2,1)} fusion(bf16[512,128]{1,0:T(8,128)(2,1)S(1)} %copy-done.6, bf16[2048,1024]{1,0:T(8,128)(2,1)} %all-gather.5.cloned.1.call-done), kind=kOutput, calls=%fused_computation.4 | convolution fusion | flops 268697600 | bytes 2752512 | tf_op jit(solution)/shard_map/dot_general | solution.py:23
  236.4 3.1 %convolution_convert_fusion = bf16[2048,128]{1,0:T(8,128)(2,1)} fusion(bf16[128,512]{1,0:T(8,128)(2,1)S(1)} %copy-done.8, bf16[2048,1024]{1,0:T(8,128)(2,1)} %all-gather.5.cloned.1.call-done), kind=kOutput, calls=%fused_computation.3 | convolution fusion | flops 268697600 | bytes 2752512 | tf_op jit(solution)/shard_map/dot_general | solution.py:23
  239.5 5.3 %all-to-all-done.3 = bf16[32,16,256]{2,1,0:T(8,128)(2,1)S(1)} async-done(((bf16[32,16,256]{2,1,0:T(8,128)(2,1)}), bf16[32,16,256]{2,1,0:T(8,128)(2,1)S(1)}, u32[]{:S(2)}, u32[]{:S(2)}) %all-to-all-start.3) | async-done | bytes 262176 | tf_op jit(solution)/shard_map/all_to_all | solution.py:327
  244.8 0.8 shard_map.118
  (31 shorter events, 0.3 us)
Async XLA Ops:
  8.0 62.4 %reduce-scatter.2.cloned.1.call-start = ((), (), s32[]{:S(2)}) async-start(), calls=%async_computation.5 | async-start | bytes 2359296 | tf_op jit(solution)/shard_map/reduce_scatter | solution.py:290
  8.0 1.0 copy-start
  9.1 1.0 copy-start.2
  10.1 0.9 copy-start.5
  11.0 0.9 copy-start.7
  12.4 5.5 %collective-permute-start = (bf16[8,128,256]{2,1,0:T(8,128)(2,1)S(1)}, bf16[8,128,256]{2,1,0:T(8,128)(2,1)S(1)}, u32[]{:S(2)}, u32[]{:S(2)}) collective-permute-start(bf16[8,128,256]{2,1,0:T(8,128)(2,1)S(1)} %get-tuple-element.10), channel_id=1, source_target_pairs={{0,1},{1,0},{2,3},{3,2},{4,5},{5,4},{6,7},{7,6},{8,9},{9,8},{10,11... | collective-permute-start | bytes 1572872 | tf_op jit(solution)/shard_map/ppermute | solution.py:288
  14.4 3.6 %collective-permute-start.1 = (bf16[128,1024]{1,0:T(8,128)(2,1)S(1)}, bf16[128,1024]{1,0:T(8,128)(2,1)S(1)}, u32[]{:S(2)}, u32[]{:S(2)}) collective-permute-start(bf16[128,1024]{1,0:T(8,128)(2,1)S(1)} %get-tuple-element.11.here_ref), channel_id=1, source_target_pairs={{0,1},{1,0},{2,3},{3,2},{4,5},{5,4},{6,7},{7,6},{8,9},{9,8},{10,11... | collective-permute-start | bytes 786440 | tf_op jit(solution)/shard_map/ppermute | solution.py:288
  17.9 2.2 copy-start.10
  20.0 1.9 copy-start.9
  20.0 89.6 %all-gather.3.cloned.1.call-start = ((), (), s32[]{:S(2)}) async-start(), calls=%async_computation.6 | async-start | bytes 5308416 | tf_op jit(solution)/shard_map/all_gather | solution.py:299
  20.2 19.7 %copy-start.11 = (s32[128,4]{0,1:T(4,128)S(1)}, s32[128,4]{0,1:T(4,128)}, u32[]{:S(2)}) copy-start(s32[128,4]{0,1:T(4,128)} %param.12) | copy-start | bytes 6148
  21.9 20.3 %copy-start.12 = (f32[128,4]{0,1:T(4,128)S(1)}, f32[128,4]{0,1:T(4,128)}, u32[]{:S(2)}) copy-start(f32[128,4]{0,1:T(4,128)} %param.13) | copy-start | bytes 6148
  22.0 11.5 %collective-permute-start.2 = (bf16[16,4608]{1,0:T(8,128)(2,1)S(1)}, bf16[16,4608]{1,0:T(8,128)(2,1)S(1)}, u32[]{:S(2)}, u32[]{:S(2)}) collective-permute-start(bf16[16,4608]{1,0:T(8,128)(2,1)S(1)} %fusion.28.refs_0_), channel_id=1, source_target_pairs={{0,48},{16,0},{32,16},{48,32},{1,49},{17,1},{33,17},{49,33},{2,50}... | collective-permute-start | bytes 442376 | tf_op jit(solution)/shard_map/ppermute | solution.py:297
  26.6 10.1 %collective-permute-start.3 = (bf16[16,4608]{1,0:T(8,128)(2,1)S(1)}, bf16[16,4608]{1,0:T(8,128)(2,1)S(1)}, u32[]{:S(2)}, u32[]{:S(2)}) collective-permute-start(bf16[16,4608]{1,0:T(8,128)(2,1)S(1)} %fusion.28.refs_0_), channel_id=1, source_target_pairs={{0,32},{16,48},{32,0},{48,16},{1,33},{17,49},{33,1},{49,17},{2,34}... | collective-permute-start | bytes 442376 | tf_op jit(solution)/shard_map/ppermute | solution.py:297
  29.4 9.7 %collective-permute-start.4 = (bf16[16,4608]{1,0:T(8,128)(2,1)S(1)}, bf16[16,4608]{1,0:T(8,128)(2,1)S(1)}, u32[]{:S(2)}, u32[]{:S(2)}) collective-permute-start(bf16[16,4608]{1,0:T(8,128)(2,1)S(1)} %fusion.28.refs_0_), channel_id=1, source_target_pairs={{0,16},{16,32},{32,48},{48,0},{1,17},{17,33},{33,49},{49,1},{2,18}... | collective-permute-start | bytes 442376 | tf_op jit(solution)/shard_map/ppermute | solution.py:297
  70.4 1.0 copy-start.4
  120.2 36.0 %all-to-all-start.1 = ((bf16[16,40,1024]{2,1,0:T(8,128)(2,1)}), bf16[16,40,1024]{2,1,0:T(8,128)(2,1)S(1)}, u32[]{:S(2)}, u32[]{:S(2)}) async-start(bf16[16,40,1024]{2,1,0:T(8,128)(2,1)} %bitcast.15), calls=%async_computation.2 | async-start | bytes 2621440 | tf_op jit(solution)/shard_map/all_to_all | solution.py:304
  123.9 77.8 %all-gather.5.cloned.1.call-start = ((), (), s32[]{:S(2)}) async-start(), calls=%async_computation.7 | async-start | bytes 4456448 | tf_op jit(solution)/shard_map/all_gather | solution.py:316
  124.2 77.5 %copy-start.1 = (bf16[2048,128]{1,0:T(8,128)(2,1)S(1)}, bf16[2048,128]{1,0:T(8,128)(2,1)}, u32[]{:S(2)}) copy-start(bf16[2048,128]{1,0:T(8,128)(2,1)} %param.8) | copy-start | bytes 1572868
  157.4 46.9 %copy-start.3 = (bf16[2048,128]{1,0:T(8,128)(2,1)S(1)}, bf16[2048,128]{1,0:T(8,128)(2,1)}, u32[]{:S(2)}) copy-start(bf16[2048,128]{1,0:T(8,128)(2,1)} %param.9) | copy-start | bytes 1572868
  201.8 2.8 %copy-start.13 = (bf16[2048,1024]{1,0:T(8,128)(2,1)S(1)}, bf16[2048,1024]{1,0:T(8,128)(2,1)}, u32[]{:S(2)}) copy-start(bf16[2048,1024]{1,0:T(8,128)(2,1)} %all-gather.5.cloned.1.call-done) | copy-start | bytes 12582916
  205.3 27.9 %copy-start.6 = (bf16[512,128]{1,0:T(8,128)(2,1)S(1)}, bf16[512,128]{1,0:T(8,128)(2,1)}, u32[]{:S(2)}) copy-start(bf16[512,128]{1,0:T(8,128)(2,1)} %up_ref.1) | copy-start | bytes 393220
  228.5 7.9 %copy-start.8 = (bf16[128,512]{1,0:T(8,128)(2,1)S(1)}, bf16[128,512]{1,0:T(8,128)(2,1)}, u32[]{:S(2)}) copy-start(bf16[128,512]{1,0:T(8,128)(2,1)} %down_ref.1) | copy-start | bytes 393220
  228.5 16.3 %all-to-all-start.3 = ((bf16[32,16,256]{2,1,0:T(8,128)(2,1)}), bf16[32,16,256]{2,1,0:T(8,128)(2,1)S(1)}, u32[]{:S(2)}, u32[]{:S(2)}) async-start(bf16[32,16,256]{2,1,0:T(8,128)(2,1)} %shard_map.117), calls=%async_computation.4 | async-start | bytes 524288 | tf_op jit(solution)/shard_map/all_to_all | solution.py:327
Sparse Core Ops, SparseCore 0:
  20.2 50.2 reduce-scatter.1
  157.5 44.1 all-gather.4
Sparse Core Ops, SparseCore 1:
  40.0 63.1 all-gather.2

commit v7 on v6

--- a/solution.py
+++ b/solution.py
@@ -11,7 +11,7 @@
 
 TOPK = 4
 CORES = 2
-CHUNK = 256
+CHUNK = 512
 ACROSS = 4
 SMALL = pltpu.CompilerParams(vmem_limit_bytes=16 * 1024 * 1024)
 INNER = (((1,), (0,)), ((), ()))
@@ -115,68 +115,75 @@
 
 
 def swap_kernel(
-    core_ref, tokens_ref, cotangent_ref, down_ref, up_ref, rows_ref, kept_ref, weights_ref, up_here, sems
+    core_ref, tokens_ref, cotangent_ref, down_ref, up_ref, given_ref, kept_ref, sems
 ):
     mine = core_ref[0]
-    features = tokens_ref.shape[3]
+    chips, _, _, features = tokens_ref.shape
     latent_width = down_ref.shape[1]
     first, second = pl.ds(0, features), pl.ds(features, features)
+    rows = pl.ds(0, chips)
     moves = [
-        (up_ref, up_here),
-        (tokens_ref.at[:, 1 - mine], rows_ref.at[:, :, first]),
-        (cotangent_ref.at[:, 1 - mine], rows_ref.at[:, :, second]),
-        (down_ref, weights_ref.at[:, pl.ds(0, latent_width)]),
-        (tokens_ref.at[:, mine], kept_ref.at[:, :, first]),
-        (cotangent_ref.at[:, mine], kept_ref.at[:, :, second]),
+        (tokens_ref.at[:, 1 - mine], given_ref.at[rows, :, first]),
+        (cotangent_ref.at[:, 1 - mine], given_ref.at[rows, :, second]),
+        (tokens_ref.at[:, mine], kept_ref.at[rows, :, first]),
+        (cotangent_ref.at[:, mine], kept_ref.at[rows, :, second]),
     ]
     copies = [pltpu.make_async_copy(*move, sems.at[i]) for i, move in enumerate(moves)]
     for copy in copies:
         copy.start()
-    copies[0].wait()
-    weights_ref[:, latent_width:] = up_here[...].T
-    for copy in copies[1:]:
+    width = 2 * features
+    down, up = down_ref[...], up_ref[...].T
+    for block in range(latent_width // width):
+        here = slice(block * width, (block + 1) * width)
+        there = latent_width // width + block
+        for result_ref in (given_ref, kept_ref):
+            result_ref[chips + block] = down[:, here]
+            result_ref[chips + there] = up[:, here]
+    for copy in copies:
         copy.wait()
 
 
 def swap_operands(core, tokens, cotangent, down_proj, up_proj):
     chips, _, tok_rows, features = tokens.shape
-    latent_width = down_proj.shape[1]
-    rows = jax.ShapeDtypeStruct((chips, tok_rows, 2 * features), jnp.bfloat16)
+    blocks = chips + 2 * (down_proj.shape[1] // (2 * features))
+    rows = jax.ShapeDtypeStruct((blocks, tok_rows, 2 * features), jnp.bfloat16)
     return pl.pallas_call(
         swap_kernel,
         in_specs=[pl.BlockSpec(memory_space=pltpu.SMEM)]
-        + [pl.BlockSpec(memory_space=pltpu.HBM)] * 4,
-        out_specs=[pl.BlockSpec(memory_space=pltpu.VMEM)] * 3,
-        out_shape=[rows, rows, jax.ShapeDtypeStruct((features, 2 * latent_width), jnp.bfloat16)],
-        scratch_shapes=[
-            pltpu.VMEM((latent_width, features), jnp.bfloat16),
-            pltpu.SemaphoreType.DMA((6,)),
-        ],
+        + [pl.BlockSpec(memory_space=pl.ANY)] * 2
+        + [pl.BlockSpec(memory_space=pltpu.VMEM)] * 2,
+        out_specs=[pl.BlockSpec(memory_space=pltpu.VMEM)] * 2,
+        out_shape=[rows, rows],
+        scratch_shapes=[pltpu.SemaphoreType.DMA((4,))],
         compiler_params=SMALL,
     )(core, tokens, cotangent, down_proj, up_proj)
 
 
-def latent_kernel(kept_ref, got_ref, here_ref, there_ref, result_ref):
-    count = result_ref.shape[0]
-    latent_width = here_ref.shape[1] // 2
+def latent_kernel(kept_ref, got_ref, result_ref):
     features = kept_ref.shape[2] // 2
-    kept = kept_ref[...].reshape(count, 2 * features)
-    got = got_ref[...].reshape(count, 2 * features)
+    count, width = result_ref.shape
+    latent_width = width // 2
+    chips = count // kept_ref.shape[1]
+    blocks = latent_width // (2 * features)
+    kept = kept_ref[:chips].reshape(count, 2 * features)
+    got = got_ref[:chips].reshape(count, 2 * features)
     for half in range(2):
         rows = slice(half * features, (half + 1) * features)
-        here = slice(half * latent_width, (half + 1) * latent_width)
         left = jnp.concatenate([kept[:, rows], got[:, rows]], axis=1)
-        right = jnp.concatenate([here_ref[:, here], there_ref[:, here]], axis=0)
-        result_ref[:, here] = dot(left, right).astype(jnp.bfloat16)
-
-
-def chip_latents(kept, got, here, there):
-    count = kept.shape[0] * kept.shape[1]
+        for block in range(blocks):
+            place = chips + half * blocks + block
+            right = jnp.concatenate([kept_ref[place], got_ref[place]], axis=0)
+            start = half * latent_width + block * 2 * features
+            result_ref[:, start : start + 2 * features] = dot(left, right).astype(jnp.bfloat16)
+
+
+def chip_latents(kept, got, chips, latent_width):
+    count = chips * kept.shape[1]
     return pl.pallas_call(
         latent_kernel,
-        out_shape=jax.ShapeDtypeStruct((count, here.shape[1]), jnp.bfloat16),
-        compiler_params=SMALL,
-    )(kept, got, here, there)
+        out_shape=jax.ShapeDtypeStruct((count, 2 * latent_width), jnp.bfloat16),
+        compiler_params=SMALL,
+    )(kept, got)
 
 
 def combine_kernel(returned_ref, gates_ref, spread_ref, result_ref):
@@ -282,11 +289,9 @@
     token_blocks = tokens.reshape(blocked)
     cotangent_blocks = cotangent.reshape(blocked)
     place = core.reshape(1).astype(jnp.int32)
-    given, kept, here = swap_operands(
-        place, token_blocks, cotangent_blocks, down_proj, up_proj
-    )
-    got, there = (lax.ppermute(array, "c", swap) for array in (given, here))
-    parts = chip_latents(kept, got, here, there)
+    given, kept = swap_operands(place, token_blocks, cotangent_blocks, down_proj, up_proj)
+    got = lax.ppermute(given, "c", swap)
+    parts = chip_latents(kept, got, chips, latent_width)
     latents = lax.psum_scatter(parts, "z", scatter_dimension=0, tiled=True)
 
     packed = packed_weights(expert_in, expert_out, dp)
@@ -298,7 +303,9 @@
     column = lax.axis_index("x").reshape(1).astype(jnp.int32)
     weights = lax.all_gather(arranged(column, neighbours), "y", axis=0, tiled=True)
 
-    to_slot, slot_gate, to_token, gates = slot_tables(routes, gate_weights, groups, capacity)
+    to_slot, slot_gate, to_token, gates = lax.optimization_barrier(
+        slot_tables(routes, gate_weights, groups, capacity)
+    )
 
     def exchange(rows):
         return lax.all_to_all(

time: 254 us -> 250 us (0.984)
  blocking collectives: 60.2 us -> 97.1 us
  waiting for transfers between devices: 117 us -> 84.5 us
  starting transfers between devices: 23.1 us -> 17 us
    all_to_all x1 -> x2, blocking collectives: 37.8 us -> 74.8 us  [exchange(): lax.all_to_all(rows.reshape(groups, capacity, rows.shape[1]), expert, spl...]
    all_to_all x1 -> x0, waiting for transfers between devices: 31.7 us -> none  [exchange(): lax.all_to_all(rows.reshape(groups, capacity, rows.shape[1]), expert, spl...]
    all_to_all x1 -> x0, starting transfers between devices: 3.7 us -> none  [exchange(): lax.all_to_all(rows.reshape(groups, capacity, rows.shape[1]), expert, spl...]
  transfers between devices with their start and end apart: 10 -> 8, of which waited for: 8 -> 7; matrix products, arithmetic and copies ran while one was open for 4% -> 4% of each run, Pallas kernels for 1% -> 1%
where the time goes in v7:
time: 250 us
  blocking collectives  97.1 us (39%)
  waiting for transfers between devices  84.5 us (34%)
  starting transfers between devices  17 us (7%)
  between operations  15.8 us (6%)
  Pallas kernels  15.7 us (6%)
  matrix products  11.1 us (4%)
  local copies, waits for them, and re-layouts  6.19 us (2%)
    all_to_all x2, blocking collectives, exchange(): lax.all_to_all(rows.reshape(groups, capacity, rows.shape[1]), expert, spl...  74.8 us
    all_gather x1, waiting for transfers between devices, on_device(): latents = lax.all_gather(latents, expert, axis=0, tiled=True)  43.1 us
    reduce_scatter x1, waiting for transfers between devices, on_device(): latents = lax.psum_scatter(parts, 'z', scatter_dimension=0, tiled=True)  27.1 us
    all_to_all x1, blocking collectives, on_device(): lax.all_to_all(grads, dp_axes, split_axis=0, concat_axis=0, tiled=True)  22.4 us
    dot_general x5, matrix products, dot(): lax.dot_general(left, right, dims, preferred_element_type=jnp.float32)  11.1 us
    ppermute x3, starting transfers between devices, on_device(): neighbours.append(lax.ppermute(packed, 'x', backward))  10.2 us
    pallas_call x1, Pallas kernels, run_expert(): pl.pallas_call(expert_kernel, grid=(steps,), in_specs=[pl.BlockSpec((coun...  9.19 us
    ppermute x3, waiting for transfers between devices, on_device(): neighbours.append(lax.ppermute(packed, 'x', backward))  6.7 us
  transfers between devices with their start and end apart: 8, of which 7 were waited for; matrix products, arithmetic and copies ran while one was open for 4% of the time, Pallas kernels for 1%

profile of v7, /device:TPU:8, one launch (start us, length us, event | category | flops | bytes accessed | tf_op | source)
XLA Modules:
  0.0 249.7 jit_solution(7378841194438877102)
XLA Ops:
  8.0 0.0 reduce-scatter.2.cloned.1.call-start
  8.0 0.0 copy-start
  8.1 1.0 copy-done
  9.1 1.0 copy-done.2
  10.1 0.9 copy-done.5
  11.0 0.9 copy-done.7
  11.9 0.3 shard_map.111
  12.3 1.9 collective-permute-start
  14.2 2.3 collective-permute-done.got_ref
  16.4 2.1 shard_map.112
  18.5 0.0 reduce-scatter.2.cloned.1.call-update
  18.6 0.0 all-gather.3.cloned.1.call-start
  18.6 0.0 copy-done.10
  18.6 0.1 slice_bitcast_fusion.1
  18.7 0.0 copy-start.11
  18.7 1.7 fusion.2
  20.4 0.0 copy-start.12
  20.4 0.0 copy-done.9
  20.5 4.7 %collective-permute-start.1 = (bf16[16,4608]{1,0:T(8,128)(2,1)S(1)}, bf16[16,4608]{1,0:T(8,128)(2,1)S(1)}, u32[]{:S(2)}, u32[]{:S(2)}) collective-permute-start(bf16[16,4608]{1,0:T(8,128)(2,1)S(1)} %fusion.28.refs_0_), channel_id=1, source_target_pairs={{0,48},{16,0},{32,16},{48,32},{1,49},{17,1},{33,17},{49,33},{2,50}... | collective-permute-start | bytes 442376 | tf_op jit(solution)/shard_map/ppermute | solution.py:302
  25.2 2.7 %collective-permute-start.2 = (bf16[16,4608]{1,0:T(8,128)(2,1)S(1)}, bf16[16,4608]{1,0:T(8,128)(2,1)S(1)}, u32[]{:S(2)}, u32[]{:S(2)}) collective-permute-start(bf16[16,4608]{1,0:T(8,128)(2,1)S(1)} %fusion.28.refs_0_), channel_id=1, source_target_pairs={{0,32},{16,48},{32,0},{48,16},{1,33},{17,49},{33,1},{49,17},{2,34}... | collective-permute-start | bytes 442376 | tf_op jit(solution)/shard_map/ppermute | solution.py:302
  27.9 2.8 %collective-permute-start.3 = (bf16[16,4608]{1,0:T(8,128)(2,1)S(1)}, bf16[16,4608]{1,0:T(8,128)(2,1)S(1)}, u32[]{:S(2)}, u32[]{:S(2)}) collective-permute-start(bf16[16,4608]{1,0:T(8,128)(2,1)S(1)} %fusion.28.refs_0_), channel_id=1, source_target_pairs={{0,16},{16,32},{32,48},{48,0},{1,17},{17,33},{33,49},{49,1},{2,18}... | collective-permute-start | bytes 442376 | tf_op jit(solution)/shard_map/ppermute | solution.py:302
  30.7 1.1 collective-permute-done.1.refs_1_
  31.7 3.6 %collective-permute-done.2.refs_2_ = bf16[16,4608]{1,0:T(8,128)(2,1)S(1)} collective-permute-done((bf16[16,4608]{1,0:T(8,128)(2,1)S(1)}, bf16[16,4608]{1,0:T(8,128)(2,1)S(1)}, u32[]{:S(2)}, u32[]{:S(2)}) %collective-permute-start.2) | collective-permute-done | bytes 147488 | tf_op jit(solution)/shard_map/ppermute | solution.py:302
  35.3 2.1 collective-permute-done.3.refs_3_
  37.4 0.9 shard_map.114
  38.2 0.0 all-gather.3.cloned.1.call-update
  38.3 0.0 all-gather.5.cloned.1.call-start
  38.3 0.0 copy-done.11
  38.3 0.1 copy.30
  38.4 0.1 eq.71
  38.6 0.1 eq.67
  38.7 1.2 reduce-window.6
  39.8 0.2 slice_reduce_fusion
  40.1 0.1 fusion.22
  40.2 0.1 reduce_sum.34
  40.3 0.1 copy.33
  40.4 0.2 fusion.10
  40.6 0.2 select_reduce_fusion.1
  40.8 0.2 fusion.9
  41.1 0.2 select_reduce_fusion
  41.4 0.2 copy.34.gate_ref
  41.6 27.1 %reduce-scatter.2.cloned.1.call-done.latents_ref = bf16[128,1024]{1,0:T(8,128)(2,1)} async-done(((bf16[1024,1024]{1,0:T(8,128)(2,1)}), bf16[128,1024]{1,0:T(8,128)(2,1)}) %reduce-scatter.2.cloned.1.call-update) | async-done | bytes 262160 | tf_op jit(solution)/shard_map/reduce_scatter | solution.py:295
  68.7 1.0 copy-done.4
  69.6 0.5 shard_map.113
  70.1 37.8 %all_to_all.20 = bf16[16,40,1024]{2,1,0:T(8,128)(2,1)S(1)} all-to-all(bf16[16,40,1024]{2,1,0:T(8,128)(2,1)S(1)} %bitcast.46), channel_id=1, replica_groups=mesh['y'=8,'x'=4,'z'=8,'c'=2] {'z','c'}, dimensions={0} | all-to-all | bytes 2621440 | tf_op jit(solution)/shard_map/all_to_all | solution.py:311
  107.9 9.2 %shard_map.115 = bf16[640,1024]{1,0:T(8,128)(2,1)S(1)} custom-call(bf16[640,1024]{1,0:T(8,128)(2,1)S(1)} %bitcast.48, bf16[512,4608]{1,0:T(8,128)(2,1)} %all-gather.3.cloned.1.call-done.gate_ref.up_ref.out_ref, bf16[512,4608]{1,0:T(8,128)(2,1)} %all-gather.3.cloned.1.call-done.gate_ref.up_ref.out_ref, ...), custom_call_target="tpu_custom_call" | custom-call | flops 6039797760 | bytes 7340032 | tf_op jit(solution)/shard_map/pallas_call | solution.py:96
  117.1 0.0 copy-start.1
  117.1 37.0 %all_to_all.21 = bf16[16,40,1024]{2,1,0:T(8,128)(2,1)S(1)} all-to-all(bf16[16,40,1024]{2,1,0:T(8,128)(2,1)S(1)} %bitcast.49), channel_id=1, replica_groups=mesh['y'=8,'x'=4,'z'=8,'c'=2] {'z','c'}, dimensions={0} | all-to-all | bytes 2621440 | tf_op jit(solution)/shard_map/all_to_all | solution.py:311
  154.1 1.2 shard_map.116
  155.3 0.0 all-gather.5.cloned.1.call-update
  155.3 0.0 copy-start.3
  155.3 43.1 %all-gather.5.cloned.1.call-done = bf16[2048,1024]{1,0:T(8,128)(2,1)} async-done(((bf16[128,1024]{1,0:T(8,128)(2,1)}), bf16[2048,1024]{1,0:T(8,128)(2,1)}) %all-gather.5.cloned.1.call-update) | async-done | bytes 4194320 | tf_op jit(solution)/shard_map/all_gather | solution.py:323
  198.4 2.5 %fusion.11 = bf16[512,128]{1,0:T(8,128)(2,1)S(1)} fusion(bf16[2048,128]{1,0:T(8,128)(2,1)S(1)} %copy-done.1, bf16[2048,1024]{1,0:T(8,128)(2,1)} %all-gather.5.cloned.1.call-done), kind=kOutput, calls=%fused_computation.18 | convolution fusion | flops 268500992 | bytes 2752512 | tf_op jit(solution)/shard_map/dot_general | solution.py:23
  200.9 0.0 copy-done.3
  200.9 0.3 copy-done.13
  201.2 0.8 fusion.14
  202.0 0.0 copy-start.6
  202.1 22.4 %all_to_all.22.pieces_ref = bf16[32,16,256]{2,1,0:T(8,128)(2,1)S(1)} all-to-all(bf16[32,16,256]{2,1,0:T(8,128)(2,1)S(1)} %pad_maximum_fusion.1), channel_id=1, replica_groups=mesh['y'=8,'x'=4,'z'=8,'c'=2] {'y','x'}, dimensions={0} | all-to-all | bytes 524288 | tf_op jit(solution)/shard_map/all_to_all | solution.py:330
  224.4 0.8 shard_map.117
  225.2 4.7 %all-to-all-start.3 = ((bf16[32,16,256]{2,1,0:T(8,128)(2,1)}), bf16[32,16,256]{2,1,0:T(8,128)(2,1)S(1)}, u32[]{:S(2)}, u32[]{:S(2)}) async-start(bf16[32,16,256]{2,1,0:T(8,128)(2,1)} %shard_map.117), calls=%async_computation.4 | async-start | bytes 524288 | tf_op jit(solution)/shard_map/all_to_all | solution.py:334
  229.9 3.1 %convolution_convert_fusion = bf16[2048,128]{1,0:T(8,128)(2,1)} fusion(bf16[128,512]{1,0:T(8,128)(2,1)S(1)} %copy-done.6, bf16[2048,1024]{1,0:T(8,128)(2,1)} %all-gather.5.cloned.1.call-done), kind=kOutput, calls=%fused_computation.3 | convolution fusion | flops 268697600 | bytes 2752512 | tf_op jit(solution)/shard_map/dot_general | solution.py:23
  233.0 3.1 %convolution_convert_fusion.1 = bf16[2048,128]{1,0:T(8,128)(2,1)} fusion(bf16[512,128]{1,0:T(8,128)(2,1)S(1)} %copy-done.8, bf16[2048,1024]{1,0:T(8,128)(2,1)} %all-gather.5.cloned.1.call-done), kind=kOutput, calls=%fused_computation.4 | convolution fusion | flops 268697600 | bytes 2752512 | tf_op jit(solution)/shard_map/dot_general | solution.py:23
  236.1 5.3 %all-to-all-done.3 = bf16[32,16,256]{2,1,0:T(8,128)(2,1)S(1)} async-done(((bf16[32,16,256]{2,1,0:T(8,128)(2,1)}), bf16[32,16,256]{2,1,0:T(8,128)(2,1)S(1)}, u32[]{:S(2)}, u32[]{:S(2)}) %all-to-all-start.3) | async-done | bytes 262176 | tf_op jit(solution)/shard_map/all_to_all | solution.py:334
  241.4 0.8 shard_map.118
  (29 shorter events, 0.3 us)
Async XLA Ops:
  8.0 60.7 %reduce-scatter.2.cloned.1.call-start = ((), (), s32[]{:S(2)}) async-start(), calls=%async_computation.5 | async-start | bytes 2359296 | tf_op jit(solution)/shard_map/reduce_scatter | solution.py:295
  8.0 1.0 copy-start
  9.1 1.0 copy-start.2
  10.1 0.9 copy-start.5
  11.0 0.9 copy-start.7
  12.3 4.2 %collective-permute-start = (bf16[12,128,256]{2,1,0:T(8,128)(2,1)S(1)}, bf16[12,128,256]{2,1,0:T(8,128)(2,1)S(1)}, u32[]{:S(2)}, u32[]{:S(2)}) collective-permute-start(bf16[12,128,256]{2,1,0:T(8,128)(2,1)S(1)} %get-tuple-element.13), channel_id=1, source_target_pairs={{0,1},{1,0},{2,3},{3,2},{4,5},{5,4},{6,7},{7,6},{8,9},{9,8},{10,11... | collective-permute-start | bytes 2359304 | tf_op jit(solution)/shard_map/ppermute | solution.py:293
  16.4 2.2 copy-start.10
  18.5 1.9 copy-start.9
  18.6 89.3 %all-gather.3.cloned.1.call-start = ((), (), s32[]{:S(2)}) async-start(), calls=%async_computation.6 | async-start | bytes 5308416 | tf_op jit(solution)/shard_map/all_gather | solution.py:304
  18.7 19.6 %copy-start.11 = (s32[128,4]{0,1:T(4,128)S(1)}, s32[128,4]{0,1:T(4,128)}, u32[]{:S(2)}) copy-start(s32[128,4]{0,1:T(4,128)} %param.12) | copy-start | bytes 6148
  20.4 20.2 %copy-start.12 = (f32[128,4]{0,1:T(4,128)S(1)}, f32[128,4]{0,1:T(4,128)}, u32[]{:S(2)}) copy-start(f32[128,4]{0,1:T(4,128)} %param.13) | copy-start | bytes 6148
  20.5 11.3 %collective-permute-start.1 = (bf16[16,4608]{1,0:T(8,128)(2,1)S(1)}, bf16[16,4608]{1,0:T(8,128)(2,1)S(1)}, u32[]{:S(2)}, u32[]{:S(2)}) collective-permute-start(bf16[16,4608]{1,0:T(8,128)(2,1)S(1)} %fusion.28.refs_0_), channel_id=1, source_target_pairs={{0,48},{16,0},{32,16},{48,32},{1,49},{17,1},{33,17},{49,33},{2,50}... | collective-permute-start | bytes 442376 | tf_op jit(solution)/shard_map/ppermute | solution.py:302
  25.2 10.1 %collective-permute-start.2 = (bf16[16,4608]{1,0:T(8,128)(2,1)S(1)}, bf16[16,4608]{1,0:T(8,128)(2,1)S(1)}, u32[]{:S(2)}, u32[]{:S(2)}) collective-permute-start(bf16[16,4608]{1,0:T(8,128)(2,1)S(1)} %fusion.28.refs_0_), channel_id=1, source_target_pairs={{0,32},{16,48},{32,0},{48,16},{1,33},{17,49},{33,1},{49,17},{2,34}... | collective-permute-start | bytes 442376 | tf_op jit(solution)/shard_map/ppermute | solution.py:302
  27.9 9.5 %collective-permute-start.3 = (bf16[16,4608]{1,0:T(8,128)(2,1)S(1)}, bf16[16,4608]{1,0:T(8,128)(2,1)S(1)}, u32[]{:S(2)}, u32[]{:S(2)}) collective-permute-start(bf16[16,4608]{1,0:T(8,128)(2,1)S(1)} %fusion.28.refs_0_), channel_id=1, source_target_pairs={{0,16},{16,32},{32,48},{48,0},{1,17},{17,33},{33,49},{49,1},{2,18}... | collective-permute-start | bytes 442376 | tf_op jit(solution)/shard_map/ppermute | solution.py:302
  38.3 160.1 %all-gather.5.cloned.1.call-start = ((), (), s32[]{:S(2)}) async-start(), calls=%async_computation.7 | async-start | bytes 4456448 | tf_op jit(solution)/shard_map/all_gather | solution.py:323
  68.7 1.0 copy-start.4
  117.1 81.3 %copy-start.1 = (bf16[2048,128]{1,0:T(8,128)(2,1)S(1)}, bf16[2048,128]{1,0:T(8,128)(2,1)}, u32[]{:S(2)}) copy-start(bf16[2048,128]{1,0:T(8,128)(2,1)} %param.9) | copy-start | bytes 1572868
  155.3 45.6 %copy-start.3 = (bf16[2048,128]{1,0:T(8,128)(2,1)S(1)}, bf16[2048,128]{1,0:T(8,128)(2,1)}, u32[]{:S(2)}) copy-start(bf16[2048,128]{1,0:T(8,128)(2,1)} %param.8) | copy-start | bytes 1572868
  198.4 2.8 %copy-start.13 = (bf16[2048,1024]{1,0:T(8,128)(2,1)S(1)}, bf16[2048,1024]{1,0:T(8,128)(2,1)}, u32[]{:S(2)}) copy-start(bf16[2048,1024]{1,0:T(8,128)(2,1)} %all-gather.5.cloned.1.call-done) | copy-start | bytes 12582916
  202.0 27.9 %copy-start.6 = (bf16[128,512]{1,0:T(8,128)(2,1)S(1)}, bf16[128,512]{1,0:T(8,128)(2,1)}, u32[]{:S(2)}) copy-start(bf16[128,512]{1,0:T(8,128)(2,1)} %down_ref.1) | copy-start | bytes 393220
  225.2 7.9 %copy-start.8 = (bf16[512,128]{1,0:T(8,128)(2,1)S(1)}, bf16[512,128]{1,0:T(8,128)(2,1)}, u32[]{:S(2)}) copy-start(bf16[512,128]{1,0:T(8,128)(2,1)} %up_ref.1) | copy-start | bytes 393220
  225.2 16.3 %all-to-all-start.3 = ((bf16[32,16,256]{2,1,0:T(8,128)(2,1)}), bf16[32,16,256]{2,1,0:T(8,128)(2,1)S(1)}, u32[]{:S(2)}, u32[]{:S(2)}) async-start(bf16[32,16,256]{2,1,0:T(8,128)(2,1)} %shard_map.117), calls=%async_computation.4 | async-start | bytes 524288 | tf_op jit(solution)/shard_map/all_to_all | solution.py:334
Sparse Core Ops, SparseCore 0:
  18.7 49.9 reduce-scatter.1
  155.4 42.9 all-gather.4
Sparse Core Ops, SparseCore 1:
  38.4 63.0 all-gather.2

commit v8 on v7

--- a/solution.py
+++ b/solution.py
@@ -14,6 +14,7 @@
 CHUNK = 512
 ACROSS = 4
 SMALL = pltpu.CompilerParams(vmem_limit_bytes=16 * 1024 * 1024)
+LARGE = pltpu.CompilerParams(vmem_limit_bytes=56 * 1024 * 1024)
 INNER = (((1,), (0,)), ((), ()))
 COLS = (((1,), (1,)), ((), ()))
 ROWS = (((0,), (0,)), ((), ()))
@@ -249,14 +250,100 @@
     )(place, *parts).reshape(-1, parts[0].shape[1])
 
 
+def grads_kernel(latents_ref, kept_ref, got_ref, mine_ref, other_ref):
+    count, width = latents_ref.shape
+    latent_width = width // 2
+    features = kept_ref.shape[2] // 2
+    chips = count // kept_ref.shape[1]
+    kept = kept_ref[:chips].reshape(count, 2 * features)
+    got = got_ref[:chips].reshape(count, 2 * features)
+    for half in range(2):
+        rows = slice((1 - half) * features, (2 - half) * features)
+        here = slice(half * features, (half + 1) * features)
+        latents = latents_ref[:, half * latent_width : (half + 1) * latent_width]
+        left = jnp.concatenate([kept[:, rows], got[:, rows]], axis=1)
+        grad = dot(left, latents, ROWS).astype(jnp.bfloat16)
+        mine_ref[here] = grad[:features]
+        other_ref[here] = grad[features:]
+
+
+def projection_grads(latents, kept, got):
+    out = jax.ShapeDtypeStruct((kept.shape[2], latents.shape[1] // 2), jnp.bfloat16)
+    return pl.pallas_call(
+        grads_kernel,
+        out_shape=[out] * 2,
+        compiler_params=LARGE,
+        cost_estimate=pl.CostEstimate(
+            flops=2 * latents.size * kept.shape[2],
+            bytes_accessed=2 * latents.size,
+            transcendentals=0,
+        ),
+    )(latents, kept, got)
+
+
+def outputs_kernel(latents_ref, kept_ref, got_ref, mine_ref, other_ref):
+    count, width = latents_ref.shape
+    latent_width = width // 2
+    features = kept_ref.shape[2] // 2
+    chips = count // kept_ref.shape[1]
+    blocks = latent_width // (2 * features)
+    for half in range(2):
+        here = slice(half * features, (half + 1) * features)
+        latents = latents_ref[:, half * latent_width : (half + 1) * latent_width]
+        first = chips + (1 - half) * blocks
+        right = [
+            jnp.concatenate([ref[first + block] for block in range(blocks)], axis=1)
+            for ref in (kept_ref, got_ref)
+        ]
+        product = dot(latents, jnp.concatenate(right, axis=0), COLS).astype(jnp.bfloat16)
+        mine_ref[:, here] = product[:, :features]
+        other_ref[:, here] = product[:, features:]
+
+
+def output_rows(latents, kept, got):
+    out = jax.ShapeDtypeStruct((latents.shape[0], kept.shape[2]), jnp.bfloat16)
+    return pl.pallas_call(
+        outputs_kernel,
+        out_shape=[out] * 2,
+        compiler_params=SMALL,
+        cost_estimate=pl.CostEstimate(
+            flops=2 * latents.size * kept.shape[2],
+            bytes_accessed=4 * latents.size,
+            transcendentals=0,
+        ),
+    )(latents, kept, got)
+
+
+def join_kernel(core_ref, mine_ref, got_ref, mixed_ref, input_ref):
+    chips, _, tok_rows, features = mixed_ref.shape
+    for ref, place in ((mine_ref, core_ref[0]), (got_ref, 1 - core_ref[0])):
+        rows = ref[...].reshape(chips, 1, tok_rows, 2 * features)
+        mixed_ref[:, pl.ds(place, 1)] = rows[..., :features]
+        input_ref[:, pl.ds(place, 1)] = rows[..., features:]
+
+
+def joined_rows(core, mine, got, blocked):
+    out = jax.ShapeDtypeStruct(blocked, jnp.bfloat16)
+    return pl.pallas_call(
+        join_kernel,
+        in_specs=[pl.BlockSpec(memory_space=pltpu.SMEM)]
+        + [pl.BlockSpec(memory_space=pltpu.VMEM)] * 2,
+        out_shape=[out] * 2,
+        compiler_params=SMALL,
+        cost_estimate=pl.CostEstimate(
+            flops=0, bytes_accessed=8 * mine.size, transcendentals=0
+        ),
+    )(core, mine, got)
+
+
 def unpack_kernel(scale, packed_ref, down_ref, up_ref):
     features = up_ref.shape[1]
-    up_ref[...] = packed_ref[:, :features].astype(jnp.float32) * scale
-    down_ref[...] = packed_ref[:, features:].astype(jnp.float32).T * scale
+    up_ref[...] = packed_ref[:features].astype(jnp.float32).T * scale
+    down_ref[...] = packed_ref[features:].astype(jnp.float32) * scale
 
 
 def unpack_grads(packed, scale):
-    latent_width, features = packed.shape[0], packed.shape[1] // 2
+    latent_width, features = packed.shape[1], packed.shape[0] // 2
     return pl.pallas_call(
         functools.partial(unpack_kernel, scale),
         out_shape=[
@@ -281,7 +368,6 @@
     capacity = min(tok_rows, tok_rows * TOPK * 5 // (4 * groups))
     slot_count = groups * capacity
     grad_scale = 1.0 / math.sqrt(group_rows * dp)
-    bf16 = jnp.bfloat16
 
     swap = [(0, 1), (1, 0)]
 
@@ -320,19 +406,19 @@
     result = run_expert(exchange(outgoing), weights)
     returned = exchange(result)
     latents = combined_latents(returned, gates, to_token)
-    latents = lax.all_gather(latents, expert, axis=0, tiled=True)
-    all_out = latents[:, :latent_width]
-    all_grad = latents[:, latent_width:]
-    up_part_grad = dot(all_out, cotangent, ROWS)
-    down_part_grad = dot(all_grad, tokens, ROWS)
-    grads = jnp.concatenate([up_part_grad, down_part_grad], axis=1).astype(bf16)
-    grads = grads.reshape(dp, latent_width // dp, 2 * features)
+    latents = lax.all_gather(latents, "z", axis=0, tiled=True)
+    grads, given_grads = projection_grads(latents, kept, got)
+    got_grads = lax.ppermute(given_grads, "c", swap)
+    outputs, given_outputs = output_rows(latents, kept, got)
+    grads = (grads.astype(jnp.float32) + got_grads.astype(jnp.float32)).astype(jnp.bfloat16)
+    grads = grads.reshape(dp, 2 * features // dp, latent_width)
     grads = lax.all_to_all(grads, dp_axes, split_axis=0, concat_axis=0, tiled=True)
-    mixed = dot(all_out, up_proj).astype(bf16)
-    input_grad = dot(all_grad, down_proj, COLS).astype(bf16)
+    got_outputs = lax.ppermute(given_outputs, "c", swap)
+    mixed, input_grad = joined_rows(place, outputs, got_outputs, blocked)
     summed = shared_sums(grads)
     summed = lax.all_to_all(summed, dp_axes, split_axis=0, concat_axis=0, tiled=True)
-    down_grad, up_grad = unpack_grads(summed.reshape(latent_width, 2 * features), grad_scale)
+    down_grad, up_grad = unpack_grads(summed.reshape(2 * features, latent_width), grad_scale)
+    mixed, input_grad = (rows.reshape(group_rows, features) for rows in (mixed, input_grad))
     return mixed, input_grad, down_grad, up_grad
 
 

time: 250 us -> 256 us (1.024)
  blocking collectives: 97.1 us -> 74.6 us
  starting transfers between devices: 17 us -> 30.8 us
  waiting for transfers between devices: 84.5 us -> 96.5 us
  matrix products: 11.1 us -> 1.66 us
  Pallas kernels: 15.7 us -> 21.9 us
  local copies, waits for them, and re-layouts: 6.19 us -> 9.52 us
    all_to_all x1 -> x0, blocking collectives: 22.4 us -> none  [on_device(): lax.all_to_all(grads, dp_axes, split_axis=0, concat_axis=0, tiled=True)]
    all_to_all x0 -> x1, starting transfers between devices: none -> 9.86 us  [on_device(): lax.all_to_all(grads, dp_axes, split_axis=0, concat_axis=0, tiled=True)]
    dot_general x5 -> x1, matrix products: 11.1 us -> 1.66 us  [dot(): lax.dot_general(left, right, dims, preferred_element_type=jnp.float32)]
    all_to_all x0 -> x1, waiting for transfers between devices: none -> 6.93 us  [on_device(): lax.all_to_all(grads, dp_axes, split_axis=0, concat_axis=0, tiled=True)]
    pallas_call x0 -> x3, Pallas kernels: none -> 6.31 us  [the longest x1 3.64 us: projection_grads(): pl.pallas_call(grads_kernel, out_shape=[out] * 2, compiler_params=LARGE,...]
    all_to_all x1, waiting for transfers between devices: 5.3 us -> 10.4 us  [on_device(): lax.all_to_all(summed, dp_axes, split_axis=0, concat_axis=0, tiled=True)]
    ppermute x0 -> x2, starting transfers between devices: none -> 4.08 us  [the longest x1 2.04 us: on_device(): got_grads = lax.ppermute(given_grads, 'c', swap)]
    unnamed x33 -> x37, local copies, waits for them, and re-layouts: 5.32 us -> 8.65 us
  transfers between devices with their start and end apart: 8 -> 11, of which waited for: 7 -> 9; matrix products, arithmetic and copies ran while one was open for 4% -> 2% of each run, Pallas kernels for 1% -> 2%
where the time goes in v8:
time: 256 us; the launch traced here: 255 us
  waiting for transfers between devices  96.5 us (38%)
  blocking collectives  74.6 us (29%)
  starting transfers between devices  30.8 us (12%)
  Pallas kernels  21.9 us (9%)
  between operations  15.8 us (6%)
  local copies, waits for them, and re-layouts  9.52 us (4%)
  other arithmetic  3.98 us (2%)
    all_to_all x2, blocking collectives, exchange(): lax.all_to_all(rows.reshape(groups, capacity, rows.shape[1]), expert, spl...  74.6 us
    all_gather x1, waiting for transfers between devices, on_device(): latents = lax.all_gather(latents, 'z', axis=0, tiled=True)  42.1 us
    reduce_scatter x1, waiting for transfers between devices, on_device(): latents = lax.psum_scatter(parts, 'z', scatter_dimension=0, tiled=True)  26.4 us
    all_to_all x1, waiting for transfers between devices, on_device(): lax.all_to_all(summed, dp_axes, split_axis=0, concat_axis=0, tiled=True)  10.4 us
    ppermute x3, starting transfers between devices, on_device(): neighbours.append(lax.ppermute(packed, 'x', backward))  10.2 us
    all_to_all x1, starting transfers between devices, on_device(): lax.all_to_all(grads, dp_axes, split_axis=0, concat_axis=0, tiled=True)  9.86 us
    pallas_call x1, Pallas kernels, run_expert(): pl.pallas_call(expert_kernel, grid=(steps,), in_specs=[pl.BlockSpec((coun...  9.09 us
    unnamed x37, local copies, waits for them, and re-layouts  8.65 us
  transfers between devices with their start and end apart: 11, of which 9 were waited for; matrix products, arithmetic and copies ran while one was open for 2% of the time, Pallas kernels for 2%

profile of v8, /device:TPU:8, one launch (start us, length us, event | category | flops | bytes accessed | tf_op | source)
XLA Modules:
  0.0 254.8 jit_solution(18282259035460502967)
XLA Ops:
  8.0 0.0 reduce-scatter.2.cloned.1.call-start
  8.1 1.0 copy-done.5
  9.1 1.0 copy-done.6
  10.1 0.9 copy-done.10
  11.0 0.9 copy-done.11
  11.9 0.3 shard_map.111
  12.3 1.9 collective-permute-start
  14.2 2.3 collective-permute-done.got_ref
  16.5 2.1 shard_map.112
  18.5 0.9 copy-done.3
  19.5 0.0 reduce-scatter.2.cloned.1.call-update
  19.5 0.0 all-gather.3.cloned.1.call-start
  19.6 0.8 copy-done.13
  20.4 0.1 slice_bitcast_fusion.1
  20.4 0.0 copy-start.12
  20.5 1.7 fusion.2
  22.1 0.0 copy-start.14
  22.2 4.7 %collective-permute-start.1 = (bf16[16,4608]{1,0:T(8,128)(2,1)S(1)}, bf16[16,4608]{1,0:T(8,128)(2,1)S(1)}, u32[]{:S(2)}, u32[]{:S(2)}) collective-permute-start(bf16[16,4608]{1,0:T(8,128)(2,1)S(1)} %fusion.17.refs_0_), channel_id=1, source_target_pairs={{0,48},{16,0},{32,16},{48,32},{1,49},{17,1},{33,17},{49,33},{2,50}... | collective-permute-start | bytes 442376 | tf_op jit(solution)/shard_map/ppermute | solution.py:388
  26.9 2.7 %collective-permute-start.2 = (bf16[16,4608]{1,0:T(8,128)(2,1)S(1)}, bf16[16,4608]{1,0:T(8,128)(2,1)S(1)}, u32[]{:S(2)}, u32[]{:S(2)}) collective-permute-start(bf16[16,4608]{1,0:T(8,128)(2,1)S(1)} %fusion.17.refs_0_), channel_id=1, source_target_pairs={{0,32},{16,48},{32,0},{48,16},{1,33},{17,49},{33,1},{49,17},{2,34}... | collective-permute-start | bytes 442376 | tf_op jit(solution)/shard_map/ppermute | solution.py:388
  29.6 2.8 %collective-permute-start.3 = (bf16[16,4608]{1,0:T(8,128)(2,1)S(1)}, bf16[16,4608]{1,0:T(8,128)(2,1)S(1)}, u32[]{:S(2)}, u32[]{:S(2)}) collective-permute-start(bf16[16,4608]{1,0:T(8,128)(2,1)S(1)} %fusion.17.refs_0_), channel_id=1, source_target_pairs={{0,16},{16,32},{32,48},{48,0},{1,17},{17,33},{33,49},{49,1},{2,18}... | collective-permute-start | bytes 442376 | tf_op jit(solution)/shard_map/ppermute | solution.py:388
  32.4 1.1 collective-permute-done.1.refs_1_
  33.5 3.5 %collective-permute-done.2.refs_2_ = bf16[16,4608]{1,0:T(8,128)(2,1)S(1)} collective-permute-done((bf16[16,4608]{1,0:T(8,128)(2,1)S(1)}, bf16[16,4608]{1,0:T(8,128)(2,1)S(1)}, u32[]{:S(2)}, u32[]{:S(2)}) %collective-permute-start.2) | collective-permute-done | bytes 147488 | tf_op jit(solution)/shard_map/ppermute | solution.py:388
  37.0 2.1 collective-permute-done.3.refs_3_
  39.1 0.9 shard_map.114
  40.0 0.0 all-gather.3.cloned.1.call-update
  40.0 0.0 all-gather.5.cloned.1.call-start
  40.1 0.1 copy.30
  40.2 0.1 eq.71
  40.3 0.1 eq.67
  40.4 1.2 reduce-window.6
  41.6 0.2 slice_reduce_fusion
  41.8 0.1 fusion.11
  41.9 0.1 reduce_sum.34
  42.1 0.1 copy.33
  42.1 0.2 fusion.4
  42.4 0.2 select_reduce_fusion.1
  42.6 0.2 fusion.3
  42.9 0.2 select_reduce_fusion
  43.2 0.2 copy.34.gate_ref
  43.3 26.4 %reduce-scatter.2.cloned.1.call-done.latents_ref = bf16[128,1024]{1,0:T(8,128)(2,1)} async-done(((bf16[1024,1024]{1,0:T(8,128)(2,1)}), bf16[128,1024]{1,0:T(8,128)(2,1)}) %reduce-scatter.2.cloned.1.call-update) | async-done | bytes 262160 | tf_op jit(solution)/shard_map/reduce_scatter | solution.py:381
  69.8 1.0 copy-done.9
  70.7 0.5 shard_map.113
  71.2 37.7 %all_to_all.20 = bf16[16,40,1024]{2,1,0:T(8,128)(2,1)S(1)} all-to-all(bf16[16,40,1024]{2,1,0:T(8,128)(2,1)S(1)} %bitcast.44), channel_id=1, replica_groups=mesh['y'=8,'x'=4,'z'=8,'c'=2] {'z','c'}, dimensions={0} | all-to-all | bytes 2621440 | tf_op jit(solution)/shard_map/all_to_all | solution.py:397
  109.0 9.1 %shard_map.115 = bf16[640,1024]{1,0:T(8,128)(2,1)S(1)} custom-call(bf16[640,1024]{1,0:T(8,128)(2,1)S(1)} %bitcast.46, bf16[512,4608]{1,0:T(8,128)(2,1)} %all-gather.3.cloned.1.call-done.gate_ref.up_ref.out_ref, bf16[512,4608]{1,0:T(8,128)(2,1)} %all-gather.3.cloned.1.call-done.gate_ref.up_ref.out_ref, ...), custom_call_target="tpu_custom_call" | custom-call | flops 6039797760 | bytes 7340032 | tf_op jit(solution)/shard_map/pallas_call | solution.py:97
  118.1 36.9 %all_to_all.21 = bf16[16,40,1024]{2,1,0:T(8,128)(2,1)S(1)} all-to-all(bf16[16,40,1024]{2,1,0:T(8,128)(2,1)S(1)} %bitcast.47), channel_id=1, replica_groups=mesh['y'=8,'x'=4,'z'=8,'c'=2] {'z','c'}, dimensions={0} | all-to-all | bytes 2621440 | tf_op jit(solution)/shard_map/all_to_all | solution.py:397
  154.9 1.2 shard_map.116
  156.1 0.0 all-gather.5.cloned.1.call-update
  156.1 42.1 %all-gather.5.cloned.1.call-done.latents_ref = bf16[1024,1024]{1,0:T(8,128)(2,1)} async-done(((bf16[128,1024]{1,0:T(8,128)(2,1)}), bf16[1024,1024]{1,0:T(8,128)(2,1)}) %all-gather.5.cloned.1.call-update) | async-done | bytes 2097168 | tf_op jit(solution)/shard_map/all_gather | solution.py:409
  198.2 3.6 %shard_map.119 = (bf16[256,512]{1,0:T(8,128)(2,1)}, bf16[256,512]{1,0:T(8,128)(2,1)}) custom-call(bf16[1024,1024]{1,0:T(8,128)(2,1)} %all-gather.5.cloned.1.call-done.latents_ref, bf16[12,128,256]{2,1,0:T(8,128)(2,1)} %copy-done.1, bf16[12,128,256]{2,1,0:T(8,128)(2,1)} %copy-done.3), custom_call_target="tpu_custom_call" | custom-call | flops 536870912 | bytes 2097152 | tf_op jit(solution)/shard_map/pallas_call | solution.py:272
  201.9 2.0 collective-permute-start.5
  203.9 1.7 collective-permute-done.5
  205.6 1.7 fusion.5
  207.4 9.9 %all-to-all-start.2 = ((bf16[32,8,512]{2,1,0:T(8,128)(2,1)}), bf16[32,8,512]{2,1,0:T(8,128)(2,1)S(1)}, u32[]{:S(2)}, u32[]{:S(2)}) async-start(bf16[32,8,512]{2,1,0:T(8,128)(2,1)} %fusion.5), calls=%async_computation.3 | async-start | bytes 524288 | tf_op jit(solution)/shard_map/all_to_all | solution.py:415
  217.2 1.1 copy-done.4
  218.4 1.5 shard_map.117
  219.9 0.8 copy-done.7
  220.7 2.0 collective-permute-start.4
  222.8 6.9 %all-to-all-done.2.pieces_ref = bf16[32,8,512]{2,1,0:T(8,128)(2,1)S(1)} async-done(((bf16[32,8,512]{2,1,0:T(8,128)(2,1)}), bf16[32,8,512]{2,1,0:T(8,128)(2,1)S(1)}, u32[]{:S(2)}, u32[]{:S(2)}) %all-to-all-start.2) | async-done | bytes 262176 | tf_op jit(solution)/shard_map/all_to_all | solution.py:415
  229.7 0.8 shard_map.120
  230.4 4.6 %all-to-all-start.3 = ((bf16[32,8,512]{2,1,0:T(8,128)(2,1)}), bf16[32,8,512]{2,1,0:T(8,128)(2,1)S(1)}, u32[]{:S(2)}, u32[]{:S(2)}) async-start(bf16[32,8,512]{2,1,0:T(8,128)(2,1)} %shard_map.120), calls=%async_computation.4 | async-start | bytes 524288 | tf_op jit(solution)/shard_map/all_to_all | solution.py:419
  235.1 0.0 collective-permute-done.4.got_ref
  235.1 1.1 shard_map.118
  236.2 10.4 %all-to-all-done.3 = bf16[32,8,512]{2,1,0:T(8,128)(2,1)S(1)} async-done(((bf16[32,8,512]{2,1,0:T(8,128)(2,1)}), bf16[32,8,512]{2,1,0:T(8,128)(2,1)S(1)}, u32[]{:S(2)}, u32[]{:S(2)}) %all-to-all-start.3) | async-done | bytes 262176 | tf_op jit(solution)/shard_map/all_to_all | solution.py:419
  246.6 0.8 shard_map.121
  (37 shorter events, 0.3 us)
Async XLA Ops:
  8.0 61.8 %reduce-scatter.2.cloned.1.call-start = ((), (), s32[]{:S(2)}) async-start(), calls=%async_computation.5 | async-start | bytes 2359296 | tf_op jit(solution)/shard_map/reduce_scatter | solution.py:381
  8.0 1.0 copy-start.5
  9.1 1.0 copy-start.6
  10.1 0.9 copy-start.10
  11.0 0.9 copy-start.11
  12.3 6.3 %copy-start.1 = (bf16[12,128,256]{2,1,0:T(8,128)(2,1)}, bf16[12,128,256]{2,1,0:T(8,128)(2,1)S(1)}, u32[]{:S(2)}) copy-start(bf16[12,128,256]{2,1,0:T(8,128)(2,1)S(1)} %get-tuple-element.18.kept_ref) | copy-start | bytes 2359300
  12.3 4.2 %collective-permute-start = (bf16[12,128,256]{2,1,0:T(8,128)(2,1)S(1)}, bf16[12,128,256]{2,1,0:T(8,128)(2,1)S(1)}, u32[]{:S(2)}, u32[]{:S(2)}) collective-permute-start(bf16[12,128,256]{2,1,0:T(8,128)(2,1)S(1)} %get-tuple-element.19), channel_id=1, source_target_pairs={{0,1},{1,0},{2,3},{3,2},{4,5},{5,4},{6,7},{7,6},{8,9},{9,8},{10,11... | collective-permute-start | bytes 2359304 | tf_op jit(solution)/shard_map/ppermute | solution.py:379
  18.5 0.9 copy-start.3
  19.5 0.9 copy-start.13
  19.5 89.5 %all-gather.3.cloned.1.call-start = ((), (), s32[]{:S(2)}) async-start(), calls=%async_computation.6 | async-start | bytes 5308416 | tf_op jit(solution)/shard_map/all_gather | solution.py:390
  20.4 1.7 copy-start.12
  22.1 18.0 %copy-start.14 = (s32[128,4]{0,1:T(4,128)S(1)}, s32[128,4]{0,1:T(4,128)}, u32[]{:S(2)}) copy-start(s32[128,4]{0,1:T(4,128)} %param.12) | copy-start | bytes 6148
  22.2 11.2 %collective-permute-start.1 = (bf16[16,4608]{1,0:T(8,128)(2,1)S(1)}, bf16[16,4608]{1,0:T(8,128)(2,1)S(1)}, u32[]{:S(2)}, u32[]{:S(2)}) collective-permute-start(bf16[16,4608]{1,0:T(8,128)(2,1)S(1)} %fusion.17.refs_0_), channel_id=1, source_target_pairs={{0,48},{16,0},{32,16},{48,32},{1,49},{17,1},{33,17},{49,33},{2,50}... | collective-permute-start | bytes 442376 | tf_op jit(solution)/shard_map/ppermute | solution.py:388
  26.9 10.1 %collective-permute-start.2 = (bf16[16,4608]{1,0:T(8,128)(2,1)S(1)}, bf16[16,4608]{1,0:T(8,128)(2,1)S(1)}, u32[]{:S(2)}, u32[]{:S(2)}) collective-permute-start(bf16[16,4608]{1,0:T(8,128)(2,1)S(1)} %fusion.17.refs_0_), channel_id=1, source_target_pairs={{0,32},{16,48},{32,0},{48,16},{1,33},{17,49},{33,1},{49,17},{2,34}... | collective-permute-start | bytes 442376 | tf_op jit(solution)/shard_map/ppermute | solution.py:388
  29.6 9.5 %collective-permute-start.3 = (bf16[16,4608]{1,0:T(8,128)(2,1)S(1)}, bf16[16,4608]{1,0:T(8,128)(2,1)S(1)}, u32[]{:S(2)}, u32[]{:S(2)}) collective-permute-start(bf16[16,4608]{1,0:T(8,128)(2,1)S(1)} %fusion.17.refs_0_), channel_id=1, source_target_pairs={{0,16},{16,32},{32,48},{48,0},{1,17},{17,33},{33,49},{49,1},{2,18}... | collective-permute-start | bytes 442376 | tf_op jit(solution)/shard_map/ppermute | solution.py:388
  39.1 3.3 %copy-start.15 = (f32[128,4]{0,1:T(4,128)S(1)}, f32[128,4]{0,1:T(4,128)}, u32[]{:S(2)}) copy-start(f32[128,4]{0,1:T(4,128)} %param.13) | copy-start | bytes 6148
  40.0 158.2 %all-gather.5.cloned.1.call-start = ((), (), s32[]{:S(2)}) async-start(), calls=%async_computation.7 | async-start | bytes 2359296 | tf_op jit(solution)/shard_map/all_gather | solution.py:409
  69.8 1.0 copy-start.9
  198.2 19.0 %copy-start = (bf16[1024,1024]{1,0:T(8,128)(2,1)S(1)}, bf16[1024,1024]{1,0:T(8,128)(2,1)}, u32[]{:S(2)}) copy-start(bf16[1024,1024]{1,0:T(8,128)(2,1)} %all-gather.5.cloned.1.call-done.latents_ref) | copy-start | bytes 6291460
  201.9 15.4 %copy-start.2 = (bf16[12,128,256]{2,1,0:T(8,128)(2,1)S(1)}, bf16[12,128,256]{2,1,0:T(8,128)(2,1)}, u32[]{:S(2)}) copy-start(bf16[12,128,256]{2,1,0:T(8,128)(2,1)} %copy-done.1) | copy-start | bytes 2359300
  201.9 3.8 %collective-permute-start.5 = (bf16[256,512]{1,0:T(8,128)(2,1)}, bf16[256,512]{1,0:T(8,128)(2,1)S(1)}, u32[]{:S(2)}, u32[]{:S(2)}) collective-permute-start(bf16[256,512]{1,0:T(8,128)(2,1)} %get-tuple-element.29), channel_id=1, source_target_pairs={{0,1},{1,0},{2,3},{3,2},{4,5},{5,4},{6,7},{7,6},{8,9},{9,8},{10,11... | collective-permute-start | bytes 786440 | tf_op jit(solution)/shard_map/ppermute | solution.py:411
  207.4 22.3 %all-to-all-start.2 = ((bf16[32,8,512]{2,1,0:T(8,128)(2,1)}), bf16[32,8,512]{2,1,0:T(8,128)(2,1)S(1)}, u32[]{:S(2)}, u32[]{:S(2)}) async-start(bf16[32,8,512]{2,1,0:T(8,128)(2,1)} %fusion.5), calls=%async_computation.3 | async-start | bytes 524288 | tf_op jit(solution)/shard_map/all_to_all | solution.py:415
  217.2 1.1 copy-start.4
  219.9 0.8 copy-start.7
  220.7 14.4 %copy-start.8 = (bf16[1024,256]{1,0:T(8,128)(2,1)S(1)}, bf16[1024,256]{1,0:T(8,128)(2,1)}, u32[]{:S(2)}) copy-start(bf16[1024,256]{1,0:T(8,128)(2,1)} %copy-done.7) | copy-start | bytes 1572868
  220.7 14.4 %collective-permute-start.4 = (bf16[1024,256]{1,0:T(8,128)(2,1)}, bf16[1024,256]{1,0:T(8,128)(2,1)S(1)}, u32[]{:S(2)}, u32[]{:S(2)}) collective-permute-start(bf16[1024,256]{1,0:T(8,128)(2,1)} %get-tuple-element.25), channel_id=1, source_target_pairs={{0,1},{1,0},{2,3},{3,2},{4,5},{5,4},{6,7},{7,6},{8,9},{9,8},{10,11... | collective-permute-start | bytes 1572872 | tf_op jit(solution)/shard_map/ppermute | solution.py:416
  230.4 16.1 %all-to-all-start.3 = ((bf16[32,8,512]{2,1,0:T(8,128)(2,1)}), bf16[32,8,512]{2,1,0:T(8,128)(2,1)S(1)}, u32[]{:S(2)}, u32[]{:S(2)}) async-start(bf16[32,8,512]{2,1,0:T(8,128)(2,1)} %shard_map.120), calls=%async_computation.4 | async-start | bytes 524288 | tf_op jit(solution)/shard_map/all_to_all | solution.py:419
Sparse Core Ops, SparseCore 0:
  19.6 50.0 reduce-scatter.1
  156.2 41.9 all-gather.4
Sparse Core Ops, SparseCore 1:
  40.1 63.0 all-gather.2

commit v9 on v7

--- a/solution.py
+++ b/solution.py
@@ -12,6 +12,7 @@
 TOPK = 4
 CORES = 2
 CHUNK = 512
+PART = 256
 ACROSS = 4
 SMALL = pltpu.CompilerParams(vmem_limit_bytes=16 * 1024 * 1024)
 INNER = (((1,), (0,)), ((), ()))
@@ -70,16 +71,27 @@
         sum_out[...] = jnp.zeros_like(sum_out)
         sum_grad[...] = jnp.zeros_like(sum_grad)
 
-    rows = rows_ref[:, :latent_width]
-    gate_part = dot(rows, gate_ref[...])
-    up_part = dot(rows, up_ref[...])
-    grad_act = dot(rows_ref[:, latent_width:], out_ref[...], COLS)
-    sigmoid_gate = jax.nn.sigmoid(gate_part)
-    silu = gate_part * sigmoid_gate
-    sum_out[...] += dot((silu * up_part).astype(jnp.bfloat16), out_ref[...])
-    grad_gate = grad_act * up_part * sigmoid_gate * (1.0 + gate_part * (1.0 - sigmoid_gate))
-    sum_grad[...] += dot(grad_gate.astype(jnp.bfloat16), gate_ref[...], COLS)
-    sum_grad[...] += dot((grad_act * silu).astype(jnp.bfloat16), up_ref[...], COLS)
+    rows, grads = rows_ref[:, :latent_width], rows_ref[:, latent_width:]
+    products = []
+    for part in range(gate_ref.shape[1] // PART):
+        here = slice(part * PART, (part + 1) * PART)
+        products.append(
+            (
+                dot(rows, gate_ref[:, here]),
+                dot(rows, up_ref[:, here]),
+                dot(grads, out_ref[here], COLS),
+            )
+        )
+    results = []
+    for gate_part, up_part, grad_act in products:
+        sigmoid_gate = jax.nn.sigmoid(gate_part)
+        silu = gate_part * sigmoid_gate
+        grad_gate = grad_act * up_part * sigmoid_gate * (1.0 + gate_part * (1.0 - sigmoid_gate))
+        values = (silu * up_part, grad_gate, grad_act * silu)
+        results.append([value.astype(jnp.bfloat16) for value in values])
+    activation, grad_gate, grad_upper = (jnp.concatenate(part, axis=1) for part in zip(*results))
+    sum_out[...] += dot(activation, out_ref[...])
+    sum_grad[...] += dot(grad_gate, gate_ref[...], COLS) + dot(grad_upper, up_ref[...], COLS)
 
     @pl.when(step == pl.num_programs(0) - 1)
     def _():
@@ -159,31 +171,35 @@
     )(core, tokens, cotangent, down_proj, up_proj)
 
 
-def latent_kernel(kept_ref, got_ref, result_ref):
+def latent_kernel(kept_ref, got_ref, here_ref, there_ref, result_ref):
     features = kept_ref.shape[2] // 2
     count, width = result_ref.shape
-    latent_width = width // 2
-    chips = count // kept_ref.shape[1]
-    blocks = latent_width // (2 * features)
-    kept = kept_ref[:chips].reshape(count, 2 * features)
-    got = got_ref[:chips].reshape(count, 2 * features)
+    blocks = here_ref.shape[0] // 2
+    kept = kept_ref[...].reshape(count, 2 * features)
+    got = got_ref[...].reshape(count, 2 * features)
     for half in range(2):
         rows = slice(half * features, (half + 1) * features)
         left = jnp.concatenate([kept[:, rows], got[:, rows]], axis=1)
         for block in range(blocks):
-            place = chips + half * blocks + block
-            right = jnp.concatenate([kept_ref[place], got_ref[place]], axis=0)
-            start = half * latent_width + block * 2 * features
+            place = half * blocks + block
+            right = jnp.concatenate([here_ref[place], there_ref[place]], axis=0)
+            start = half * (width // 2) + block * 2 * features
             result_ref[:, start : start + 2 * features] = dot(left, right).astype(jnp.bfloat16)
 
 
 def chip_latents(kept, got, chips, latent_width):
-    count = chips * kept.shape[1]
+    blocks, tok_rows, width = kept.shape
+    last = blocks - chips
+    rows = pl.BlockSpec((chips // 2, tok_rows, width), lambda i: (i, 0, 0))
+    projections = pl.BlockSpec((last, tok_rows, width), lambda i: (chips // last, 0, 0))
     return pl.pallas_call(
         latent_kernel,
-        out_shape=jax.ShapeDtypeStruct((count, 2 * latent_width), jnp.bfloat16),
-        compiler_params=SMALL,
-    )(kept, got)
+        grid=(2,),
+        in_specs=[rows, rows, projections, projections],
+        out_specs=pl.BlockSpec((chips // 2 * tok_rows, 2 * latent_width), lambda i: (i, 0)),
+        out_shape=jax.ShapeDtypeStruct((chips * tok_rows, 2 * latent_width), jnp.bfloat16),
+        compiler_params=SMALL,
+    )(kept, got, kept, got)
 
 
 def combine_kernel(returned_ref, gates_ref, spread_ref, result_ref):
@@ -251,12 +267,12 @@
 
 def unpack_kernel(scale, packed_ref, down_ref, up_ref):
     features = up_ref.shape[1]
-    up_ref[...] = packed_ref[:, :features].astype(jnp.float32) * scale
-    down_ref[...] = packed_ref[:, features:].astype(jnp.float32).T * scale
+    up_ref[...] = packed_ref[:features].astype(jnp.float32).T * scale
+    down_ref[...] = packed_ref[features:].astype(jnp.float32) * scale
 
 
 def unpack_grads(packed, scale):
-    latent_width, features = packed.shape[0], packed.shape[1] // 2
+    latent_width, features = packed.shape[1], packed.shape[0] // 2
     return pl.pallas_call(
         functools.partial(unpack_kernel, scale),
         out_shape=[
@@ -323,16 +339,16 @@
     latents = lax.all_gather(latents, expert, axis=0, tiled=True)
     all_out = latents[:, :latent_width]
     all_grad = latents[:, latent_width:]
-    up_part_grad = dot(all_out, cotangent, ROWS)
-    down_part_grad = dot(all_grad, tokens, ROWS)
-    grads = jnp.concatenate([up_part_grad, down_part_grad], axis=1).astype(bf16)
-    grads = grads.reshape(dp, latent_width // dp, 2 * features)
+    up_part_grad = dot(cotangent, all_out, ROWS)
+    down_part_grad = dot(tokens, all_grad, ROWS)
+    grads = jnp.concatenate([up_part_grad, down_part_grad], axis=0).astype(bf16)
+    grads = grads.reshape(dp, 2 * features // dp, latent_width)
     grads = lax.all_to_all(grads, dp_axes, split_axis=0, concat_axis=0, tiled=True)
     mixed = dot(all_out, up_proj).astype(bf16)
     input_grad = dot(all_grad, down_proj, COLS).astype(bf16)
     summed = shared_sums(grads)
     summed = lax.all_to_all(summed, dp_axes, split_axis=0, concat_axis=0, tiled=True)
-    down_grad, up_grad = unpack_grads(summed.reshape(latent_width, 2 * features), grad_scale)
+    down_grad, up_grad = unpack_grads(summed.reshape(2 * features, latent_width), grad_scale)
     return mixed, input_grad, down_grad, up_grad
 
 

time: 250 us -> 250 us (level)
  no operation moved by 1% of the time
where the time goes in v9:
time: 250 us; the launch traced here: 249 us
  blocking collectives  96.9 us (39%)
  waiting for transfers between devices  84.2 us (34%)
  starting transfers between devices  17 us (7%)
  between operations  15.8 us (6%)
  Pallas kernels  15.1 us (6%)
  matrix products  10.6 us (4%)
  local copies, waits for them, and re-layouts  7.23 us (3%)
    all_to_all x2, blocking collectives, exchange(): lax.all_to_all(rows.reshape(groups, capacity, rows.shape[1]), expert, spl...  74.5 us
    all_gather x1, waiting for transfers between devices, on_device(): latents = lax.all_gather(latents, expert, axis=0, tiled=True)  43.2 us
    reduce_scatter x1, waiting for transfers between devices, on_device(): latents = lax.psum_scatter(parts, 'z', scatter_dimension=0, tiled=True)  26.7 us
    all_to_all x1, blocking collectives, on_device(): lax.all_to_all(grads, dp_axes, split_axis=0, concat_axis=0, tiled=True)  22.4 us
    dot_general x5, matrix products, dot(): lax.dot_general(left, right, dims, preferred_element_type=jnp.float32)  10.6 us
    ppermute x3, starting transfers between devices, on_device(): neighbours.append(lax.ppermute(packed, 'x', backward))  10.2 us
    pallas_call x1, Pallas kernels, run_expert(): pl.pallas_call(expert_kernel, grid=(steps,), in_specs=[pl.BlockSpec((coun...  8.82 us
    ppermute x3, waiting for transfers between devices, on_device(): neighbours.append(lax.ppermute(packed, 'x', backward))  6.69 us
  transfers between devices with their start and end apart: 8, of which 7 were waited for; matrix products, arithmetic and copies ran while one was open for 4% of the time, Pallas kernels for 1%

profile of v9, /device:TPU:8, one launch (start us, length us, event | category | flops | bytes accessed | tf_op | source)
XLA Modules:
  0.0 249.1 jit_solution(2088458129787985316)
XLA Ops:
  8.0 0.0 reduce-scatter.2.cloned.1.call-start
  8.0 0.0 copy-start
  8.1 1.0 copy-done
  9.1 1.0 copy-done.2
  10.1 0.9 copy-done.5
  11.0 0.9 copy-done.7
  11.9 0.3 shard_map.111
  12.3 1.9 collective-permute-start
  14.2 2.3 collective-permute-done.got_ref.there_ref
  16.4 1.9 shard_map.112
  18.3 0.0 reduce-scatter.2.cloned.1.call-update
  18.4 0.0 all-gather.3.cloned.1.call-start
  18.4 0.8 copy-done.10
  19.2 0.1 slice_bitcast_fusion.1
  19.3 0.0 copy-start.11
  19.3 1.7 fusion.2
  21.0 0.0 copy-start.12
  21.0 0.0 copy-done.9
  21.1 4.7 %collective-permute-start.1 = (bf16[16,4608]{1,0:T(8,128)(2,1)S(1)}, bf16[16,4608]{1,0:T(8,128)(2,1)S(1)}, u32[]{:S(2)}, u32[]{:S(2)}) collective-permute-start(bf16[16,4608]{1,0:T(8,128)(2,1)S(1)} %fusion.34.refs_0_), channel_id=1, source_target_pairs={{0,48},{16,0},{32,16},{48,32},{1,49},{17,1},{33,17},{49,33},{2,50}... | collective-permute-start | bytes 442376 | tf_op jit(solution)/shard_map/ppermute | solution.py:318
  25.7 2.7 %collective-permute-start.2 = (bf16[16,4608]{1,0:T(8,128)(2,1)S(1)}, bf16[16,4608]{1,0:T(8,128)(2,1)S(1)}, u32[]{:S(2)}, u32[]{:S(2)}) collective-permute-start(bf16[16,4608]{1,0:T(8,128)(2,1)S(1)} %fusion.34.refs_0_), channel_id=1, source_target_pairs={{0,32},{16,48},{32,0},{48,16},{1,33},{17,49},{33,1},{49,17},{2,34}... | collective-permute-start | bytes 442376 | tf_op jit(solution)/shard_map/ppermute | solution.py:318
  28.5 2.8 %collective-permute-start.3 = (bf16[16,4608]{1,0:T(8,128)(2,1)S(1)}, bf16[16,4608]{1,0:T(8,128)(2,1)S(1)}, u32[]{:S(2)}, u32[]{:S(2)}) collective-permute-start(bf16[16,4608]{1,0:T(8,128)(2,1)S(1)} %fusion.34.refs_0_), channel_id=1, source_target_pairs={{0,16},{16,32},{32,48},{48,0},{1,17},{17,33},{33,49},{49,1},{2,18}... | collective-permute-start | bytes 442376 | tf_op jit(solution)/shard_map/ppermute | solution.py:318
  31.3 1.1 collective-permute-done.1.refs_1_
  32.3 3.5 %collective-permute-done.2.refs_2_ = bf16[16,4608]{1,0:T(8,128)(2,1)S(1)} collective-permute-done((bf16[16,4608]{1,0:T(8,128)(2,1)S(1)}, bf16[16,4608]{1,0:T(8,128)(2,1)S(1)}, u32[]{:S(2)}, u32[]{:S(2)}) %collective-permute-start.2) | collective-permute-done | bytes 147488 | tf_op jit(solution)/shard_map/ppermute | solution.py:318
  35.9 2.1 collective-permute-done.3.refs_3_
  38.0 0.9 shard_map.114
  38.8 0.0 all-gather.3.cloned.1.call-update
  38.8 0.0 all-gather.5.cloned.1.call-start
  38.9 0.0 copy-done.11
  38.9 0.1 copy.30
  39.0 0.1 eq.71
  39.1 0.1 eq.67
  39.2 1.2 reduce-window.6
  40.4 0.2 slice_reduce_fusion
  40.7 0.1 fusion.28
  40.8 0.1 reduce_sum.34
  40.9 0.1 copy.33
  40.9 0.2 fusion.10
  41.2 0.0 copy-done.12
  41.2 0.2 select_reduce_fusion.1
  41.4 0.2 fusion.9
  41.7 0.2 select_reduce_fusion
  42.0 0.2 copy.34.gate_ref
  42.1 26.7 %reduce-scatter.2.cloned.1.call-done.latents_ref = bf16[128,1024]{1,0:T(8,128)(2,1)} async-done(((bf16[1024,1024]{1,0:T(8,128)(2,1)}), bf16[128,1024]{1,0:T(8,128)(2,1)}) %reduce-scatter.2.cloned.1.call-update) | async-done | bytes 262160 | tf_op jit(solution)/shard_map/reduce_scatter | solution.py:311
  68.8 0.9 copy-done.4
  69.8 0.5 shard_map.113
  70.3 37.5 %all_to_all.20 = bf16[16,40,1024]{2,1,0:T(8,128)(2,1)S(1)} all-to-all(bf16[16,40,1024]{2,1,0:T(8,128)(2,1)S(1)} %bitcast.50), channel_id=1, replica_groups=mesh['y'=8,'x'=4,'z'=8,'c'=2] {'z','c'}, dimensions={0} | all-to-all | bytes 2621440 | tf_op jit(solution)/shard_map/all_to_all | solution.py:327
  107.8 8.8 %shard_map.115 = bf16[640,1024]{1,0:T(8,128)(2,1)S(1)} custom-call(bf16[640,1024]{1,0:T(8,128)(2,1)S(1)} %bitcast.52, bf16[512,4608]{1,0:T(8,128)(2,1)} %all-gather.3.cloned.1.call-done.gate_ref.up_ref.out_ref, bf16[512,4608]{1,0:T(8,128)(2,1)} %all-gather.3.cloned.1.call-done.gate_ref.up_ref.out_ref, ...), custom_call_target="tpu_custom_call" | custom-call | flops 6039797760 | bytes 7340032 | tf_op jit(solution)/shard_map/pallas_call | solution.py:108
  116.6 0.0 copy-start.1
  116.6 37.0 %all_to_all.21 = bf16[16,40,1024]{2,1,0:T(8,128)(2,1)S(1)} all-to-all(bf16[16,40,1024]{2,1,0:T(8,128)(2,1)S(1)} %bitcast.53), channel_id=1, replica_groups=mesh['y'=8,'x'=4,'z'=8,'c'=2] {'z','c'}, dimensions={0} | all-to-all | bytes 2621440 | tf_op jit(solution)/shard_map/all_to_all | solution.py:327
  153.6 1.2 shard_map.116
  154.8 0.0 all-gather.5.cloned.1.call-update
  154.8 0.0 copy-start.3
  154.9 43.2 %all-gather.5.cloned.1.call-done = bf16[2048,1024]{1,0:T(8,128)(2,1)} async-done(((bf16[128,1024]{1,0:T(8,128)(2,1)}), bf16[2048,1024]{1,0:T(8,128)(2,1)}) %all-gather.5.cloned.1.call-update) | async-done | bytes 4194320 | tf_op jit(solution)/shard_map/all_gather | solution.py:339
  198.0 2.2 fusion.17
  200.3 0.6 copy-done.13
  200.9 0.5 fusion.20
  201.4 0.0 copy-start.6
  201.4 22.4 %all_to_all.22.pieces_ref = bf16[32,8,512]{2,1,0:T(8,128)(2,1)S(1)} all-to-all(bf16[32,8,512]{2,1,0:T(8,128)(2,1)S(1)} %maximum_bitcast_fusion), channel_id=1, replica_groups=mesh['y'=8,'x'=4,'z'=8,'c'=2] {'y','x'}, dimensions={0} | all-to-all | bytes 524288 | tf_op jit(solution)/shard_map/all_to_all | solution.py:346
  223.8 0.8 shard_map.117
  224.5 4.7 %all-to-all-start.3 = ((bf16[32,8,512]{2,1,0:T(8,128)(2,1)}), bf16[32,8,512]{2,1,0:T(8,128)(2,1)S(1)}, u32[]{:S(2)}, u32[]{:S(2)}) async-start(bf16[32,8,512]{2,1,0:T(8,128)(2,1)} %shard_map.117), calls=%async_computation.4 | async-start | bytes 524288 | tf_op jit(solution)/shard_map/all_to_all | solution.py:350
  229.3 3.1 %convolution_convert_fusion = bf16[2048,128]{1,0:T(8,128)(2,1)} fusion(bf16[128,512]{1,0:T(8,128)(2,1)S(1)} %copy-done.6, bf16[2048,1024]{1,0:T(8,128)(2,1)} %all-gather.5.cloned.1.call-done), kind=kOutput, calls=%fused_computation.3 | convolution fusion | flops 268697600 | bytes 2752512 | tf_op jit(solution)/shard_map/dot_general | solution.py:24
  232.4 3.1 %convolution_convert_fusion.1 = bf16[2048,128]{1,0:T(8,128)(2,1)} fusion(bf16[512,128]{1,0:T(8,128)(2,1)S(1)} %copy-done.8, bf16[2048,1024]{1,0:T(8,128)(2,1)} %all-gather.5.cloned.1.call-done), kind=kOutput, calls=%fused_computation.4 | convolution fusion | flops 268697600 | bytes 2752512 | tf_op jit(solution)/shard_map/dot_general | solution.py:24
  235.5 5.3 %all-to-all-done.3 = bf16[32,8,512]{2,1,0:T(8,128)(2,1)S(1)} async-done(((bf16[32,8,512]{2,1,0:T(8,128)(2,1)}), bf16[32,8,512]{2,1,0:T(8,128)(2,1)S(1)}, u32[]{:S(2)}, u32[]{:S(2)}) %all-to-all-start.3) | async-done | bytes 262176 | tf_op jit(solution)/shard_map/all_to_all | solution.py:350
  240.8 0.8 shard_map.118
  (29 shorter events, 0.3 us)
Async XLA Ops:
  8.0 60.9 %reduce-scatter.2.cloned.1.call-start = ((), (), s32[]{:S(2)}) async-start(), calls=%async_computation.5 | async-start | bytes 2359296 | tf_op jit(solution)/shard_map/reduce_scatter | solution.py:311
  8.0 1.0 copy-start
  9.1 1.0 copy-start.2
  10.1 0.9 copy-start.5
  11.0 0.9 copy-start.7
  12.3 4.2 %collective-permute-start = (bf16[12,128,256]{2,1,0:T(8,128)(2,1)S(1)}, bf16[12,128,256]{2,1,0:T(8,128)(2,1)S(1)}, u32[]{:S(2)}, u32[]{:S(2)}) collective-permute-start(bf16[12,128,256]{2,1,0:T(8,128)(2,1)S(1)} %get-tuple-element.13), channel_id=1, source_target_pairs={{0,1},{1,0},{2,3},{3,2},{4,5},{5,4},{6,7},{7,6},{8,9},{9,8},{10,11... | collective-permute-start | bytes 2359304 | tf_op jit(solution)/shard_map/ppermute | solution.py:309
  18.3 0.9 copy-start.10
  18.3 2.7 %copy-start.9 = (bf16[1,42,512]{2,1,0:T(8,128)(2,1)S(1)}, bf16[1,42,512]{2,1,0:T(8,128)(2,1)}, u32[]{:S(2)}) copy-start(bf16[1,42,512]{2,1,0:T(8,128)(2,1)} %param.15) | copy-start | bytes 129028
  18.4 89.4 %all-gather.3.cloned.1.call-start = ((), (), s32[]{:S(2)}) async-start(), calls=%async_computation.6 | async-start | bytes 5308416 | tf_op jit(solution)/shard_map/all_gather | solution.py:320
  19.3 19.6 %copy-start.11 = (s32[128,4]{0,1:T(4,128)S(1)}, s32[128,4]{0,1:T(4,128)}, u32[]{:S(2)}) copy-start(s32[128,4]{0,1:T(4,128)} %param.12) | copy-start | bytes 6148
  21.0 20.2 %copy-start.12 = (f32[128,4]{0,1:T(4,128)S(1)}, f32[128,4]{0,1:T(4,128)}, u32[]{:S(2)}) copy-start(f32[128,4]{0,1:T(4,128)} %param.13) | copy-start | bytes 6148
  21.1 11.3 %collective-permute-start.1 = (bf16[16,4608]{1,0:T(8,128)(2,1)S(1)}, bf16[16,4608]{1,0:T(8,128)(2,1)S(1)}, u32[]{:S(2)}, u32[]{:S(2)}) collective-permute-start(bf16[16,4608]{1,0:T(8,128)(2,1)S(1)} %fusion.34.refs_0_), channel_id=1, source_target_pairs={{0,48},{16,0},{32,16},{48,32},{1,49},{17,1},{33,17},{49,33},{2,50}... | collective-permute-start | bytes 442376 | tf_op jit(solution)/shard_map/ppermute | solution.py:318
  25.7 10.1 %collective-permute-start.2 = (bf16[16,4608]{1,0:T(8,128)(2,1)S(1)}, bf16[16,4608]{1,0:T(8,128)(2,1)S(1)}, u32[]{:S(2)}, u32[]{:S(2)}) collective-permute-start(bf16[16,4608]{1,0:T(8,128)(2,1)S(1)} %fusion.34.refs_0_), channel_id=1, source_target_pairs={{0,32},{16,48},{32,0},{48,16},{1,33},{17,49},{33,1},{49,17},{2,34}... | collective-permute-start | bytes 442376 | tf_op jit(solution)/shard_map/ppermute | solution.py:318
  28.5 9.5 %collective-permute-start.3 = (bf16[16,4608]{1,0:T(8,128)(2,1)S(1)}, bf16[16,4608]{1,0:T(8,128)(2,1)S(1)}, u32[]{:S(2)}, u32[]{:S(2)}) collective-permute-start(bf16[16,4608]{1,0:T(8,128)(2,1)S(1)} %fusion.34.refs_0_), channel_id=1, source_target_pairs={{0,16},{16,32},{32,48},{48,0},{1,17},{17,33},{33,49},{49,1},{2,18}... | collective-permute-start | bytes 442376 | tf_op jit(solution)/shard_map/ppermute | solution.py:318
  38.8 159.2 %all-gather.5.cloned.1.call-start = ((), (), s32[]{:S(2)}) async-start(), calls=%async_computation.7 | async-start | bytes 4456448 | tf_op jit(solution)/shard_map/all_gather | solution.py:339
  68.8 1.0 copy-start.4
  116.6 81.4 %copy-start.1 = (bf16[2048,128]{1,0:T(8,128)(2,1)S(1)}, bf16[2048,128]{1,0:T(8,128)(2,1)}, u32[]{:S(2)}) copy-start(bf16[2048,128]{1,0:T(8,128)(2,1)} %param.8) | copy-start | bytes 1572868
  154.8 45.4 %copy-start.3 = (bf16[2048,128]{1,0:T(8,128)(2,1)S(1)}, bf16[2048,128]{1,0:T(8,128)(2,1)}, u32[]{:S(2)}) copy-start(bf16[2048,128]{1,0:T(8,128)(2,1)} %param.9) | copy-start | bytes 1572868
  198.0 2.8 %copy-start.13 = (bf16[2048,1024]{1,0:T(8,128)(2,1)S(1)}, bf16[2048,1024]{1,0:T(8,128)(2,1)}, u32[]{:S(2)}) copy-start(bf16[2048,1024]{1,0:T(8,128)(2,1)} %all-gather.5.cloned.1.call-done) | copy-start | bytes 12582916
  201.4 27.9 %copy-start.6 = (bf16[128,512]{1,0:T(8,128)(2,1)S(1)}, bf16[128,512]{1,0:T(8,128)(2,1)}, u32[]{:S(2)}) copy-start(bf16[128,512]{1,0:T(8,128)(2,1)} %down_ref.1) | copy-start | bytes 393220
  224.5 7.9 %copy-start.8 = (bf16[512,128]{1,0:T(8,128)(2,1)S(1)}, bf16[512,128]{1,0:T(8,128)(2,1)}, u32[]{:S(2)}) copy-start(bf16[512,128]{1,0:T(8,128)(2,1)} %up_ref.1) | copy-start | bytes 393220
  224.5 16.3 %all-to-all-start.3 = ((bf16[32,8,512]{2,1,0:T(8,128)(2,1)}), bf16[32,8,512]{2,1,0:T(8,128)(2,1)S(1)}, u32[]{:S(2)}, u32[]{:S(2)}) async-start(bf16[32,8,512]{2,1,0:T(8,128)(2,1)} %shard_map.117), calls=%async_computation.4 | async-start | bytes 524288 | tf_op jit(solution)/shard_map/all_to_all | solution.py:350
Sparse Core Ops, SparseCore 0:
  18.5 50.3 reduce-scatter.1
  155.0 43.0 all-gather.4
Sparse Core Ops, SparseCore 1:
  38.9 63.0 all-gather.2

commit v10 on v9

--- a/solution.py
+++ b/solution.py
@@ -305,12 +305,13 @@
     token_blocks = tokens.reshape(blocked)
     cotangent_blocks = cotangent.reshape(blocked)
     place = core.reshape(1).astype(jnp.int32)
+    packed, place = lax.optimization_barrier((packed_weights(expert_in, expert_out, dp), place))
     given, kept = swap_operands(place, token_blocks, cotangent_blocks, down_proj, up_proj)
     got = lax.ppermute(given, "c", swap)
     parts = chip_latents(kept, got, chips, latent_width)
+    packed, parts = lax.optimization_barrier((packed, parts))
     latents = lax.psum_scatter(parts, "z", scatter_dimension=0, tiled=True)
 
-    packed = packed_weights(expert_in, expert_out, dp)
     across = lax.axis_size("x")
     neighbours = [packed]
     for step in range(1, across):

time: 250 us -> 248 us (level)
  local copies, waits for them, and re-layouts: 7.23 us -> 3.46 us
    unnamed x33 -> x23, local copies, waits for them, and re-layouts: 6.36 us -> 1.69 us
    reduce_scatter x1, waiting for transfers between devices: 26.7 us -> 29.4 us  [on_device(): latents = lax.psum_scatter(parts, 'z', scatter_dimension=0, tiled=True)]
where the time goes in v10:
time: 248 us; the launch traced here: 247 us
  blocking collectives  96.8 us (39%)
  waiting for transfers between devices  86.5 us (35%)
  starting transfers between devices  16.8 us (7%)
  between operations  15.8 us (6%)
  Pallas kernels  15.2 us (6%)
  matrix products  10.6 us (4%)
  local copies, waits for them, and re-layouts  3.46 us (1%)
    all_to_all x2, blocking collectives, exchange(): lax.all_to_all(rows.reshape(groups, capacity, rows.shape[1]), expert, spl...  74.6 us
    all_gather x1, waiting for transfers between devices, on_device(): latents = lax.all_gather(latents, expert, axis=0, tiled=True)  42.8 us
    reduce_scatter x1, waiting for transfers between devices, on_device(): latents = lax.psum_scatter(parts, 'z', scatter_dimension=0, tiled=True)  29.4 us
    all_to_all x1, blocking collectives, on_device(): lax.all_to_all(grads, dp_axes, split_axis=0, concat_axis=0, tiled=True)  22.2 us
    dot_general x5, matrix products, dot(): lax.dot_general(left, right, dims, preferred_element_type=jnp.float32)  10.6 us
    ppermute x3, starting transfers between devices, on_device(): neighbours.append(lax.ppermute(packed, 'x', backward))  10.2 us
    pallas_call x1, Pallas kernels, run_expert(): pl.pallas_call(expert_kernel, grid=(steps,), in_specs=[pl.BlockSpec((coun...  8.82 us
    ppermute x3, waiting for transfers between devices, on_device(): neighbours.append(lax.ppermute(packed, 'x', backward))  6.7 us
  transfers between devices with their start and end apart: 8, of which 7 were waited for; matrix products, arithmetic and copies ran while one was open for 4% of the time, Pallas kernels for 1%

profile of v10, /device:TPU:8, one launch (start us, length us, event | category | flops | bytes accessed | tf_op | source)
XLA Modules:
  0.0 247.5 jit_solution(387973452118091450)
XLA Ops:
  8.0 0.0 copy-start.5
  8.0 0.0 copy-start.3
  8.0 0.0 copy-start
  8.0 0.0 copy-start.1
  8.0 0.0 copy-start.4
  8.0 0.0 reduce-scatter.2.cloned.1.call-start
  8.1 1.0 slice_bitcast_fusion.1
  9.1 1.7 fusion.2
  10.8 0.0 copy-done.5
  10.8 0.0 copy-done.3
  10.9 0.0 copy-done
  10.9 0.0 copy-done.1
  10.9 0.0 copy-done.4
  10.9 0.3 shard_map.111
  11.2 1.9 collective-permute-start
  13.1 2.3 collective-permute-done.got_ref.there_ref
  15.4 1.9 shard_map.112
  17.3 0.0 copy-start.6
  17.3 0.0 copy-start.7
  17.3 0.0 reduce-scatter.2.cloned.1.call-update
  17.3 0.0 all-gather.3.cloned.1.call-start
  17.4 4.7 %collective-permute-start.1 = (bf16[16,4608]{1,0:T(8,128)(2,1)S(1)}, bf16[16,4608]{1,0:T(8,128)(2,1)S(1)}, u32[]{:S(2)}, u32[]{:S(2)}) collective-permute-start(bf16[16,4608]{1,0:T(8,128)(2,1)S(1)} %fusion.34.refs_0_), channel_id=1, source_target_pairs={{0,48},{16,0},{32,16},{48,32},{1,49},{17,1},{33,17},{49,33},{2,50}... | collective-permute-start | bytes 442376 | tf_op jit(solution)/shard_map/ppermute | solution.py:319
  22.0 2.7 %collective-permute-start.2 = (bf16[16,4608]{1,0:T(8,128)(2,1)S(1)}, bf16[16,4608]{1,0:T(8,128)(2,1)S(1)}, u32[]{:S(2)}, u32[]{:S(2)}) collective-permute-start(bf16[16,4608]{1,0:T(8,128)(2,1)S(1)} %fusion.34.refs_0_), channel_id=1, source_target_pairs={{0,32},{16,48},{32,0},{48,16},{1,33},{17,49},{33,1},{49,17},{2,34}... | collective-permute-start | bytes 442376 | tf_op jit(solution)/shard_map/ppermute | solution.py:319
  24.8 2.8 %collective-permute-start.3 = (bf16[16,4608]{1,0:T(8,128)(2,1)S(1)}, bf16[16,4608]{1,0:T(8,128)(2,1)S(1)}, u32[]{:S(2)}, u32[]{:S(2)}) collective-permute-start(bf16[16,4608]{1,0:T(8,128)(2,1)S(1)} %fusion.34.refs_0_), channel_id=1, source_target_pairs={{0,16},{16,32},{32,48},{48,0},{1,17},{17,33},{33,49},{49,1},{2,18}... | collective-permute-start | bytes 442376 | tf_op jit(solution)/shard_map/ppermute | solution.py:319
  27.6 1.1 collective-permute-done.1.refs_1_
  28.6 3.6 %collective-permute-done.2.refs_2_ = bf16[16,4608]{1,0:T(8,128)(2,1)S(1)} collective-permute-done((bf16[16,4608]{1,0:T(8,128)(2,1)S(1)}, bf16[16,4608]{1,0:T(8,128)(2,1)S(1)}, u32[]{:S(2)}, u32[]{:S(2)}) %collective-permute-start.2) | collective-permute-done | bytes 147488 | tf_op jit(solution)/shard_map/ppermute | solution.py:319
  32.2 2.1 collective-permute-done.3.refs_3_
  34.3 0.9 shard_map.114
  35.1 0.0 all-gather.3.cloned.1.call-update
  35.2 0.0 all-gather.5.cloned.1.call-start
  35.2 0.0 copy-done.6
  35.2 0.1 copy.30
  35.3 0.1 eq.70
  35.4 0.1 eq.74
  35.6 1.2 reduce-window.6
  36.7 0.2 slice_reduce_fusion
  37.0 0.1 fusion.28
  37.1 0.1 reduce_sum.34
  37.2 0.1 copy.33
  37.3 0.2 fusion.10
  37.5 0.0 copy-done.7
  37.5 0.2 select_reduce_fusion.1
  37.7 0.2 fusion.9
  38.0 0.2 select_reduce_fusion
  38.3 0.2 copy.34.gate_ref
  38.5 29.4 %reduce-scatter.2.cloned.1.call-done.latents_ref = bf16[128,1024]{1,0:T(8,128)(2,1)} async-done(((bf16[1024,1024]{1,0:T(8,128)(2,1)}), bf16[128,1024]{1,0:T(8,128)(2,1)}) %reduce-scatter.2.cloned.1.call-update) | async-done | bytes 262160 | tf_op jit(solution)/shard_map/reduce_scatter | solution.py:313
  67.8 1.0 copy-done.2
  68.8 0.5 shard_map.113
  69.3 37.7 %all_to_all.20 = bf16[16,40,1024]{2,1,0:T(8,128)(2,1)S(1)} all-to-all(bf16[16,40,1024]{2,1,0:T(8,128)(2,1)S(1)} %bitcast.50), channel_id=1, replica_groups=mesh['y'=8,'x'=4,'z'=8,'c'=2] {'z','c'}, dimensions={0} | all-to-all | bytes 2621440 | tf_op jit(solution)/shard_map/all_to_all | solution.py:328
  107.0 8.8 %shard_map.115 = bf16[640,1024]{1,0:T(8,128)(2,1)S(1)} custom-call(bf16[640,1024]{1,0:T(8,128)(2,1)S(1)} %bitcast.52, bf16[512,4608]{1,0:T(8,128)(2,1)} %all-gather.3.cloned.1.call-done.gate_ref.up_ref.out_ref, bf16[512,4608]{1,0:T(8,128)(2,1)} %all-gather.3.cloned.1.call-done.gate_ref.up_ref.out_ref, ...), custom_call_target="tpu_custom_call" | custom-call | flops 6039797760 | bytes 7340032 | tf_op jit(solution)/shard_map/pallas_call | solution.py:108
  115.8 36.9 %all_to_all.21 = bf16[16,40,1024]{2,1,0:T(8,128)(2,1)S(1)} all-to-all(bf16[16,40,1024]{2,1,0:T(8,128)(2,1)S(1)} %bitcast.53), channel_id=1, replica_groups=mesh['y'=8,'x'=4,'z'=8,'c'=2] {'z','c'}, dimensions={0} | all-to-all | bytes 2621440 | tf_op jit(solution)/shard_map/all_to_all | solution.py:328
  152.7 1.2 shard_map.116
  153.9 0.0 all-gather.5.cloned.1.call-update
  153.9 42.8 %all-gather.5.cloned.1.call-done = bf16[2048,1024]{1,0:T(8,128)(2,1)} async-done(((bf16[128,1024]{1,0:T(8,128)(2,1)}), bf16[2048,1024]{1,0:T(8,128)(2,1)}) %all-gather.5.cloned.1.call-update) | async-done | bytes 4194320 | tf_op jit(solution)/shard_map/all_gather | solution.py:340
  196.8 2.2 fusion.17
  199.0 0.6 copy-done.8
  199.6 0.5 fusion.20
  200.1 22.2 %all_to_all.22.pieces_ref = bf16[32,8,512]{2,1,0:T(8,128)(2,1)S(1)} all-to-all(bf16[32,8,512]{2,1,0:T(8,128)(2,1)S(1)} %maximum_bitcast_fusion), channel_id=1, replica_groups=mesh['y'=8,'x'=4,'z'=8,'c'=2] {'y','x'}, dimensions={0} | all-to-all | bytes 524288 | tf_op jit(solution)/shard_map/all_to_all | solution.py:347
  222.3 0.8 shard_map.117
  223.1 4.6 %all-to-all-start.3 = ((bf16[32,8,512]{2,1,0:T(8,128)(2,1)}), bf16[32,8,512]{2,1,0:T(8,128)(2,1)S(1)}, u32[]{:S(2)}, u32[]{:S(2)}) async-start(bf16[32,8,512]{2,1,0:T(8,128)(2,1)} %shard_map.117), calls=%async_computation.4 | async-start | bytes 524288 | tf_op jit(solution)/shard_map/all_to_all | solution.py:351
  227.7 3.1 %convolution_convert_fusion.1 = bf16[2048,128]{1,0:T(8,128)(2,1)} fusion(bf16[512,128]{1,0:T(8,128)(2,1)S(1)} %copy-done.3, bf16[2048,1024]{1,0:T(8,128)(2,1)} %all-gather.5.cloned.1.call-done), kind=kOutput, calls=%fused_computation.4 | convolution fusion | flops 268697600 | bytes 2752512 | tf_op jit(solution)/shard_map/dot_general | solution.py:24
  230.8 3.1 %convolution_convert_fusion = bf16[2048,128]{1,0:T(8,128)(2,1)} fusion(bf16[128,512]{1,0:T(8,128)(2,1)S(1)} %copy-done.4, bf16[2048,1024]{1,0:T(8,128)(2,1)} %all-gather.5.cloned.1.call-done), kind=kOutput, calls=%fused_computation.3 | convolution fusion | flops 268697600 | bytes 2752512 | tf_op jit(solution)/shard_map/dot_general | solution.py:24
  233.9 5.3 %all-to-all-done.3 = bf16[32,8,512]{2,1,0:T(8,128)(2,1)S(1)} async-done(((bf16[32,8,512]{2,1,0:T(8,128)(2,1)}), bf16[32,8,512]{2,1,0:T(8,128)(2,1)S(1)}, u32[]{:S(2)}, u32[]{:S(2)}) %all-to-all-start.3) | async-done | bytes 262176 | tf_op jit(solution)/shard_map/all_to_all | solution.py:351
  239.2 0.8 shard_map.118
  (19 shorter events, 0.2 us)
Async XLA Ops:
  8.0 2.8 %copy-start.5 = (bf16[1,42,512]{2,1,0:T(8,128)(2,1)S(1)}, bf16[1,42,512]{2,1,0:T(8,128)(2,1)}, u32[]{:S(2)}) copy-start(bf16[1,42,512]{2,1,0:T(8,128)(2,1)} %param.15) | copy-start | bytes 129028
  8.0 2.8 %copy-start.3 = (bf16[512,128]{1,0:T(8,128)(2,1)S(1)}, bf16[512,128]{1,0:T(8,128)(2,1)}, u32[]{:S(2)}) copy-start(bf16[512,128]{1,0:T(8,128)(2,1)} %up_ref.1) | copy-start | bytes 393220
  8.0 2.8 %copy-start = (bf16[2048,128]{1,0:T(8,128)(2,1)S(1)}, bf16[2048,128]{1,0:T(8,128)(2,1)}, u32[]{:S(2)}) copy-start(bf16[2048,128]{1,0:T(8,128)(2,1)} %param.8) | copy-start | bytes 1572868
  8.0 2.8 %copy-start.1 = (bf16[2048,128]{1,0:T(8,128)(2,1)S(1)}, bf16[2048,128]{1,0:T(8,128)(2,1)}, u32[]{:S(2)}) copy-start(bf16[2048,128]{1,0:T(8,128)(2,1)} %param.9) | copy-start | bytes 1572868
  8.0 2.8 %copy-start.4 = (bf16[128,512]{1,0:T(8,128)(2,1)S(1)}, bf16[128,512]{1,0:T(8,128)(2,1)}, u32[]{:S(2)}) copy-start(bf16[128,512]{1,0:T(8,128)(2,1)} %down_ref.1) | copy-start | bytes 393220
  8.0 59.8 %reduce-scatter.2.cloned.1.call-start = ((), (), s32[]{:S(2)}) async-start(), calls=%async_computation.5 | async-start | bytes 2359296 | tf_op jit(solution)/shard_map/reduce_scatter | solution.py:313
  11.2 4.2 %collective-permute-start = (bf16[12,128,256]{2,1,0:T(8,128)(2,1)S(1)}, bf16[12,128,256]{2,1,0:T(8,128)(2,1)S(1)}, u32[]{:S(2)}, u32[]{:S(2)}) collective-permute-start(bf16[12,128,256]{2,1,0:T(8,128)(2,1)S(1)} %get-tuple-element.19), channel_id=1, source_target_pairs={{0,1},{1,0},{2,3},{3,2},{4,5},{5,4},{6,7},{7,6},{8,9},{9,8},{10,11... | collective-permute-start | bytes 2359304 | tf_op jit(solution)/shard_map/ppermute | solution.py:310
  17.3 17.9 %copy-start.6 = (s32[128,4]{0,1:T(4,128)S(1)}, s32[128,4]{0,1:T(4,128)}, u32[]{:S(2)}) copy-start(s32[128,4]{0,1:T(4,128)} %param.12) | copy-start | bytes 6148
  17.3 20.2 %copy-start.7 = (f32[128,4]{0,1:T(4,128)S(1)}, f32[128,4]{0,1:T(4,128)}, u32[]{:S(2)}) copy-start(f32[128,4]{0,1:T(4,128)} %param.13) | copy-start | bytes 6148
  17.3 89.7 %all-gather.3.cloned.1.call-start = ((), (), s32[]{:S(2)}) async-start(), calls=%async_computation.6 | async-start | bytes 5308416 | tf_op jit(solution)/shard_map/all_gather | solution.py:321
  17.4 11.3 %collective-permute-start.1 = (bf16[16,4608]{1,0:T(8,128)(2,1)S(1)}, bf16[16,4608]{1,0:T(8,128)(2,1)S(1)}, u32[]{:S(2)}, u32[]{:S(2)}) collective-permute-start(bf16[16,4608]{1,0:T(8,128)(2,1)S(1)} %fusion.34.refs_0_), channel_id=1, source_target_pairs={{0,48},{16,0},{32,16},{48,32},{1,49},{17,1},{33,17},{49,33},{2,50}... | collective-permute-start | bytes 442376 | tf_op jit(solution)/shard_map/ppermute | solution.py:319
  22.0 10.1 %collective-permute-start.2 = (bf16[16,4608]{1,0:T(8,128)(2,1)S(1)}, bf16[16,4608]{1,0:T(8,128)(2,1)S(1)}, u32[]{:S(2)}, u32[]{:S(2)}) collective-permute-start(bf16[16,4608]{1,0:T(8,128)(2,1)S(1)} %fusion.34.refs_0_), channel_id=1, source_target_pairs={{0,32},{16,48},{32,0},{48,16},{1,33},{17,49},{33,1},{49,17},{2,34}... | collective-permute-start | bytes 442376 | tf_op jit(solution)/shard_map/ppermute | solution.py:319
  24.8 9.5 %collective-permute-start.3 = (bf16[16,4608]{1,0:T(8,128)(2,1)S(1)}, bf16[16,4608]{1,0:T(8,128)(2,1)S(1)}, u32[]{:S(2)}, u32[]{:S(2)}) collective-permute-start(bf16[16,4608]{1,0:T(8,128)(2,1)S(1)} %fusion.34.refs_0_), channel_id=1, source_target_pairs={{0,16},{16,32},{32,48},{48,0},{1,17},{17,33},{33,49},{49,1},{2,18}... | collective-permute-start | bytes 442376 | tf_op jit(solution)/shard_map/ppermute | solution.py:319
  35.2 161.6 %all-gather.5.cloned.1.call-start = ((), (), s32[]{:S(2)}) async-start(), calls=%async_computation.7 | async-start | bytes 4456448 | tf_op jit(solution)/shard_map/all_gather | solution.py:340
  67.8 1.0 copy-start.2
  196.8 2.8 %copy-start.8 = (bf16[2048,1024]{1,0:T(8,128)(2,1)S(1)}, bf16[2048,1024]{1,0:T(8,128)(2,1)}, u32[]{:S(2)}) copy-start(bf16[2048,1024]{1,0:T(8,128)(2,1)} %all-gather.5.cloned.1.call-done) | copy-start | bytes 12582916
  223.1 16.1 %all-to-all-start.3 = ((bf16[32,8,512]{2,1,0:T(8,128)(2,1)}), bf16[32,8,512]{2,1,0:T(8,128)(2,1)S(1)}, u32[]{:S(2)}, u32[]{:S(2)}) async-start(bf16[32,8,512]{2,1,0:T(8,128)(2,1)} %shard_map.117), calls=%async_computation.4 | async-start | bytes 524288 | tf_op jit(solution)/shard_map/all_to_all | solution.py:351
Sparse Core Ops, SparseCore 0:
  17.4 50.3 reduce-scatter.1
  154.0 42.6 all-gather.4
Sparse Core Ops, SparseCore 1:
  35.2 63.0 all-gather.2

commit v11 on v9

--- a/solution.py
+++ b/solution.py
@@ -45,7 +45,7 @@
     return to_slot, slot_gate, to_token, jnp.concatenate([gate_high, gate_low], axis=0)
 
 
-def packed_weights(expert_in, expert_out, dp):
+def regrouped(expert_in, expert_out, dp):
     in_rows, width = expert_in.shape[1:]
     own, latent_width = expert_out.shape[1:]
     hidden = width // 2
@@ -57,6 +57,13 @@
     pick = (jnp.arange(hidden, dtype=jnp.int32)[:, None] == source[None, :]).astype(jnp.bfloat16)
     both = jnp.concatenate([expert_in[0, :, :hidden], expert_in[0, :, hidden:]], axis=0)
     both = dot(both, pick).astype(jnp.bfloat16)
+    return both
+
+
+def packed_weights(both, expert_out):
+    in_rows = both.shape[0] // 2
+    own = expert_out.shape[1]
+    tiles = -(-own // in_rows)
     rows = jnp.pad(expert_out[0], ((0, tiles * in_rows - own), (0, 0)))
     rows = [rows[t * in_rows : (t + 1) * in_rows] for t in range(tiles)]
     return jnp.concatenate([both[:in_rows], both[in_rows:], *rows], axis=1)
@@ -305,12 +312,14 @@
     token_blocks = tokens.reshape(blocked)
     cotangent_blocks = cotangent.reshape(blocked)
     place = core.reshape(1).astype(jnp.int32)
+    both, place = lax.optimization_barrier((regrouped(expert_in, expert_out, dp), place))
     given, kept = swap_operands(place, token_blocks, cotangent_blocks, down_proj, up_proj)
     got = lax.ppermute(given, "c", swap)
     parts = chip_latents(kept, got, chips, latent_width)
+    both, parts = lax.optimization_barrier((both, parts))
+    packed = packed_weights(both, expert_out)
     latents = lax.psum_scatter(parts, "z", scatter_dimension=0, tiled=True)
 
-    packed = packed_weights(expert_in, expert_out, dp)
     across = lax.axis_size("x")
     neighbours = [packed]
     for step in range(1, across):

time: 250 us -> 248 us (level)
  local copies, waits for them, and re-layouts: 7.23 us -> 4.14 us
    unnamed x33 -> x23, local copies, waits for them, and re-layouts: 6.36 us -> 2.37 us
where the time goes in v11:
time: 248 us; the launch traced here: 247 us
  blocking collectives  96.5 us (39%)
  waiting for transfers between devices  86.1 us (35%)
  starting transfers between devices  16.8 us (7%)
  between operations  15.8 us (6%)
  Pallas kernels  15.2 us (6%)
  matrix products  10.6 us (4%)
  local copies, waits for them, and re-layouts  4.14 us (2%)
    all_to_all x2, blocking collectives, exchange(): lax.all_to_all(rows.reshape(groups, capacity, rows.shape[1]), expert, spl...  74.3 us
    all_gather x1, waiting for transfers between devices, on_device(): latents = lax.all_gather(latents, expert, axis=0, tiled=True)  43.1 us
    reduce_scatter x1, waiting for transfers between devices, on_device(): latents = lax.psum_scatter(parts, 'z', scatter_dimension=0, tiled=True)  28.7 us
    all_to_all x1, blocking collectives, on_device(): lax.all_to_all(grads, dp_axes, split_axis=0, concat_axis=0, tiled=True)  22.2 us
    dot_general x5, matrix products, dot(): lax.dot_general(left, right, dims, preferred_element_type=jnp.float32)  10.6 us
    ppermute x3, starting transfers between devices, on_device(): neighbours.append(lax.ppermute(packed, 'x', backward))  10.2 us
    pallas_call x1, Pallas kernels, run_expert(): pl.pallas_call(expert_kernel, grid=(steps,), in_specs=[pl.BlockSpec((coun...  8.82 us
    ppermute x3, waiting for transfers between devices, on_device(): neighbours.append(lax.ppermute(packed, 'x', backward))  6.7 us
  transfers between devices with their start and end apart: 8, of which 7 were waited for; matrix products, arithmetic and copies ran while one was open for 4% of the time, Pallas kernels for 1%

profile of v11, /device:TPU:8, one launch (start us, length us, event | category | flops | bytes accessed | tf_op | source)
XLA Modules:
  0.0 247.4 jit_solution(13869057732673118699)
XLA Ops:
  8.0 0.0 copy-start.3
  8.0 0.0 copy-start
  8.0 0.0 copy-start.1
  8.0 0.0 copy-start.4
  8.0 0.0 reduce-scatter.2.cloned.1.call-start
  8.1 1.0 slice_bitcast_fusion.1
  9.1 1.7 fusion.2
  10.8 0.0 copy-done.3
  10.8 0.0 copy-done
  10.8 0.0 copy-done.1
  10.8 0.0 copy-done.4
  10.8 0.3 shard_map.111
  11.1 1.9 collective-permute-start
  13.1 2.3 collective-permute-done.got_ref.there_ref
  15.3 1.9 shard_map.112
  17.2 0.0 copy-start.5
  17.2 0.0 copy-start.6
  17.2 0.0 copy-start.7
  17.2 0.0 reduce-scatter.2.cloned.1.call-update
  17.2 0.0 all-gather.3.cloned.1.call-start
  17.3 0.7 copy-done.5
  18.0 4.7 %collective-permute-start.1 = (bf16[16,4608]{1,0:T(8,128)(2,1)S(1)}, bf16[16,4608]{1,0:T(8,128)(2,1)S(1)}, u32[]{:S(2)}, u32[]{:S(2)}) collective-permute-start(bf16[16,4608]{1,0:T(8,128)(2,1)S(1)} %fusion.34.refs_0_), channel_id=1, source_target_pairs={{0,48},{16,0},{32,16},{48,32},{1,49},{17,1},{33,17},{49,33},{2,50}... | collective-permute-start | bytes 442376 | tf_op jit(solution)/shard_map/ppermute | solution.py:327
  22.7 2.7 %collective-permute-start.2 = (bf16[16,4608]{1,0:T(8,128)(2,1)S(1)}, bf16[16,4608]{1,0:T(8,128)(2,1)S(1)}, u32[]{:S(2)}, u32[]{:S(2)}) collective-permute-start(bf16[16,4608]{1,0:T(8,128)(2,1)S(1)} %fusion.34.refs_0_), channel_id=1, source_target_pairs={{0,32},{16,48},{32,0},{48,16},{1,33},{17,49},{33,1},{49,17},{2,34}... | collective-permute-start | bytes 442376 | tf_op jit(solution)/shard_map/ppermute | solution.py:327
  25.4 2.8 %collective-permute-start.3 = (bf16[16,4608]{1,0:T(8,128)(2,1)S(1)}, bf16[16,4608]{1,0:T(8,128)(2,1)S(1)}, u32[]{:S(2)}, u32[]{:S(2)}) collective-permute-start(bf16[16,4608]{1,0:T(8,128)(2,1)S(1)} %fusion.34.refs_0_), channel_id=1, source_target_pairs={{0,16},{16,32},{32,48},{48,0},{1,17},{17,33},{33,49},{49,1},{2,18}... | collective-permute-start | bytes 442376 | tf_op jit(solution)/shard_map/ppermute | solution.py:327
  28.2 1.1 collective-permute-done.1.refs_1_
  29.3 3.5 %collective-permute-done.2.refs_2_ = bf16[16,4608]{1,0:T(8,128)(2,1)S(1)} collective-permute-done((bf16[16,4608]{1,0:T(8,128)(2,1)S(1)}, bf16[16,4608]{1,0:T(8,128)(2,1)S(1)}, u32[]{:S(2)}, u32[]{:S(2)}) %collective-permute-start.2) | collective-permute-done | bytes 147488 | tf_op jit(solution)/shard_map/ppermute | solution.py:327
  32.8 2.1 collective-permute-done.3.refs_3_
  34.9 0.9 shard_map.114
  35.8 0.0 all-gather.3.cloned.1.call-update
  35.8 0.0 all-gather.5.cloned.1.call-start
  35.8 0.0 copy-done.6
  35.9 0.1 copy.30
  36.0 0.1 eq.70
  36.1 0.1 eq.74
  36.2 1.2 reduce-window.6
  37.4 0.2 slice_reduce_fusion
  37.6 0.1 fusion.28
  37.7 0.1 reduce_sum.34
  37.8 0.1 copy.33
  37.9 0.2 fusion.10
  38.1 0.0 copy-done.7
  38.1 0.2 select_reduce_fusion.1
  38.4 0.2 fusion.9
  38.6 0.2 select_reduce_fusion
  38.9 0.2 copy.34.gate_ref
  39.1 28.7 %reduce-scatter.2.cloned.1.call-done.latents_ref = bf16[128,1024]{1,0:T(8,128)(2,1)} async-done(((bf16[1024,1024]{1,0:T(8,128)(2,1)}), bf16[128,1024]{1,0:T(8,128)(2,1)}) %reduce-scatter.2.cloned.1.call-update) | async-done | bytes 262160 | tf_op jit(solution)/shard_map/reduce_scatter | solution.py:321
  67.8 1.0 copy-done.2
  68.7 0.5 shard_map.113
  69.2 37.4 %all_to_all.20 = bf16[16,40,1024]{2,1,0:T(8,128)(2,1)S(1)} all-to-all(bf16[16,40,1024]{2,1,0:T(8,128)(2,1)S(1)} %bitcast.50), channel_id=1, replica_groups=mesh['y'=8,'x'=4,'z'=8,'c'=2] {'z','c'}, dimensions={0} | all-to-all | bytes 2621440 | tf_op jit(solution)/shard_map/all_to_all | solution.py:336
  106.7 8.8 %shard_map.115 = bf16[640,1024]{1,0:T(8,128)(2,1)S(1)} custom-call(bf16[640,1024]{1,0:T(8,128)(2,1)S(1)} %bitcast.52, bf16[512,4608]{1,0:T(8,128)(2,1)} %all-gather.3.cloned.1.call-done.gate_ref.up_ref.out_ref, bf16[512,4608]{1,0:T(8,128)(2,1)} %all-gather.3.cloned.1.call-done.gate_ref.up_ref.out_ref, ...), custom_call_target="tpu_custom_call" | custom-call | flops 6039797760 | bytes 7340032 | tf_op jit(solution)/shard_map/pallas_call | solution.py:115
  115.5 36.9 %all_to_all.21 = bf16[16,40,1024]{2,1,0:T(8,128)(2,1)S(1)} all-to-all(bf16[16,40,1024]{2,1,0:T(8,128)(2,1)S(1)} %bitcast.53), channel_id=1, replica_groups=mesh['y'=8,'x'=4,'z'=8,'c'=2] {'z','c'}, dimensions={0} | all-to-all | bytes 2621440 | tf_op jit(solution)/shard_map/all_to_all | solution.py:336
  152.4 1.2 shard_map.116
  153.6 0.0 all-gather.5.cloned.1.call-update
  153.6 43.1 %all-gather.5.cloned.1.call-done = bf16[2048,1024]{1,0:T(8,128)(2,1)} async-done(((bf16[128,1024]{1,0:T(8,128)(2,1)}), bf16[2048,1024]{1,0:T(8,128)(2,1)}) %all-gather.5.cloned.1.call-update) | async-done | bytes 4194320 | tf_op jit(solution)/shard_map/all_gather | solution.py:348
  196.7 2.2 fusion.17
  198.9 0.6 copy-done.8
  199.5 0.5 fusion.20
  200.0 22.2 %all_to_all.22.pieces_ref = bf16[32,8,512]{2,1,0:T(8,128)(2,1)S(1)} all-to-all(bf16[32,8,512]{2,1,0:T(8,128)(2,1)S(1)} %maximum_bitcast_fusion), channel_id=1, replica_groups=mesh['y'=8,'x'=4,'z'=8,'c'=2] {'y','x'}, dimensions={0} | all-to-all | bytes 524288 | tf_op jit(solution)/shard_map/all_to_all | solution.py:355
  222.2 0.8 shard_map.117
  223.0 4.6 %all-to-all-start.3 = ((bf16[32,8,512]{2,1,0:T(8,128)(2,1)}), bf16[32,8,512]{2,1,0:T(8,128)(2,1)S(1)}, u32[]{:S(2)}, u32[]{:S(2)}) async-start(bf16[32,8,512]{2,1,0:T(8,128)(2,1)} %shard_map.117), calls=%async_computation.4 | async-start | bytes 524288 | tf_op jit(solution)/shard_map/all_to_all | solution.py:359
  227.6 3.1 %convolution_convert_fusion.1 = bf16[2048,128]{1,0:T(8,128)(2,1)} fusion(bf16[512,128]{1,0:T(8,128)(2,1)S(1)} %copy-done.3, bf16[2048,1024]{1,0:T(8,128)(2,1)} %all-gather.5.cloned.1.call-done), kind=kOutput, calls=%fused_computation.4 | convolution fusion | flops 268697600 | bytes 2752512 | tf_op jit(solution)/shard_map/dot_general | solution.py:24
  230.7 3.1 %convolution_convert_fusion = bf16[2048,128]{1,0:T(8,128)(2,1)} fusion(bf16[128,512]{1,0:T(8,128)(2,1)S(1)} %copy-done.4, bf16[2048,1024]{1,0:T(8,128)(2,1)} %all-gather.5.cloned.1.call-done), kind=kOutput, calls=%fused_computation.3 | convolution fusion | flops 268697600 | bytes 2752512 | tf_op jit(solution)/shard_map/dot_general | solution.py:24
  233.8 5.3 %all-to-all-done.3 = bf16[32,8,512]{2,1,0:T(8,128)(2,1)S(1)} async-done(((bf16[32,8,512]{2,1,0:T(8,128)(2,1)}), bf16[32,8,512]{2,1,0:T(8,128)(2,1)S(1)}, u32[]{:S(2)}, u32[]{:S(2)}) %all-to-all-start.3) | async-done | bytes 262176 | tf_op jit(solution)/shard_map/all_to_all | solution.py:359
  239.1 0.8 shard_map.118
  (19 shorter events, 0.2 us)
Async XLA Ops:
  8.0 2.8 %copy-start.3 = (bf16[512,128]{1,0:T(8,128)(2,1)S(1)}, bf16[512,128]{1,0:T(8,128)(2,1)}, u32[]{:S(2)}) copy-start(bf16[512,128]{1,0:T(8,128)(2,1)} %up_ref.1) | copy-start | bytes 393220
  8.0 2.8 %copy-start = (bf16[2048,128]{1,0:T(8,128)(2,1)S(1)}, bf16[2048,128]{1,0:T(8,128)(2,1)}, u32[]{:S(2)}) copy-start(bf16[2048,128]{1,0:T(8,128)(2,1)} %param.8) | copy-start | bytes 1572868
  8.0 2.8 %copy-start.1 = (bf16[2048,128]{1,0:T(8,128)(2,1)S(1)}, bf16[2048,128]{1,0:T(8,128)(2,1)}, u32[]{:S(2)}) copy-start(bf16[2048,128]{1,0:T(8,128)(2,1)} %param.9) | copy-start | bytes 1572868
  8.0 2.8 %copy-start.4 = (bf16[128,512]{1,0:T(8,128)(2,1)S(1)}, bf16[128,512]{1,0:T(8,128)(2,1)}, u32[]{:S(2)}) copy-start(bf16[128,512]{1,0:T(8,128)(2,1)} %down_ref.1) | copy-start | bytes 393220
  8.0 59.8 %reduce-scatter.2.cloned.1.call-start = ((), (), s32[]{:S(2)}) async-start(), calls=%async_computation.5 | async-start | bytes 2359296 | tf_op jit(solution)/shard_map/reduce_scatter | solution.py:321
  11.1 4.2 %collective-permute-start = (bf16[12,128,256]{2,1,0:T(8,128)(2,1)S(1)}, bf16[12,128,256]{2,1,0:T(8,128)(2,1)S(1)}, u32[]{:S(2)}, u32[]{:S(2)}) collective-permute-start(bf16[12,128,256]{2,1,0:T(8,128)(2,1)S(1)} %get-tuple-element.19), channel_id=1, source_target_pairs={{0,1},{1,0},{2,3},{3,2},{4,5},{5,4},{6,7},{7,6},{8,9},{9,8},{10,11... | collective-permute-start | bytes 2359304 | tf_op jit(solution)/shard_map/ppermute | solution.py:317
  17.2 0.8 copy-start.5
  17.2 18.7 %copy-start.6 = (s32[128,4]{0,1:T(4,128)S(1)}, s32[128,4]{0,1:T(4,128)}, u32[]{:S(2)}) copy-start(s32[128,4]{0,1:T(4,128)} %param.12) | copy-start | bytes 6148
  17.2 20.9 %copy-start.7 = (f32[128,4]{0,1:T(4,128)S(1)}, f32[128,4]{0,1:T(4,128)}, u32[]{:S(2)}) copy-start(f32[128,4]{0,1:T(4,128)} %param.13) | copy-start | bytes 6148
  17.2 89.5 %all-gather.3.cloned.1.call-start = ((), (), s32[]{:S(2)}) async-start(), calls=%async_computation.6 | async-start | bytes 5308416 | tf_op jit(solution)/shard_map/all_gather | solution.py:329
  18.0 11.3 %collective-permute-start.1 = (bf16[16,4608]{1,0:T(8,128)(2,1)S(1)}, bf16[16,4608]{1,0:T(8,128)(2,1)S(1)}, u32[]{:S(2)}, u32[]{:S(2)}) collective-permute-start(bf16[16,4608]{1,0:T(8,128)(2,1)S(1)} %fusion.34.refs_0_), channel_id=1, source_target_pairs={{0,48},{16,0},{32,16},{48,32},{1,49},{17,1},{33,17},{49,33},{2,50}... | collective-permute-start | bytes 442376 | tf_op jit(solution)/shard_map/ppermute | solution.py:327
  22.7 10.1 %collective-permute-start.2 = (bf16[16,4608]{1,0:T(8,128)(2,1)S(1)}, bf16[16,4608]{1,0:T(8,128)(2,1)S(1)}, u32[]{:S(2)}, u32[]{:S(2)}) collective-permute-start(bf16[16,4608]{1,0:T(8,128)(2,1)S(1)} %fusion.34.refs_0_), channel_id=1, source_target_pairs={{0,32},{16,48},{32,0},{48,16},{1,33},{17,49},{33,1},{49,17},{2,34}... | collective-permute-start | bytes 442376 | tf_op jit(solution)/shard_map/ppermute | solution.py:327
  25.4 9.5 %collective-permute-start.3 = (bf16[16,4608]{1,0:T(8,128)(2,1)S(1)}, bf16[16,4608]{1,0:T(8,128)(2,1)S(1)}, u32[]{:S(2)}, u32[]{:S(2)}) collective-permute-start(bf16[16,4608]{1,0:T(8,128)(2,1)S(1)} %fusion.34.refs_0_), channel_id=1, source_target_pairs={{0,16},{16,32},{32,48},{48,0},{1,17},{17,33},{33,49},{49,1},{2,18}... | collective-permute-start | bytes 442376 | tf_op jit(solution)/shard_map/ppermute | solution.py:327
  35.8 160.9 %all-gather.5.cloned.1.call-start = ((), (), s32[]{:S(2)}) async-start(), calls=%async_computation.7 | async-start | bytes 4456448 | tf_op jit(solution)/shard_map/all_gather | solution.py:348
  67.8 1.0 copy-start.2
  196.7 2.8 %copy-start.8 = (bf16[2048,1024]{1,0:T(8,128)(2,1)S(1)}, bf16[2048,1024]{1,0:T(8,128)(2,1)}, u32[]{:S(2)}) copy-start(bf16[2048,1024]{1,0:T(8,128)(2,1)} %all-gather.5.cloned.1.call-done) | copy-start | bytes 12582916
  223.0 16.1 %all-to-all-start.3 = ((bf16[32,8,512]{2,1,0:T(8,128)(2,1)}), bf16[32,8,512]{2,1,0:T(8,128)(2,1)S(1)}, u32[]{:S(2)}, u32[]{:S(2)}) async-start(bf16[32,8,512]{2,1,0:T(8,128)(2,1)} %shard_map.117), calls=%async_computation.4 | async-start | bytes 524288 | tf_op jit(solution)/shard_map/all_to_all | solution.py:359
Sparse Core Ops, SparseCore 0:
  17.3 50.4 reduce-scatter.1
  153.7 42.8 all-gather.4
Sparse Core Ops, SparseCore 1:
  35.9 63.0 all-gather.2
